TPU v7x, 32 devices: a whole 2x2x4 slice. The times are simulated.
32 devices in a mesh: group: 2 (over x), dom: 16 (over z, y, core).
Axes of the slice: x: 2, y: 2, z: 4, core: 2. Of those that a mesh axis runs over, the one named last changes fastest.
Arguments:
- orbitals: bfloat16 [98304, 512], P(('group', 'dom')), may hold values from -6 to 6
- density_rows: bfloat16 [1024, 512], P(('group', 'dom')), may hold values from -0.01171875 to 0.01171875
- near_blocks: int32 [32, 32], P(('group', 'dom')), may hold values from 0 to 31, as said below
- leaf_coords: int32 [3, 192], P(None, ('group', 'dom')), may hold values from 0 to 31, as said below
- near_leaves: int32 [192, 3], P(('group', 'dom')), may hold values from 0 to 17, as said below
- leaf_basis: float32 [64, 98304], P(None, ('group', 'dom')), may hold values from -2 to 2
- leaf_transfer: float32 [192, 64, 64], P(('group', 'dom')), may hold values from -0.75 to 0.75
- dev_transfer: float32 [32, 64, 64], P(('group', 'dom')), may hold values from -0.375 to 0.375
- dev_far: int32 [32, 16], P(('group', 'dom')), may hold values 0 or 1
- group_far: int32 [2, 2], P('group'), may hold values 0 or 1
Outputs:
- density: float32 [98304], P(('group', 'dom'))
- hartree: float32 [98304], P(('group', 'dom'))
Inputs may be any that keep to these rules, and one draw needn't show every extreme that they name: `near_blocks`: each row names 32 distinct blocks of its own coarse domain; block b is rows b * 16 to b * 16 + 15 of the domain's density matrix, held by the device of dom index b // 2. The first 2 entries of every row of a domain are the same: all blocks of one device of that domain, in order. Every other entry is a block held by a device whose dom index differs from the row's own by at most 8, counted cyclically over the 16 dom indices. `near_leaves`: each row names 3 distinct window positions, among them the leaf's own position 6 + (t mod 6) for row t. `leaf_coords`: distinct positions for all leaves.
All inputs are finite; a program needn't handle non-finite values. No bound on the sum of `dev_far` or of `group_far` on one device may be relied on, other than what follows from the above.
Results may differ from a plain program's by a relative error of at most 0.0003.
Values may be sent and summed in bfloat16 or wider, within the bound.
No kernel may reach another device: no remote copies, remote signals or barrier semaphores. Data moves between devices by JAX's collectives and lax.ppermute only.
A program may use at most 128 MiB of HBM per device.

v0:
```python
import math

import jax
import jax.numpy as jnp
from jax import lax
from jax.sharding import PartitionSpec as P

SIDE = 8
LEAF = 512
CHEB = 4
BW = 16
NEARL = 3


vol_weight = 0.1
soft_square = 1.0


def with_halo(value, sides, width):
    for axis, dim in sides:
        peers, length = (lax.axis_size(axis), value.shape[dim])
        up = [(i, (i + 1) % peers) for i in range(peers - 1)]
        down = [(j, i) for i, j in up]
        last = lax.slice_in_dim(value, length - width, length, axis=dim)
        first = lax.slice_in_dim(value, 0, width, axis=dim)
        before = lax.ppermute(last, axis, up)
        after = lax.ppermute(first, axis, down)
        value = jnp.concatenate([before, value, after], axis=dim)
    return value


def coulomb(target, source):
    diff_x = target[0][:, None] - source[0][None, :]
    diff_y = target[1][:, None] - source[1][None, :]
    diff_z = target[2][:, None] - source[2][None, :]
    return 1.0 / jnp.sqrt(diff_x * diff_x + diff_y * diff_y + diff_z * diff_z + soft_square)


def cluster_nodes(bounds):
    steps_idx = jnp.arange(CHEB).astype(jnp.float32)
    cheb_points = jnp.cos((2.0 * steps_idx + 1.0) * (math.pi / (2.0 * CHEB)))
    centre = 0.5 * (bounds[:3] + bounds[3:])
    half_size = 0.5 * (bounds[3:] - bounds[:3])
    along = centre[:, None] + half_size[:, None] * cheb_points[None, :]
    node_index = jnp.arange(CHEB * CHEB * CHEB)
    first = node_index // (CHEB * CHEB)
    second = node_index // CHEB % CHEB
    third = node_index % CHEB
    return jnp.stack([along[0][first], along[1][second], along[2][third]])


def point_offsets():
    place = jnp.arange(LEAF)
    return jnp.stack([place // (SIDE * SIDE), place // SIDE % SIDE, place % SIDE]).astype(
        jnp.float32
    )


def far_coupling(own_nodes, other_bounds, mask_row, moments):
    other_nodes = jax.vmap(cluster_nodes)(other_bounds)
    coupling = jax.vmap(lambda other: coulomb(own_nodes, other))(other_nodes)
    coupling = coupling * mask_row.astype(jnp.float32)[:, None, None]
    return vol_weight * jnp.einsum("srq,sq->r", coupling, moments, precision=lax.Precision.HIGHEST)


def local(
    orbitals,
    density_rows,
    near_blocks,
    leaf_coords,
    near_leaves,
    leaf_basis,
    leaf_transfer,
    dev_transfer,
    dev_far,
    group_far,
):
    near_list = near_blocks[0]
    near_width = orbitals.shape[1]
    blocks_group = density_rows.shape[1] // BW
    rows_global = (near_list[:, None] * BW + jnp.arange(BW)[None, :]).reshape(-1)
    row_piece = lax.all_gather(density_rows, "dom", axis=0, tiled=True)
    piece_rows = row_piece.shape[0]
    columns = jnp.take(row_piece.reshape(piece_rows, blocks_group, BW), near_list, axis=1).reshape(
        piece_rows, near_width
    )
    inside = (rows_global >= 0) & (rows_global < piece_rows)
    chosen = jnp.take(columns, jnp.clip(rows_global, 0, piece_rows - 1), axis=0)
    local_matrix = jnp.where(
        inside[:, None], chosen, jnp.zeros((near_width, near_width), jnp.bfloat16)
    )
    product = jnp.dot(orbitals, local_matrix, preferred_element_type=jnp.float32)
    density = jnp.sum(product * orbitals.astype(jnp.float32), axis=1)
    leaf_count = leaf_coords.shape[1]
    coords_f = leaf_coords.astype(jnp.float32)
    points = SIDE * coords_f.T[:, :, None] + point_offsets()[None]
    rho_leaf = density.reshape(leaf_count, LEAF)
    packed = jnp.concatenate([points, rho_leaf[:, None, :]], axis=1)
    window = with_halo(packed, (("dom", 0),), leaf_count)

    def near_one(leaf_index):
        own_points = points[leaf_index]
        running = jnp.zeros((LEAF,), jnp.float32)
        for near_slot in range(NEARL):
            source_leaf = window[near_leaves[leaf_index, near_slot]]
            running = running + jnp.dot(
                coulomb(own_points, source_leaf[:3]),
                source_leaf[3],
                precision=lax.Precision.HIGHEST,
            )
        return running

    near_part = lax.map(near_one, jnp.arange(leaf_count)) * vol_weight
    rank = leaf_basis.shape[0]
    leaf_bases = leaf_basis.reshape(rank, leaf_count, LEAF)
    leaf_mom = jnp.einsum("rlp,lp->lr", leaf_bases, rho_leaf, precision=lax.Precision.HIGHEST)
    dev_mom = jnp.einsum("lqr,lq->r", leaf_transfer, leaf_mom, precision=lax.Precision.HIGHEST)
    bounds = jnp.concatenate(
        [SIDE * jnp.min(coords_f, axis=1), SIDE * jnp.max(coords_f, axis=1) + (SIDE - 1)]
    )
    upward = jnp.einsum("qr,q->r", dev_transfer[0], dev_mom, precision=lax.Precision.HIGHEST)
    all_mom, all_bounds = (
        lax.all_gather(dev_mom[None], "dom", axis=0, tiled=True),
        lax.all_gather(bounds[None], "dom", axis=0, tiled=True),
    )
    group_mom = lax.psum(upward, "dom")
    dev_local = far_coupling(cluster_nodes(bounds), all_bounds, dev_far[0], all_mom)
    group_bounds = jnp.concatenate(
        [jnp.min(all_bounds[:, :3], axis=0), jnp.max(all_bounds[:, 3:], axis=0)]
    )
    coarse_mom, coarse_bounds = (
        lax.all_gather(group_mom[None], "group", axis=0, tiled=True),
        lax.all_gather(group_bounds[None], "group", axis=0, tiled=True),
    )
    group_local = far_coupling(cluster_nodes(group_bounds), coarse_bounds, group_far[0], coarse_mom)
    dev_total = dev_local + jnp.einsum(
        "qr,r->q", dev_transfer[0], group_local, precision=lax.Precision.HIGHEST
    )
    leaf_local = jnp.einsum("lqr,r->lq", leaf_transfer, dev_total, precision=lax.Precision.HIGHEST)
    far_part = jnp.einsum("rlp,lr->lp", leaf_bases, leaf_local, precision=lax.Precision.HIGHEST)
    hartree = (near_part + far_part).reshape(-1)
    return (density, hartree)


def solution(mesh):
    in_specs = (
        P(("group", "dom"), None),
        P(("group", "dom"), None),
        P(("group", "dom"), None),
        P(None, ("group", "dom")),
        P(("group", "dom"), None),
        P(None, ("group", "dom")),
        P(("group", "dom"), None, None),
        P(("group", "dom"), None, None),
        P(("group", "dom"), None),
        P("group", None),
    )
    out_specs = (P(("group", "dom")), P(("group", "dom")))
    return jax.shard_map(local, mesh=mesh, in_specs=in_specs, out_specs=out_specs, check_vma=False)
```

profile of v0, /device:TPU:0, one launch (start us, length us, event | category | flops | bytes accessed | tf_op | source)
XLA Modules:
  0.0 194.4 jit_solution(13754105599990443870)
XLA Ops:
  0.6 0.7 bitcast_multiply_fusion.1
  1.3 0.7 fusion.135
  2.0 0.7 compare_and_fusion
  3.0 0.8 convert_reduce_fusion.1
  3.9 24.8 %all_gather.15 = bf16[512,512]{1,0:T(8,128)(2,1)S(1)} all-gather(bf16[32,512]{1,0:T(8,128)(2,1)} %param.13), channel_id=1, replica_groups=mesh['group'=2,'dom'=16] {'dom'}, dimensions={0}, use_global_device_ids=true | all-gather | bytes 557056 | tf_op jit(solution)/shard_map/all_gather | solution.py:82
  30.0 4.6 %copy.46 = bf16[3072,512]{0,1:T(8,128)(2,1)} copy(bf16[3072,512]{1,0:T(8,128)(2,1)} %param.12) | data formatting | bytes 6291456 | tf_op args[0]
  34.7 2.0 %gather_fusion.1 = bf16[512,512]{1,0:T(8,128)(2,1)S(1)} fusion(bf16[512,512]{1,0:T(8,128)(2,1)S(1)} %broadcast_select_fusion, s32[1024]{0:T(1024)S(1)} %pad_clamp_fusion.3), kind=kCustom, calls=%fused_computation.1 | custom fusion | bytes 1050624 | tf_op jit(solution)/shard_map/jit(_take)/gather | solution.py:88
  36.9 5.0 %fusion.63 = f32[3072]{0:T(1024)S(1)} fusion(bf16[3072,512]{0,1:T(8,128)(2,1)} %copy.46, bf16[3072,512]{1,0:T(8,128)(2,1)} %param.12, bf16[512,512]{1,0:T(8,128)(2,1)S(1)} %gather_fusion.1, pred[512]{0:T(512)(128)(4,1)S(1)} %compare_and_fusion.1, pred[512]{0:T(512)(128)(4,1)S(1)} %and.221), kind=kOutput, calls=%fused_computation.88 | convolution fusion | flops 1615852544 | bytes 6829056 | tf_op jit(solution)/shard_map/dot_general | solution.py:92
  41.9 2.3 %collective-permute-start = (f32[6,4,512]{2,1,0:T(4,128)S(1)}, f32[6,4,512]{2,1,0:T(4,128)S(1)}, u32[]{:S(2)}, u32[]{:S(2)}) collective-permute-start(f32[6,4,512]{2,1,0:T(4,128)S(1)} %pad_maximum_fusion.1), channel_id=1, source_target_pairs={{0,1},{1,2},{2,3},{3,4},{4,5},{5,6},{6,7},{7,8},{8,9},{9,10},{10,1... | collective-permute-start | bytes 147464 | tf_op jit(solution)/shard_map/ppermute | solution.py:26
  44.2 1.3 collective-permute-start.1
  45.6 0.7 fusion.71
  48.9 31.1 %all-reduce.3 = (f32[1024]{0:T(1024)S(1)}, f32[96]{0:T(128)S(1)}, f32[1,64]{1,0:T(1,128)S(1)}) all-reduce(f32[1024]{0:T(1024)S(1)} %bitcast_dynamic-update-slice_fusion, f32[96]{0:T(128)S(1)} %maximum_dynamic-update-slice_fusion, f32[1,64]{1,0:T(1,128)S(1)} %fusion.112), channel_id=3, replica_groups=mesh['group'=2,'dom'=16] {'dom'}, use_global_device_ids=true, to_apply=%add.1 | all-reduce | flops 1184 | bytes 9472
  80.3 0.7 fusion.141
  82.4 4.9 %all-reduce.2 = f32[12]{0:T(128)S(1)} all-reduce(f32[12]{0:T(128)S(1)} %maximum_dynamic-update-slice_fusion.1), channel_id=4, replica_groups=mesh['group'=2,'dom'=16] {'group'}, use_global_device_ids=true, to_apply=%add.2 | all-reduce | flops 12 | bytes 96
  90.1 4.2 %all-gather.3 = f32[2,1,64]{2,1,0:T(1,128)S(1)} all-gather(f32[1,1,64]{2,1,0:T(1,128)S(1)} %bitcast.298), channel_id=1, replica_groups=mesh['group'=2,'dom'=16] {'group'}, dimensions={0}, use_global_device_ids=true | all-gather | bytes 768 | tf_op jit(solution)/shard_map/all_gather | solution.py:132
  94.4 0.7 fusion.142
  97.4 2.6 %compare_select_fusion.23 = f32[64]{0:T(128)S(1)} fusion(f32[]{:T(128)} %bitcast.73, f32[]{:T(128)} %bitcast.74, f32[]{:T(128)} %bitcast.75, f32[]{:T(128)} %bitcast.76), kind=kLoop, calls=%fused_computation.229 | loop fusion | flops 1088 | bytes 272 | tf_op jit(solution)/shard_map/gather | solution.py:49
  100.0 2.6 %compare_select_fusion.24 = f32[64]{0:T(128)S(1)} fusion(f32[]{:T(128)} %bitcast.37, f32[]{:T(128)} %bitcast.38, f32[]{:T(128)} %bitcast.39, f32[]{:T(128)} %bitcast.40), kind=kLoop, calls=%fused_computation.230 | loop fusion | flops 1088 | bytes 272 | tf_op jit(solution)/shard_map/gather | solution.py:49
  102.6 5.0 %compare_select_fusion.11 = (f32[64]{0:T(128)S(1)}, f32[64]{0:T(128)S(1)}) fusion(f32[]{:T(128)} %bitcast.94, f32[]{:T(128)} %bitcast.95, f32[]{:T(128)} %bitcast.96, f32[]{:T(128)} %bitcast.97, f32[]{:T(128)} %bitcast.92, f32[]{:T(128)} %bitcast.91, f32[]{:T(128)} %bitcast.90, f32[]{:T(128)} %bitcast.89), kind=kLoop, calls=%fused_computation.217 | loop fusion | flops 2624 | bytes 544 | tf_op jit(solution)/shard_map/gather | solution.py:49
  107.8 5.0 %compare_select_fusion.12 = (f32[64]{0:T(128)S(1)}, f32[64]{0:T(128)S(1)}) fusion(f32[]{:T(128)} %bitcast.60, f32[]{:T(128)} %bitcast.61, f32[]{:T(128)} %bitcast.62, f32[]{:T(128)} %bitcast.63, f32[]{:T(128)} %bitcast.58, f32[]{:T(128)} %bitcast.57, f32[]{:T(128)} %bitcast.56, f32[]{:T(128)} %bitcast.55), kind=kLoop, calls=%fused_computation.218 | loop fusion | flops 2624 | bytes 544 | tf_op jit(solution)/shard_map/gather | solution.py:49
  112.9 0.8 fusion.68
  115.0 78.7 %while.10 = (s32[]{:T(128)}, f32[6,512]{1,0:T(8,128)S(1)}, s32[6]{0:T(128)S(1)}, f32[6,3,512]{2,1,0:T(4,128)S(1)}, s32[6,3]{0,1:T(4,128)S(1)}, /*index=5*/f32[18...) while((s32[]{:T(128)}, f32[6,512]{1,0:T(8,128)S(1)}, ...), condition=%wide.region_2.3_spmd, body=%wide.region_1.2_spmd.sunk | while | flops 16516113 | bytes 110981 | solution.py:113
  115.0 0.6 dynamic_slice.31
  117.5 0.7 constant_dynamic-slice_fusion.20
  123.9 1.4 fusion.168
  125.3 1.4 fusion.167
  126.7 1.4 fusion.166
  128.1 0.6 dynamic_slice.31
  130.7 0.7 constant_dynamic-slice_fusion.20
  137.0 1.4 fusion.168
  138.4 1.4 fusion.167
  139.8 1.4 fusion.166
  143.8 0.7 constant_dynamic-slice_fusion.20
  150.1 1.4 fusion.168
  151.5 1.4 fusion.167
  152.9 1.4 fusion.166
  156.9 0.7 constant_dynamic-slice_fusion.20
  163.3 1.4 fusion.168
  164.6 1.4 fusion.167
  166.0 1.4 fusion.166
  170.0 0.7 constant_dynamic-slice_fusion.20
  176.4 1.4 fusion.168
  177.8 1.4 fusion.167
  179.2 1.4 fusion.166
  183.1 0.7 constant_dynamic-slice_fusion.20
  189.5 1.4 fusion.168
  190.9 1.4 fusion.167
  192.3 1.4 fusion.166
  (128 shorter events, 14.7 us)
Async XLA Ops:
  0.6 47.6 %copy-start = (f32[6,64,64]{2,1,0:T(8,128)S(1)}, f32[6,64,64]{2,1,0:T(8,128)}, u32[]{:S(2)}) copy-start(f32[6,64,64]{2,1,0:T(8,128)} %param.18) | copy-start | bytes 294916
  36.8 8.8 %copy-start.1 = (f32[64,3072]{1,0:T(8,128)S(1)}, f32[64,3072]{1,0:T(8,128)}, u32[]{:S(2)}) copy-start(f32[64,3072]{1,0:T(8,128)} %param.17) | copy-start | bytes 2359300
  36.8 9.5 %copy-start.8 = (u32[32]{0:T(128)S(1)}, u32[32]{0:T(128)}, u32[]{:S(2)}) copy-start(u32[32]{0:T(128)} %constant.248) | copy-start | bytes 388
  36.8 11.7 %copy-start.2 = (f32[1,64,64]{2,1,0:T(8,128)S(1)}, f32[1,64,64]{2,1,0:T(8,128)}, u32[]{:S(2)}) copy-start(f32[1,64,64]{2,1,0:T(8,128)} %param.19) | copy-start | bytes 49156
  36.9 44.2 %copy-start.7 = (u32[32]{0:T(128)S(1)}, u32[32]{0:T(128)}, u32[]{:S(2)}) copy-start(u32[32]{0:T(128)} %constant.258) | copy-start | bytes 388
  36.9 57.5 %copy-start.5 = (s32[1,2]{1,0:T(1,128)S(1)}, s32[1,2]{1,0:T(1,128)}, u32[]{:S(2)}) copy-start(s32[1,2]{1,0:T(1,128)} %param.21) | copy-start | bytes 28
  36.9 60.5 %copy-start.6 = (s32[1,16]{1,0:T(1,128)S(1)}, s32[1,16]{1,0:T(1,128)}, u32[]{:S(2)}) copy-start(s32[1,16]{1,0:T(1,128)} %param.20) | copy-start | bytes 196
  41.9 73.1 %copy-start.3 = (f32[3072]{0:T(1024)}, f32[3072]{0:T(1024)S(1)}, u32[]{:S(2)}) copy-start(f32[3072]{0:T(1024)S(1)} %fusion.63) | copy-start | bytes 36868
  41.9 73.1 %copy-start.4 = (s32[6,3]{0,1:T(4,128)S(1)}, s32[6,3]{0,1:T(4,128)}, u32[]{:S(2)}) copy-start(s32[6,3]{0,1:T(4,128)} %param.16) | copy-start | bytes 220
  41.9 73.0 %collective-permute-start = (f32[6,4,512]{2,1,0:T(4,128)S(1)}, f32[6,4,512]{2,1,0:T(4,128)S(1)}, u32[]{:S(2)}, u32[]{:S(2)}) collective-permute-start(f32[6,4,512]{2,1,0:T(4,128)S(1)} %pad_maximum_fusion.1), channel_id=1, source_target_pairs={{0,1},{1,2},{2,3},{3,4},{4,5},{5,6},{6,7},{7,8},{8,9},{9,10},{10,1... | collective-permute-start | bytes 147464 | tf_op jit(solution)/shard_map/ppermute | solution.py:26
  44.2 70.7 %collective-permute-start.1 = (f32[6,4,512]{2,1,0:T(4,128)S(1)}, f32[6,4,512]{2,1,0:T(4,128)S(1)}, u32[]{:S(2)}, u32[]{:S(2)}) collective-permute-start(f32[6,4,512]{2,1,0:T(4,128)S(1)} %pad_maximum_fusion.1), channel_id=1, source_target_pairs={{1,0},{2,1},{3,2},{4,3},{5,4},{6,5},{7,6},{8,7},{9,8},{10,9},{11,1... | collective-permute-start | bytes 147464 | tf_op jit(solution)/shard_map/ppermute | solution.py:27
where the time goes:
time: 196 us; the launch traced here: 194 us
  blocking collectives  65 us (33%)
  loops' own time  45.4 us (23%)
  matrix products  33.4 us (17%)
  local copies, waits for them, and re-layouts  24.7 us (13%)
  other arithmetic  19.4 us (10%)
  starting transfers between devices  3.55 us (2%)
  between operations  2.96 us (2%)
    another operation x1, loops' own time, local(): near_part = lax.map(near_one, jnp.arange(leaf_count)) * vol_weight  45.4 us
    unnamed x2, blocking collectives  36 us
    dot_general x18, matrix products, near_one(): jnp.dot(coulomb(own_points, source_leaf[:3]), source_leaf[3], precision=l...  25 us
    all_gather x1, blocking collectives, local(): row_piece = lax.all_gather(density_rows, 'dom', axis=0, tiled=True)  24.8 us
    gather x7, other arithmetic, cluster_nodes(): return jnp.stack([along[0][first], along[1][second], along[2][third]])  15.2 us
    unnamed x25, local copies, waits for them, and re-layouts  5.98 us
    gather x11, local copies, waits for them, and re-layouts, cluster_nodes(): return jnp.stack([along[0][first], along[1][second], along[2][third]])  5.24 us
    dot_general x1, matrix products, local(): jnp.dot(orbitals, local_matrix, preferred_element_type=jnp.float32)  4.97 us
  transfers between devices with their start and end apart: 2, of which 0 were waited for; matrix products, arithmetic and copies ran while one was open for 14% of the time, Pallas kernels for 0%

commit v1 on v0

v1 whole, which is shorter than its diff:
```python
import functools
import math

import jax
import jax.numpy as jnp
from jax import lax
from jax.experimental import pallas as pl
from jax.experimental.pallas import tpu as pltpu
from jax.sharding import PartitionSpec as P

SIDE = 8
LEAF = 512
CHEB = 4
RANK = CHEB * CHEB * CHEB
BW = 16
NEARL = 3
LANES = 128
LEAF_ROWS = LEAF // LANES
HIGHEST = lax.Precision.HIGHEST

vol_weight = 0.1
soft_square = 1.0


def xor_stages(count):
    bits = count.bit_length() - 1
    stages, bit = ([(2,)], 2) if bits > 1 else ([], 1)
    while bit < bits:
        wide = 2 if bit + 1 < bits else 1
        stages.append(tuple(m << bit for m in range(1, 1 << wide)))
        bit += wide
    return stages


def swap(value, axis, mask):
    return lax.ppermute(value, axis, [(i, i ^ mask) for i in range(lax.axis_size(axis))])


def gather_rows(rows):
    held = rows
    for masks in xor_stages(lax.axis_size("dom")):
        held = jnp.concatenate([held] + [swap(held, "dom", m) for m in masks], axis=0)
    return held, swap(held, "dom", 1)


def iota(shape, dim):
    return lax.broadcasted_iota(jnp.int32, shape, dim)


def lane_sums(x):
    hi = x.astype(jnp.bfloat16)
    lo = (x - hi.astype(jnp.float32)).astype(jnp.bfloat16)
    both = jnp.concatenate([hi, lo], axis=1)
    ones = jnp.ones((8, 2 * LANES), jnp.bfloat16)
    return lax.dot_general(ones, both, (((1,), (1,)), ((), ())), preferred_element_type=jnp.float32)


def prepare_kernel(near_ref, basis_ref, transfer_ref, dev_ref, pick_ref, weights_ref):
    blocks = near_ref.shape[1]
    width = blocks * BW
    spread = (iota((blocks, width), 1) // BW == iota((blocks, width), 0)).astype(jnp.float32)
    near = jnp.broadcast_to(near_ref[...].astype(jnp.float32), (8, blocks))
    column = jnp.dot(near, spread, preferred_element_type=jnp.float32)[:1].astype(jnp.int32) * BW
    column = column + iota((1, width), 1) % BW
    for start in range(0, pick_ref.shape[0], LEAF):
        size = min(LEAF, pick_ref.shape[0] - start)
        hit = iota((size, width), 0) + start == column
        pick_ref[start : start + size, :] = jnp.where(hit, 1.0, 0.0).astype(jnp.bfloat16)
    dev = dev_ref[0]
    for leaf in range(transfer_ref.shape[0]):
        points = slice(leaf * LEAF, (leaf + 1) * LEAF)
        own = lax.dot_general(
            transfer_ref[leaf],
            basis_ref[:, points],
            (((0,), (0,)), ((), ())),
            precision=HIGHEST,
            preferred_element_type=jnp.float32,
        )
        weights_ref[:RANK, points] = own
        weights_ref[RANK:, points] = lax.dot_general(
            dev, own, (((0,), (0,)), ((), ())), precision=HIGHEST, preferred_element_type=jnp.float32
        )


def density_kernel(
    near_ref,
    coords_ref,
    orbitals_ref,
    held_ref,
    other_ref,
    pick_ref,
    weights_ref,
    density_ref,
    halo_ref,
    expansion_ref,
    rows_ref,
    orbit_ref,
    sems,
):
    leaves = coords_ref.shape[1]
    copies = []
    for leaf in range(leaves):
        points = pl.ds(leaf * LEAF, LEAF)
        copies.append(
            pltpu.make_async_copy(orbitals_ref.at[points], orbit_ref.at[points], sems.at[leaf])
        )
        copies[-1].start()
    me = lax.axis_index("dom")
    for k in range(near_ref.shape[1]):
        block = near_ref[0, k]
        apart = jnp.bitwise_xor(lax.shift_right_logical(block, 1), me)
        first = lax.shift_right_logical(apart, 1) * (2 * BW) + jnp.bitwise_and(block, 1) * BW
        at = pl.ds(pl.multiple_of(first, BW), BW)
        mine = jnp.bitwise_and(apart, 1) == 0
        rows_ref[k * BW : (k + 1) * BW, :] = jnp.where(mine, held_ref[at, :], other_ref[at, :])
    matrix = jnp.dot(rows_ref[...], pick_ref[...], preferred_element_type=jnp.float32)
    matrix = matrix.astype(jnp.bfloat16)
    total = jnp.zeros((2 * RANK, LANES), jnp.float32)
    for leaf in range(leaves):
        copies[leaf].wait()
        orbit = orbit_ref[leaf * LEAF : (leaf + 1) * LEAF, :]
        product = jnp.dot(orbit, matrix, preferred_element_type=jnp.float32)
        product = product * orbit.astype(jnp.float32)
        folded = product[:, :LANES]
        for start in range(LANES, product.shape[1], LANES):
            folded = folded + product[:, start : start + LANES]
        values = lane_sums(folded)[:1]
        for j in range(LEAF_ROWS):
            row = leaf * LEAF_ROWS + j
            part = values[:, j * LANES : (j + 1) * LANES]
            density_ref[row : row + 1, :] = part
            halo_ref[row : row + 1, :] = part
            total = total + weights_ref[:, row * LANES : (row + 1) * LANES] * part
    coords = coords_ref[...].astype(jnp.float32)
    rows = leaves * LEAF_ROWS
    halo_ref[rows:, :] = jnp.zeros((halo_ref.shape[0] - rows, LANES), jnp.float32)
    halo_ref[rows : rows + 3, :leaves] = coords
    low = SIDE * jnp.min(coords, axis=1, keepdims=True)
    high = SIDE * jnp.max(coords, axis=1, keepdims=True) + (SIDE - 1)
    lane = iota((1, LANES), 1)
    bounds = jnp.zeros((1, LANES), jnp.float32)
    for k in range(3):
        bounds = jnp.where(lane == k, low[k : k + 1], bounds)
        bounds = jnp.where(lane == 3 + k, high[k : k + 1], bounds)
    both = jnp.concatenate([lane_sums(total)[:1], bounds], axis=0)
    expansion_ref[...] = jnp.broadcast_to(both[None], expansion_ref.shape)


def pattern(index):
    steps = (index // (CHEB * CHEB) % CHEB, index // CHEB % CHEB, index % CHEB)
    points = [math.cos((2 * a + 1) * math.pi / (2 * CHEB)) for a in range(CHEB)]
    out = []
    for step in steps:
        value = jnp.full(index.shape, points[CHEB - 1], jnp.float32)
        for a in range(CHEB - 1):
            value = jnp.where(step == a, points[a], value)
        out.append(value)
    return out


def nodes(bounds, unit):
    out = []
    for k in range(3):
        low, high = bounds[:, k : k + 1], bounds[:, 3 + k : 4 + k]
        out.append(0.5 * (low + high) + 0.5 * (high - low) * unit[k])
    return out


def node_coupling(target, source):
    square = soft_square
    for t, s in zip(target, source, strict=True):
        apart = t - s
        square = square + apart * apart
    return lax.rsqrt(square)


def potential_kernel(
    leaves_ref,
    far_ref,
    group_far_ref,
    halo_ref,
    even_ref,
    odd_ref,
    expansion_ref,
    weights_ref,
    dev_ref,
    out_ref,
    density_ref,
    place_ref,
    sum_ref,
    local_ref,
):
    leaves = leaves_ref.shape[0]
    rows = leaves * LEAF_ROWS
    group_count, dom_count = group_far_ref.shape[1], far_ref.shape[1]
    group, me = lax.axis_index("group"), lax.axis_index("dom")

    is_odd = jnp.bitwise_and(me, 1) == 1
    even, odd = even_ref[...], odd_ref[...]
    window = (jnp.where(is_odd, even, odd), halo_ref[...], jnp.where(is_odd, odd, even))
    ones = jnp.ones((LANES, LANES), jnp.bfloat16)
    diagonal = iota((8, LANES), 0) == iota((8, LANES), 1)
    spread = []
    for side, held in enumerate(window):
        density_ref[side * rows : (side + 1) * rows, :] = held[:rows]
        for k in range(3):
            spread.append(jnp.where(diagonal, held[rows + k : rows + k + 1], 0.0))
    spread = jnp.concatenate(spread, axis=0).astype(jnp.bfloat16)
    place_ref[...] = SIDE * jnp.dot(spread, ones, preferred_element_type=jnp.float32)

    sent = expansion_ref[...]
    moments, bounds = sent[:, 0, :], sent[:, 1, :]
    lane = iota((1, LANES), 1)
    unit_row = pattern(lane % RANK)
    unit_column = pattern(iota((RANK, LANES), 0))
    group_bounds = []
    for h in range(group_count):
        part = bounds[h * dom_count : (h + 1) * dom_count]
        low = jnp.min(part, axis=0, keepdims=True)
        high = jnp.max(part, axis=0, keepdims=True)
        group_bounds.append(jnp.where(lane < 3, low, high))
    own_group_bounds = group_bounds[0]
    for h in range(1, group_count):
        own_group_bounds = jnp.where(group == h, group_bounds[h], own_group_bounds)
    target = nodes(own_group_bounds, unit_column)
    total = jnp.zeros((RANK, LANES), jnp.float32)
    for h in range(group_count):
        raised = jnp.sum(moments[h * dom_count : (h + 1) * dom_count], axis=0, keepdims=True)
        raised = jnp.where(lane >= RANK, raised, 0.0) * group_far_ref[0, h].astype(jnp.float32)
        total = total + node_coupling(target, nodes(group_bounds[h], unit_row)) * raised
    group_local = vol_weight * lane_sums(total)[:1, :RANK]
    local = jnp.sum(dev_ref[0] * group_local, axis=1, keepdims=True)
    base = group * dom_count
    own = expansion_ref[pl.ds(base, dom_count)]
    own_bounds = expansion_ref[pl.ds(base + me, 1)][:, 1, :]
    target = nodes(own_bounds, unit_column)
    source = nodes(own[:, 1, :], unit_row)
    own_moments = jnp.where(lane < RANK, own[:, 0, :], 0.0)
    total = jnp.zeros((RANK, LANES), jnp.float32)
    for s in range(dom_count):
        coupling = node_coupling(target, [x[s : s + 1] for x in source])
        total = total + coupling * (own_moments[s : s + 1] * far_ref[0, s].astype(jnp.float32))
    local = local + vol_weight * jnp.sum(total, axis=1, keepdims=True)
    local_ref[...] = jnp.broadcast_to(local, (RANK, LANES))

    lane8, row8 = iota((8, LANES), 1), iota((8, LANES), 0)
    half = (lane8 // (SIDE * SIDE)).astype(jnp.float32)
    at_y = (lane8 // SIDE % SIDE).astype(jnp.float32)
    along_z = (row8 - lane8 % SIDE).astype(jnp.float32)

    def place(position):
        side = (position >= leaves).astype(jnp.int32) + (position >= 2 * leaves).astype(jnp.int32)
        first = side * 24 + (position - side * leaves)
        return [place_ref[pl.ds(first + 8 * k, 1), :] for k in range(3)]

    def one_leaf(leaf, carry):
        own_place = place(leaf + leaves)
        for slot in range(NEARL):
            position = leaves_ref[leaf, slot]
            shift = [a - b for a, b in zip(own_place, place(position), strict=True)]
            rho = [density_ref[pl.ds(position * LEAF_ROWS + j, 1), :] for j in range(LEAF_ROWS)]
            along = shift[2] + along_z
            square_z = along * along + soft_square
            square_x = []
            for m in range(-6, SIDE):
                apart = shift[0] + (m - half)
                square_x.append(apart * apart)
            for y in range(SIDE):
                apart = shift[1] + (y - at_y)
                square = apart * apart + square_z
                kernel = [lax.rsqrt(x + square) for x in square_x]
                for x in range(SIDE):
                    value = kernel[x + 6] * rho[0]
                    for j in range(1, LEAF_ROWS):
                        value = value + kernel[x - 2 * j + 6] * rho[j]
                    at = slice((x * SIDE + y) * SIDE, (x * SIDE + y + 1) * SIDE)
                    if slot == 0:
                        sum_ref[at, :] = value
                    else:
                        sum_ref[at, :] += value
        near = vol_weight * lane_sums(sum_ref[...])[:1]
        spread_local = local_ref[...]
        for j in range(LEAF_ROWS):
            row = leaf * LEAF_ROWS + j
            at = pl.ds(pl.multiple_of(row * LANES, LANES), LANES)
            far = jnp.sum(weights_ref[:RANK, at] * spread_local, axis=0, keepdims=True)
            out_ref[pl.ds(row, 1), :] = near[:, j * LANES : (j + 1) * LANES] + far
        return carry

    lax.fori_loop(0, leaves, one_leaf, 0)


VMEM = pl.BlockSpec(memory_space=pltpu.VMEM)
SMEM = pl.BlockSpec(memory_space=pltpu.SMEM)


def local(
    orbitals,
    density_rows,
    near_blocks,
    leaf_coords,
    near_leaves,
    leaf_basis,
    leaf_transfer,
    dev_transfer,
    dev_far,
    group_far,
):
    points, width = orbitals.shape
    leaves = leaf_coords.shape[1]
    rows = leaves * LEAF_ROWS
    natural = density_rows.shape[1]
    devices = lax.axis_size("group") * lax.axis_size("dom")
    dom_count = lax.axis_size("dom")
    f32 = jnp.float32
    params = pltpu.CompilerParams(vmem_limit_bytes=(24 << 20) + 4 * natural * natural)

    pick, weights = pl.pallas_call(
        prepare_kernel,
        out_shape=(
            jax.ShapeDtypeStruct((natural, width), jnp.bfloat16),
            jax.ShapeDtypeStruct((2 * RANK, points), f32),
        ),
        in_specs=[VMEM] * 4,
        out_specs=(VMEM, VMEM),
        compiler_params=params,
        cost_estimate=pl.CostEstimate(
            flops=2 * 6 * 2 * RANK * RANK * points, bytes_accessed=8 << 20, transcendentals=0
        ),
        name="prepare",
    )(near_blocks, leaf_basis, leaf_transfer, dev_transfer)

    held, other = gather_rows(density_rows)

    density, halo, expansion = pl.pallas_call(
        density_kernel,
        out_shape=(
            jax.ShapeDtypeStruct((rows, LANES), f32),
            jax.ShapeDtypeStruct((rows + 8, LANES), f32),
            jax.ShapeDtypeStruct((devices, 2, LANES), f32),
        ),
        in_specs=[SMEM, VMEM, pl.BlockSpec(memory_space=pl.ANY)] + [VMEM] * 4,
        out_specs=(VMEM, VMEM, VMEM),
        scratch_shapes=[
            pltpu.VMEM((width, natural), jnp.bfloat16),
            pltpu.VMEM((points, width), jnp.bfloat16),
            pltpu.SemaphoreType.DMA((leaves,)),
        ],
        compiler_params=params,
        cost_estimate=pl.CostEstimate(
            flops=2 * points * width * width, bytes_accessed=8 << 20, transcendentals=0
        ),
        name="density",
    )(near_blocks, leaf_coords, orbitals, held, other, pick, weights)

    even = swap(halo, "dom", 1)
    pairs = [(i, i + 1 if i % 2 else i - 1) for i in range(1, dom_count - 1)]
    odd = lax.ppermute(halo, "dom", pairs)
    everyone = lax.all_to_all(expansion, ("group", "dom"), 0, 0)

    hartree = pl.pallas_call(
        potential_kernel,
        out_shape=jax.ShapeDtypeStruct((rows, LANES), f32),
        in_specs=[SMEM, SMEM, SMEM] + [VMEM] * 6,
        out_specs=VMEM,
        scratch_shapes=[
            pltpu.VMEM((3 * rows, LANES), f32),
            pltpu.VMEM((72, LANES), f32),
            pltpu.VMEM((LEAF, LANES), f32),
            pltpu.VMEM((RANK, LANES), f32),
        ],
        compiler_params=params,
        cost_estimate=pl.CostEstimate(
            flops=20 << 20, bytes_accessed=2 << 20, transcendentals=4 << 20
        ),
        name="potential",
    )(near_leaves, dev_far, group_far, halo, even, odd, everyone, weights, dev_transfer)
    return (density.reshape(-1), hartree.reshape(-1))


def solution(mesh):
    in_specs = (
        P(("group", "dom"), None),
        P(("group", "dom"), None),
        P(("group", "dom"), None),
        P(None, ("group", "dom")),
        P(("group", "dom"), None),
        P(None, ("group", "dom")),
        P(("group", "dom"), None, None),
        P(("group", "dom"), None, None),
        P(("group", "dom"), None),
        P("group", None),
    )
    out_specs = (P(("group", "dom")), P(("group", "dom")))
    return jax.shard_map(local, mesh=mesh, in_specs=in_specs, out_specs=out_specs, check_vma=False)
```

time: 196 us -> 46.3 us (0.24)
  blocking collectives: 65 us -> 0 us
  loops' own time: 45.4 us -> 0 us
  matrix products: 33.4 us -> 0 us
  other arithmetic: 19.4 us -> 0 us
  local copies, waits for them, and re-layouts: 24.7 us -> 6.99 us
  waiting for transfers between devices: 0.01 us -> 13.5 us
  Pallas kernels: 0 us -> 12.6 us
  starting transfers between devices: 3.55 us -> 12 us
  between operations: 2.96 us -> 0.74 us
    another operation x1 -> x0, loops' own time: 45.4 us -> none  [local(): near_part = lax.map(near_one, jnp.arange(leaf_count)) * vol_weight]
    unnamed x2 -> x0, blocking collectives: 36 us -> none
    dot_general x27 -> x0, matrix products: 33.4 us -> none  [the longest x18 25 us: near_one(): jnp.dot(coulomb(own_points, source_leaf[:3]), source_leaf[3], precision=l...]
    all_gather x2 -> x0, blocking collectives: 29 us -> none  [the longest x1 24.8 us: local(): row_piece = lax.all_gather(density_rows, 'dom', axis=0, tiled=True)]
    gather x9 -> x0, other arithmetic: 15.2 us -> none  [the longest x7 15.2 us: cluster_nodes(): return jnp.stack([along[0][first], along[1][second], along[2][third]])]
    pallas_call x0 -> x3, Pallas kernels: none -> 12.6 us  [the longest x1 5.44 us: local(): pl.pallas_call(density_kernel, out_shape=(jax.ShapeDtypeStruct((rows, LAN...]
    gather x14 -> x0, local copies, waits for them, and re-layouts: 8.01 us -> none  [the longest x11 5.24 us: cluster_nodes(): return jnp.stack([along[0][first], along[1][second], along[2][third]])]
    dynamic_slice x12 -> x0, local copies, waits for them, and re-layouts: 7.77 us -> none  [the longest x6 3.93 us: near_one(): source_leaf = window[near_leaves[leaf_index, near_slot]]]
  transfers between devices with their start and end apart: 2 -> 8, of which waited for: 0 -> 6; matrix products, arithmetic and copies ran while one was open for 14% -> 2% of each run, Pallas kernels for 0% -> 5%
where the time goes in v1:
time: 46.3 us; the launch traced here: 45.9 us
  waiting for transfers between devices  13.5 us (29%)
  Pallas kernels  12.6 us (27%)
  starting transfers between devices  12 us (26%)
  local copies, waits for them, and re-layouts  6.99 us (15%)
  between operations  0.74 us (2%)
    ppermute x6, starting transfers between devices, swap(): lax.ppermute(value, axis, [(i, i ^ mask) for i in range(lax.axis_size(axi...  8.02 us
    ppermute x6, waiting for transfers between devices, swap(): lax.ppermute(value, axis, [(i, i ^ mask) for i in range(lax.axis_size(axi...  7.53 us
    unnamed x24, local copies, waits for them, and re-layouts  6.98 us
    all_to_all x1, waiting for transfers between devices, local(): everyone = lax.all_to_all(expansion, ('group', 'dom'), 0, 0)  6 us
    pallas_call x1, Pallas kernels, local(): pl.pallas_call(density_kernel, out_shape=(jax.ShapeDtypeStruct((rows, LAN...  5.44 us
    pallas_call x1, Pallas kernels, local(): pl.pallas_call(potential_kernel, out_shape=jax.ShapeDtypeStruct((rows, LA...  4.85 us
    all_to_all x1, starting transfers between devices, local(): everyone = lax.all_to_all(expansion, ('group', 'dom'), 0, 0)  3.36 us
    pallas_call x1, Pallas kernels, local(): pl.pallas_call(prepare_kernel, out_shape=(jax.ShapeDtypeStruct((natural,...  2.32 us
  transfers between devices with their start and end apart: 8, of which 6 were waited for; matrix products, arithmetic and copies ran while one was open for 2% of the time, Pallas kernels for 5%

profile of v1, /device:TPU:0, one launch (start us, length us, event | category | flops | bytes accessed | tf_op | source)
XLA Modules:
  0.0 45.9 jit_solution(10746469278464628949)
XLA Ops:
  0.6 3.0 %collective-permute-start = (bf16[32,512]{1,0:T(8,128)(2,1)}, bf16[32,512]{1,0:T(8,128)(2,1)S(1)}, u32[]{:S(2)}, u32[]{:S(2)}) collective-permute-start(bf16[32,512]{1,0:T(8,128)(2,1)} %param.11), channel_id=1, source_target_pairs={{0,2},{1,3},{2,0},{3,1},{4,6},{5,7},{6,4},{7,5},{8,10},{9,11},{10,... | collective-permute-start | bytes 98312 | tf_op jit(solution)/shard_map/ppermute | solution.py:36
  3.7 0.8 %constant_dynamic-update-slice_fusion.1 = (bf16[64,512]{1,0:T(8,128)(2,1)S(1)}, bf16[256,512]{1,0:T(8,128)(2,1)S(1)}) fusion(bf16[32,512]{1,0:T(8,128)(2,1)} %param.11), kind=kLoop, calls=%fused_computation.1 | loop fusion | bytes 98304
  4.5 1.3 %collective-permute-done = bf16[32,512]{1,0:T(8,128)(2,1)S(1)} collective-permute-done((bf16[32,512]{1,0:T(8,128)(2,1)}, bf16[32,512]{1,0:T(8,128)(2,1)S(1)}, u32[]{:S(2)}, u32[]{:S(2)}) %collective-permute-start) | collective-permute-done | bytes 32800 | tf_op jit(solution)/shard_map/ppermute | solution.py:36
  5.8 2.1 %collective-permute-start.1 = (bf16[64,512]{1,0:T(8,128)(2,1)S(1)}, bf16[64,512]{1,0:T(8,128)(2,1)S(1)}, u32[]{:S(2)}, u32[]{:S(2)}) collective-permute-start(bf16[64,512]{1,0:T(8,128)(2,1)S(1)} %get-tuple-element.12), channel_id=1, source_target_pairs={{0,4},{1,5},{2,6},{3,7},{4,0},{5,1},{6,2},{7,3},{8,12},{9,13},{10,... | collective-permute-start | bytes 196616 | tf_op jit(solution)/shard_map/ppermute | solution.py:36
  7.8 2.6 %collective-permute-start.2 = (bf16[64,512]{1,0:T(8,128)(2,1)S(1)}, bf16[64,512]{1,0:T(8,128)(2,1)S(1)}, u32[]{:S(2)}, u32[]{:S(2)}) collective-permute-start(bf16[64,512]{1,0:T(8,128)(2,1)S(1)} %get-tuple-element.12), channel_id=1, source_target_pairs={{0,8},{1,9},{2,10},{3,11},{4,12},{5,13},{6,14},{7,15},{8,0},{9,1},... | collective-permute-start | bytes 196616 | tf_op jit(solution)/shard_map/ppermute | solution.py:36
  10.4 0.0 collective-permute-start.3
  10.4 0.3 collective-permute-done.1
  10.7 3.7 %collective-permute-done.2 = bf16[64,512]{1,0:T(8,128)(2,1)S(1)} collective-permute-done((bf16[64,512]{1,0:T(8,128)(2,1)S(1)}, bf16[64,512]{1,0:T(8,128)(2,1)S(1)}, u32[]{:S(2)}, u32[]{:S(2)}) %collective-permute-start.2) | collective-permute-done | bytes 65568 | tf_op jit(solution)/shard_map/ppermute | solution.py:36
  14.4 2.1 %collective-permute-done.3 = bf16[64,512]{1,0:T(8,128)(2,1)S(1)} collective-permute-done((bf16[64,512]{1,0:T(8,128)(2,1)S(1)}, bf16[64,512]{1,0:T(8,128)(2,1)S(1)}, u32[]{:S(2)}, u32[]{:S(2)}) %collective-permute-start.3) | collective-permute-done | bytes 65568 | tf_op jit(solution)/shard_map/ppermute | solution.py:36
  16.5 0.0 collective-permute-start.4
  16.5 0.0 copy-start.1
  16.5 1.1 %copy-done.1 = f32[64,3072]{1,0:T(8,128)S(1)} copy-done((f32[64,3072]{1,0:T(8,128)S(1)}, f32[64,3072]{1,0:T(8,128)}, u32[]{:S(2)}) %copy-start.1) | copy-done | bytes 786456
  17.7 0.0 copy-start.2
  17.7 0.9 %copy-done.2 = f32[6,64,64]{2,1,0:T(8,128)S(1)} copy-done((f32[6,64,64]{2,1,0:T(8,128)S(1)}, f32[6,64,64]{2,1,0:T(8,128)}, u32[]{:S(2)}) %copy-start.2) | copy-done | bytes 98328
  18.6 0.0 copy-start.3
  18.6 0.8 %copy-done.3 = f32[1,64,64]{2,1,0:T(8,128)S(1)} copy-done((f32[1,64,64]{2,1,0:T(8,128)S(1)}, f32[1,64,64]{2,1,0:T(8,128)}, u32[]{:S(2)}) %copy-start.3) | copy-done | bytes 16408
  19.3 0.0 copy-start.6
  19.3 0.7 %copy-done.6 = s32[1,32]{1,0:T(1,128)S(1)} copy-done((s32[1,32]{1,0:T(1,128)S(1)}, s32[1,32]{1,0:T(1,128)}, u32[]{:S(2)}) %copy-start.6) | copy-done | bytes 152
  20.0 0.0 copy-start.4
  20.0 2.3 %prepare.1 = (bf16[512,512]{1,0:T(8,128)(2,1)S(1)}, f32[128,3072]{1,0:T(8,128)S(1)}) custom-call(s32[1,32]{1,0:T(1,128)S(1)} %copy-done.6, f32[64,3072]{1,0:T(8,128)S(1)} %copy-done.1, f32[6,64,64]{2,1,0:T(8,128)S(1)} %copy-done.2, f32[1,64,64]{2,1,0:T(8,128)S(1)} %copy-done.3), custom_call_target="tpu_custom_call" | custom-call | flops 301989888 | bytes 8388608 | tf_op jit(solution)/shard_map/prepare/pallas_call | solution.py:318
  22.3 0.0 copy-start.9
  22.3 0.0 copy-start.7
  22.4 0.0 copy-start.8
  22.4 0.0 collective-permute-done.4.other_ref
  22.4 0.0 copy-start
  22.4 1.9 %copy-done = bf16[3072,512]{1,0:T(8,128)(2,1)S(1)} copy-done((bf16[3072,512]{1,0:T(8,128)(2,1)S(1)}, bf16[3072,512]{1,0:T(8,128)(2,1)}, u32[]{:S(2)}) %copy-start) | copy-done | bytes 3145752
  24.3 0.0 copy-start.5
  24.3 0.7 %copy-done.5 = s32[3,6]{1,0:T(4,128)S(1)} copy-done((s32[3,6]{1,0:T(4,128)S(1)}, s32[3,6]{1,0:T(4,128)}, u32[]{:S(2)}) %copy-start.5) | copy-done | bytes 96
  25.0 5.4 %density.1 = (f32[24,128]{1,0:T(8,128)}, f32[32,128]{1,0:T(8,128)S(1)}, f32[32,2,128]{2,1,0:T(2,128)}) custom-call(s32[1,32]{1,0:T(1,128)S(1)} %copy-done.6, s32[3,6]{1,0:T(4,128)S(1)} %copy-done.5, bf16[3072,512]{1,0:T(8,128)(2,1)S(1)} %copy-done, bf16[256,512]{1,0:T(8,128)(2,1)S(1)} %constant_dynamic-update-slice_fusion.2.held_ref, ...), custom_call_target="tpu_custom_call" | custom-call | flops 1610612736 | bytes 8388608 | tf_op jit(solution)/shard_map/density/pallas_call | solution.py:335
  30.4 3.4 %all-to-all-start = ((f32[32,2,128]{2,1,0:T(2,128)}), f32[32,2,128]{2,1,0:T(2,128)S(1)}, u32[]{:S(2)}, u32[]{:S(2)}) async-start(f32[32,2,128]{2,1,0:T(2,128)} %get-tuple-element.11), calls=%async_computation | async-start | bytes 65536 | tf_op jit(solution)/shard_map/all_to_all | solution.py:359
  33.8 0.3 collective-permute-start.5
  34.1 0.7 %collective-permute-start.6 = (f32[32,128]{1,0:T(8,128)S(1)}, f32[32,128]{1,0:T(8,128)S(1)}, u32[]{:S(2)}, u32[]{:S(2)}) collective-permute-start(f32[32,128]{1,0:T(8,128)S(1)} %get-tuple-element.10.halo_ref), channel_id=1, source_target_pairs={{1,2},{2,1},{3,4},{4,3},{5,6},{6,5},{7,8},{8,7},{9,10},{10,9},{11,... | collective-permute-start | bytes 49160 | tf_op jit(solution)/shard_map/ppermute | solution.py:358
  34.8 0.0 copy-done.9
  34.8 0.1 copy.12.leaves_ref
  34.9 0.2 collective-permute-done.5.even_ref
  35.0 0.0 collective-permute-done.6.odd_ref
  35.1 6.0 %all-to-all-done.expansion_ref = f32[32,2,128]{2,1,0:T(2,128)S(1)} async-done(((f32[32,2,128]{2,1,0:T(2,128)}), f32[32,2,128]{2,1,0:T(2,128)S(1)}, u32[]{:S(2)}, u32[]{:S(2)}) %all-to-all-start) | async-done | bytes 32800 | tf_op jit(solution)/shard_map/all_to_all | solution.py:359
  41.0 0.0 copy-done.4
  41.1 0.0 copy-done.7
  41.1 0.0 copy-done.8
  41.1 4.8 %potential.1 = f32[24,128]{1,0:T(8,128)} custom-call(s32[6,3]{1,0:T(8,128)S(1)} %copy.12.leaves_ref, s32[1,16]{1,0:T(1,128)S(1)} %copy-done.7, s32[1,2]{1,0:T(1,128)S(1)} %copy-done.8, f32[32,128]{1,0:T(8,128)S(1)} %get-tuple-element.10.halo_ref, f32[32,128]{1,0:T(8,128)S(1)} %collective-permute-done.5.even_ref, ...), custom_call_target="tpu_custom_call" | custom-call | flops 20971520 | bytes 2097152 | tf_op jit(solution)/shard_map/potential/pallas_call | solution.py:361
  (4 shorter events, 0.0 us)
Async XLA Ops:
  0.6 5.1 %collective-permute-start = (bf16[32,512]{1,0:T(8,128)(2,1)}, bf16[32,512]{1,0:T(8,128)(2,1)S(1)}, u32[]{:S(2)}, u32[]{:S(2)}) collective-permute-start(bf16[32,512]{1,0:T(8,128)(2,1)} %param.11), channel_id=1, source_target_pairs={{0,2},{1,3},{2,0},{3,1},{4,6},{5,7},{6,4},{7,5},{8,10},{9,11},{10,... | collective-permute-start | bytes 98312 | tf_op jit(solution)/shard_map/ppermute | solution.py:36
  5.8 5.0 %collective-permute-start.1 = (bf16[64,512]{1,0:T(8,128)(2,1)S(1)}, bf16[64,512]{1,0:T(8,128)(2,1)S(1)}, u32[]{:S(2)}, u32[]{:S(2)}) collective-permute-start(bf16[64,512]{1,0:T(8,128)(2,1)S(1)} %get-tuple-element.12), channel_id=1, source_target_pairs={{0,4},{1,5},{2,6},{3,7},{4,0},{5,1},{6,2},{7,3},{8,12},{9,13},{10,... | collective-permute-start | bytes 196616 | tf_op jit(solution)/shard_map/ppermute | solution.py:36
  7.8 6.6 %collective-permute-start.2 = (bf16[64,512]{1,0:T(8,128)(2,1)S(1)}, bf16[64,512]{1,0:T(8,128)(2,1)S(1)}, u32[]{:S(2)}, u32[]{:S(2)}) collective-permute-start(bf16[64,512]{1,0:T(8,128)(2,1)S(1)} %get-tuple-element.12), channel_id=1, source_target_pairs={{0,8},{1,9},{2,10},{3,11},{4,12},{5,13},{6,14},{7,15},{8,0},{9,1},... | collective-permute-start | bytes 196616 | tf_op jit(solution)/shard_map/ppermute | solution.py:36
  10.4 6.1 %collective-permute-start.3 = (bf16[64,512]{1,0:T(8,128)(2,1)S(1)}, bf16[64,512]{1,0:T(8,128)(2,1)S(1)}, u32[]{:S(2)}, u32[]{:S(2)}) collective-permute-start(bf16[64,512]{1,0:T(8,128)(2,1)S(1)} %get-tuple-element.12), channel_id=1, source_target_pairs={{0,12},{1,13},{2,14},{3,15},{4,8},{5,9},{6,10},{7,11},{8,4},{9,5},... | collective-permute-start | bytes 196616 | tf_op jit(solution)/shard_map/ppermute | solution.py:36
  16.5 5.9 %collective-permute-start.4 = (bf16[256,512]{1,0:T(8,128)(2,1)S(1)}, bf16[256,512]{1,0:T(8,128)(2,1)S(1)}, u32[]{:S(2)}, u32[]{:S(2)}) collective-permute-start(bf16[256,512]{1,0:T(8,128)(2,1)S(1)} %constant_dynamic-update-slice_fusion.2.held_ref), channel_id=1, source_target_pairs={{0,1},{1,0},{2,3},{3,2},{4,5},{5,4},{6,7},{7,6},{8,9},{9,8},{10,11... | collective-permute-start | bytes 786440 | tf_op jit(solution)/shard_map/ppermute | solution.py:36
  16.5 1.1 %copy-start.1 = (f32[64,3072]{1,0:T(8,128)S(1)}, f32[64,3072]{1,0:T(8,128)}, u32[]{:S(2)}) copy-start(f32[64,3072]{1,0:T(8,128)} %basis_ref.1) | copy-start | bytes 2359300
  17.7 0.9 %copy-start.2 = (f32[6,64,64]{2,1,0:T(8,128)S(1)}, f32[6,64,64]{2,1,0:T(8,128)}, u32[]{:S(2)}) copy-start(f32[6,64,64]{2,1,0:T(8,128)} %transfer_ref.1) | copy-start | bytes 294916
  18.6 0.8 %copy-start.3 = (f32[1,64,64]{2,1,0:T(8,128)S(1)}, f32[1,64,64]{2,1,0:T(8,128)}, u32[]{:S(2)}) copy-start(f32[1,64,64]{2,1,0:T(8,128)} %dev_ref.3) | copy-start | bytes 49156
  19.3 0.7 %copy-start.6 = (s32[1,32]{1,0:T(1,128)S(1)}, s32[1,32]{1,0:T(1,128)}, u32[]{:S(2)}) copy-start(s32[1,32]{1,0:T(1,128)} %near_ref.3) | copy-start | bytes 388
  20.0 21.1 %copy-start.4 = (f32[1,64,64]{2,1,0:T(8,128)S(1)}, f32[1,64,64]{2,1,0:T(8,128)}, u32[]{:S(2)}) copy-start(f32[1,64,64]{2,1,0:T(8,128)} %dev_ref.3) | copy-start | bytes 49156
  22.3 12.4 %copy-start.9 = (s32[6,3]{0,1:T(4,128)S(1)}, s32[6,3]{0,1:T(4,128)}, u32[]{:S(2)}) copy-start(s32[6,3]{0,1:T(4,128)} %param.14) | copy-start | bytes 220
  22.3 18.7 %copy-start.7 = (s32[1,16]{1,0:T(1,128)S(1)}, s32[1,16]{1,0:T(1,128)}, u32[]{:S(2)}) copy-start(s32[1,16]{1,0:T(1,128)} %far_ref.1) | copy-start | bytes 196
  22.4 18.7 %copy-start.8 = (s32[1,2]{1,0:T(1,128)S(1)}, s32[1,2]{1,0:T(1,128)}, u32[]{:S(2)}) copy-start(s32[1,2]{1,0:T(1,128)} %group_far_ref.1) | copy-start | bytes 28
  22.4 1.9 %copy-start = (bf16[3072,512]{1,0:T(8,128)(2,1)S(1)}, bf16[3072,512]{1,0:T(8,128)(2,1)}, u32[]{:S(2)}) copy-start(bf16[3072,512]{1,0:T(8,128)(2,1)} %orbitals_ref.1) | copy-start | bytes 9437188
  24.3 0.7 %copy-start.5 = (s32[3,6]{1,0:T(4,128)S(1)}, s32[3,6]{1,0:T(4,128)}, u32[]{:S(2)}) copy-start(s32[3,6]{1,0:T(4,128)} %coords_ref.1) | copy-start | bytes 220
  30.4 10.6 %all-to-all-start = ((f32[32,2,128]{2,1,0:T(2,128)}), f32[32,2,128]{2,1,0:T(2,128)S(1)}, u32[]{:S(2)}, u32[]{:S(2)}) async-start(f32[32,2,128]{2,1,0:T(2,128)} %get-tuple-element.11), calls=%async_computation | async-start | bytes 65536 | tf_op jit(solution)/shard_map/all_to_all | solution.py:359
  33.8 1.2 %collective-permute-start.5 = (f32[32,128]{1,0:T(8,128)S(1)}, f32[32,128]{1,0:T(8,128)S(1)}, u32[]{:S(2)}, u32[]{:S(2)}) collective-permute-start(f32[32,128]{1,0:T(8,128)S(1)} %get-tuple-element.10.halo_ref), channel_id=1, source_target_pairs={{0,1},{1,0},{2,3},{3,2},{4,5},{5,4},{6,7},{7,6},{8,9},{9,8},{10,11... | collective-permute-start | bytes 49160 | tf_op jit(solution)/shard_map/ppermute | solution.py:36
  34.1 0.9 %collective-permute-start.6 = (f32[32,128]{1,0:T(8,128)S(1)}, f32[32,128]{1,0:T(8,128)S(1)}, u32[]{:S(2)}, u32[]{:S(2)}) collective-permute-start(f32[32,128]{1,0:T(8,128)S(1)} %get-tuple-element.10.halo_ref), channel_id=1, source_target_pairs={{1,2},{2,1},{3,4},{4,3},{5,6},{6,5},{7,8},{8,7},{9,10},{10,9},{11,... | collective-permute-start | bytes 49160 | tf_op jit(solution)/shard_map/ppermute | solution.py:358

commit v2 on v1

--- a/solution.py
+++ b/solution.py
@@ -36,11 +36,19 @@
     return lax.ppermute(value, axis, [(i, i ^ mask) for i in range(lax.axis_size(axis))])
 
 
-def gather_rows(rows):
-    held = rows
-    for masks in xor_stages(lax.axis_size("dom")):
-        held = jnp.concatenate([held] + [swap(held, "dom", m) for m in masks], axis=0)
-    return held, swap(held, "dom", 1)
+def farthest_first(mask):
+    return -(mask & -mask), -mask
+
+
+def gather_rows(rows, beside):
+    held, result = rows, None
+    for stage, masks in enumerate(xor_stages(lax.axis_size("dom"))):
+        if stage == 1:
+            result = beside(held)
+        arrived = {m: swap(held, "dom", m) for m in sorted(masks, key=farthest_first)}
+        held = jnp.concatenate([held] + [arrived[m] for m in masks], axis=0)
+    held, result = lax.optimization_barrier((held, result))
+    return held, swap(held, "dom", 1), result
 
 
 def iota(shape, dim):
@@ -55,7 +63,29 @@
     return lax.dot_general(ones, both, (((1,), (1,)), ((), ())), preferred_element_type=jnp.float32)
 
 
-def prepare_kernel(near_ref, basis_ref, transfer_ref, dev_ref, pick_ref, weights_ref):
+def prepare_kernel(
+    near_hbm,
+    basis_hbm,
+    transfer_hbm,
+    dev_hbm,
+    orbitals_hbm,
+    gate_ref,
+    orbit_ref,
+    pick_ref,
+    weights_ref,
+    near_ref,
+    basis_ref,
+    transfer_ref,
+    dev_ref,
+    sems,
+):
+    del gate_ref
+    moves = ((near_hbm, near_ref), (transfer_hbm, transfer_ref), (dev_hbm, dev_ref))
+    moves += ((basis_hbm, basis_ref), (orbitals_hbm, orbit_ref))
+    copies = [pltpu.make_async_copy(a, b, sems.at[i]) for i, (a, b) in enumerate(moves)]
+    for copy in copies:
+        copy.start()
+    copies[0].wait()
     blocks = near_ref.shape[1]
     width = blocks * BW
     spread = (iota((blocks, width), 1) // BW == iota((blocks, width), 0)).astype(jnp.float32)
@@ -66,6 +96,8 @@
         size = min(LEAF, pick_ref.shape[0] - start)
         hit = iota((size, width), 0) + start == column
         pick_ref[start : start + size, :] = jnp.where(hit, 1.0, 0.0).astype(jnp.bfloat16)
+    for copy in copies[1:4]:
+        copy.wait()
     dev = dev_ref[0]
     for leaf in range(transfer_ref.shape[0]):
         points = slice(leaf * LEAF, (leaf + 1) * LEAF)
@@ -80,12 +112,13 @@
         weights_ref[RANK:, points] = lax.dot_general(
             dev, own, (((0,), (0,)), ((), ())), precision=HIGHEST, preferred_element_type=jnp.float32
         )
+    copies[4].wait()
 
 
 def density_kernel(
     near_ref,
     coords_ref,
-    orbitals_ref,
+    orbit_ref,
     held_ref,
     other_ref,
     pick_ref,
@@ -94,17 +127,8 @@
     halo_ref,
     expansion_ref,
     rows_ref,
-    orbit_ref,
-    sems,
 ):
     leaves = coords_ref.shape[1]
-    copies = []
-    for leaf in range(leaves):
-        points = pl.ds(leaf * LEAF, LEAF)
-        copies.append(
-            pltpu.make_async_copy(orbitals_ref.at[points], orbit_ref.at[points], sems.at[leaf])
-        )
-        copies[-1].start()
     me = lax.axis_index("dom")
     for k in range(near_ref.shape[1]):
         block = near_ref[0, k]
@@ -117,7 +141,6 @@
     matrix = matrix.astype(jnp.bfloat16)
     total = jnp.zeros((2 * RANK, LANES), jnp.float32)
     for leaf in range(leaves):
-        copies[leaf].wait()
         orbit = orbit_ref[leaf * LEAF : (leaf + 1) * LEAF, :]
         product = jnp.dot(orbit, matrix, preferred_element_type=jnp.float32)
         product = product * orbit.astype(jnp.float32)
@@ -290,8 +313,13 @@
     lax.fori_loop(0, leaves, one_leaf, 0)
 
 
+def in_hbm(x):
+    return pltpu.with_memory_space_constraint(x, pltpu.HBM)
+
+
 VMEM = pl.BlockSpec(memory_space=pltpu.VMEM)
 SMEM = pl.BlockSpec(memory_space=pltpu.SMEM)
+HBM = pl.BlockSpec(memory_space=pltpu.HBM)
 
 
 def local(
@@ -315,22 +343,31 @@
     f32 = jnp.float32
     params = pltpu.CompilerParams(vmem_limit_bytes=(24 << 20) + 4 * natural * natural)
 
-    pick, weights = pl.pallas_call(
-        prepare_kernel,
-        out_shape=(
-            jax.ShapeDtypeStruct((natural, width), jnp.bfloat16),
-            jax.ShapeDtypeStruct((2 * RANK, points), f32),
-        ),
-        in_specs=[VMEM] * 4,
-        out_specs=(VMEM, VMEM),
-        compiler_params=params,
-        cost_estimate=pl.CostEstimate(
-            flops=2 * 6 * 2 * RANK * RANK * points, bytes_accessed=8 << 20, transcendentals=0
-        ),
-        name="prepare",
-    )(near_blocks, leaf_basis, leaf_transfer, dev_transfer)
-
-    held, other = gather_rows(density_rows)
+    def prepare(gate):
+        return pl.pallas_call(
+            prepare_kernel,
+            out_shape=(
+                jax.ShapeDtypeStruct((points, width), jnp.bfloat16),
+                jax.ShapeDtypeStruct((natural, width), jnp.bfloat16),
+                jax.ShapeDtypeStruct((2 * RANK, points), f32),
+            ),
+            in_specs=[HBM] * 5 + [pl.BlockSpec(memory_space=pl.ANY)],
+            out_specs=(VMEM, VMEM, VMEM),
+            scratch_shapes=[
+                pltpu.VMEM(near_blocks.shape, jnp.int32),
+                pltpu.VMEM(leaf_basis.shape, f32),
+                pltpu.VMEM(leaf_transfer.shape, f32),
+                pltpu.VMEM(dev_transfer.shape, f32),
+                pltpu.SemaphoreType.DMA((5,)),
+            ],
+            compiler_params=params,
+            cost_estimate=pl.CostEstimate(
+                flops=2 * 6 * 2 * RANK * RANK * points, bytes_accessed=8 << 20, transcendentals=0
+            ),
+            name="prepare",
+        )(*[in_hbm(x) for x in (near_blocks, leaf_basis, leaf_transfer, dev_transfer, orbitals)], gate)
+
+    held, other, (orbit, pick, weights) = gather_rows(density_rows, prepare)
 
     density, halo, expansion = pl.pallas_call(
         density_kernel,
@@ -339,19 +376,15 @@
             jax.ShapeDtypeStruct((rows + 8, LANES), f32),
             jax.ShapeDtypeStruct((devices, 2, LANES), f32),
         ),
-        in_specs=[SMEM, VMEM, pl.BlockSpec(memory_space=pl.ANY)] + [VMEM] * 4,
+        in_specs=[SMEM] + [VMEM] * 6,
         out_specs=(VMEM, VMEM, VMEM),
-        scratch_shapes=[
-            pltpu.VMEM((width, natural), jnp.bfloat16),
-            pltpu.VMEM((points, width), jnp.bfloat16),
-            pltpu.SemaphoreType.DMA((leaves,)),
-        ],
+        scratch_shapes=[pltpu.VMEM((width, natural), jnp.bfloat16)],
         compiler_params=params,
         cost_estimate=pl.CostEstimate(
             flops=2 * points * width * width, bytes_accessed=8 << 20, transcendentals=0
         ),
         name="density",
-    )(near_blocks, leaf_coords, orbitals, held, other, pick, weights)
+    )(near_blocks, leaf_coords, orbit, held, other, pick, weights)
 
     even = swap(halo, "dom", 1)
     pairs = [(i, i + 1 if i % 2 else i - 1) for i in range(1, dom_count - 1)]

time: 46.3 us -> 38.7 us (0.84)
  local copies, waits for them, and re-layouts: 6.99 us -> 0.95 us
  waiting for transfers between devices: 13.5 us -> 11.4 us
  starting transfers between devices: 12 us -> 12.5 us
    unnamed x24 -> x16, local copies, waits for them, and re-layouts: 6.98 us -> 0.94 us
    ppermute x6, waiting for transfers between devices: 7.53 us -> 5.39 us  [swap(): lax.ppermute(value, axis, [(i, i ^ mask) for i in range(lax.axis_size(axi...]
    pallas_call x1, Pallas kernels: 2.32 us -> 3.59 us  [prepare(): pl.pallas_call(prepare_kernel, out_shape=(jax.ShapeDtypeStruct((points, w...]
    pallas_call x1, Pallas kernels: 5.44 us -> 4.46 us  [local(): pl.pallas_call(density_kernel, out_shape=(jax.ShapeDtypeStruct((rows, LAN...]
  transfers between devices with their start and end apart: 8 -> 8, of which waited for: 6 -> 6; matrix products, arithmetic and copies ran while one was open for 2% -> 2% of each run, Pallas kernels for 5% -> 9%
where the time goes in v2:
time: 38.7 us; the launch traced here: 38.4 us
  Pallas kernels  12.9 us (33%)
  starting transfers between devices  12.5 us (32%)
  waiting for transfers between devices  11.4 us (29%)
  local copies, waits for them, and re-layouts  0.95 us (2%)
  between operations  0.75 us (2%)
    ppermute x6, starting transfers between devices, swap(): lax.ppermute(value, axis, [(i, i ^ mask) for i in range(lax.axis_size(axi...  8.02 us
    all_to_all x1, waiting for transfers between devices, local(): everyone = lax.all_to_all(expansion, ('group', 'dom'), 0, 0)  6 us
    ppermute x6, waiting for transfers between devices, swap(): lax.ppermute(value, axis, [(i, i ^ mask) for i in range(lax.axis_size(axi...  5.39 us
    pallas_call x1, Pallas kernels, local(): pl.pallas_call(potential_kernel, out_shape=jax.ShapeDtypeStruct((rows, LA...  4.84 us
    pallas_call x1, Pallas kernels, local(): pl.pallas_call(density_kernel, out_shape=(jax.ShapeDtypeStruct((rows, LAN...  4.46 us
    all_to_all x1, starting transfers between devices, local(): everyone = lax.all_to_all(expansion, ('group', 'dom'), 0, 0)  3.79 us
    pallas_call x1, Pallas kernels, prepare(): pl.pallas_call(prepare_kernel, out_shape=(jax.ShapeDtypeStruct((points, w...  3.59 us
    unnamed x16, local copies, waits for them, and re-layouts  0.94 us
  transfers between devices with their start and end apart: 8, of which 6 were waited for; matrix products, arithmetic and copies ran while one was open for 2% of the time, Pallas kernels for 9%

profile of v2, /device:TPU:0, one launch (start us, length us, event | category | flops | bytes accessed | tf_op | source)
XLA Modules:
  0.0 38.4 jit_solution(6967825072763348470)
XLA Ops:
  0.6 0.0 copy-start.1
  0.6 0.0 copy-start.2
  0.7 3.0 %collective-permute-start = (bf16[32,512]{1,0:T(8,128)(2,1)}, bf16[32,512]{1,0:T(8,128)(2,1)S(1)}, u32[]{:S(2)}, u32[]{:S(2)}) collective-permute-start(bf16[32,512]{1,0:T(8,128)(2,1)} %param.11), channel_id=1, source_target_pairs={{0,2},{1,3},{2,0},{3,1},{4,6},{5,7},{6,4},{7,5},{8,10},{9,11},{10,... | collective-permute-start | bytes 98312 | tf_op jit(solution)/shard_map/ppermute | solution.py:36
  3.7 0.8 %constant_dynamic-update-slice_fusion.1 = (bf16[64,512]{1,0:T(8,128)(2,1)S(1)}, bf16[256,512]{1,0:T(8,128)(2,1)S(1)}) fusion(bf16[32,512]{1,0:T(8,128)(2,1)} %param.11), kind=kLoop, calls=%fused_computation.1 | loop fusion | bytes 98304
  4.5 1.3 %collective-permute-done = bf16[32,512]{1,0:T(8,128)(2,1)S(1)} collective-permute-done((bf16[32,512]{1,0:T(8,128)(2,1)}, bf16[32,512]{1,0:T(8,128)(2,1)S(1)}, u32[]{:S(2)}, u32[]{:S(2)}) %collective-permute-start) | collective-permute-done | bytes 32800 | tf_op jit(solution)/shard_map/ppermute | solution.py:36
  5.8 2.1 %collective-permute-start.1 = (bf16[64,512]{1,0:T(8,128)(2,1)S(1)}, bf16[64,512]{1,0:T(8,128)(2,1)S(1)}, u32[]{:S(2)}, u32[]{:S(2)}) collective-permute-start(bf16[64,512]{1,0:T(8,128)(2,1)S(1)} %get-tuple-element.22.gate_ref), channel_id=1, source_target_pairs={{0,4},{1,5},{2,6},{3,7},{4,0},{5,1},{6,2},{7,3},{8,12},{9,13},{10,... | collective-permute-start | bytes 196616 | tf_op jit(solution)/shard_map/ppermute | solution.py:36
  7.9 2.6 %collective-permute-start.2 = (bf16[64,512]{1,0:T(8,128)(2,1)S(1)}, bf16[64,512]{1,0:T(8,128)(2,1)S(1)}, u32[]{:S(2)}, u32[]{:S(2)}) collective-permute-start(bf16[64,512]{1,0:T(8,128)(2,1)S(1)} %get-tuple-element.22.gate_ref), channel_id=1, source_target_pairs={{0,8},{1,9},{2,10},{3,11},{4,12},{5,13},{6,14},{7,15},{8,0},{9,1},... | collective-permute-start | bytes 196616 | tf_op jit(solution)/shard_map/ppermute | solution.py:36
  10.5 0.0 collective-permute-start.3
  10.5 3.6 %prepare.1 = (bf16[3072,512]{1,0:T(8,128)(2,1)S(1)}, bf16[512,512]{1,0:T(8,128)(2,1)S(1)}, f32[128,3072]{1,0:T(8,128)S(1)}) custom-call(s32[1,32]{1,0:T(1,128)} %near_ref.1, f32[64,3072]{1,0:T(8,128)} %basis_hbm.1, f32[6,64,64]{2,1,0:T(8,128)} %transfer_hbm.1, f32[1,64,64]{2,1,0:T(8,128)} %dev_ref.1, bf16[3072,512]{1,0:T(8,128)(2,1)} %orbitals_hbm.1, ...), custom_call_target="tpu_custom_call" | custom-call | flops 301989888 | bytes 8388608 | tf_op jit(solution)/shard_map/prepare/pallas_call | solution.py:347
  14.1 0.0 collective-permute-done.1
  14.1 0.0 copy-start.5
  14.1 0.0 copy-start
  14.1 0.0 copy-start.3
  14.1 0.0 copy-start.4
  14.1 0.3 collective-permute-done.2
  14.4 2.1 %collective-permute-done.3 = bf16[64,512]{1,0:T(8,128)(2,1)S(1)} collective-permute-done((bf16[64,512]{1,0:T(8,128)(2,1)S(1)}, bf16[64,512]{1,0:T(8,128)(2,1)S(1)}, u32[]{:S(2)}, u32[]{:S(2)}) %collective-permute-start.3) | collective-permute-done | bytes 65568 | tf_op jit(solution)/shard_map/ppermute | solution.py:36
  16.5 0.0 collective-permute-start.4
  16.5 1.5 %collective-permute-done.4.other_ref = bf16[256,512]{1,0:T(8,128)(2,1)S(1)} collective-permute-done((bf16[256,512]{1,0:T(8,128)(2,1)S(1)}, bf16[256,512]{1,0:T(8,128)(2,1)S(1)}, u32[]{:S(2)}, u32[]{:S(2)}) %collective-permute-start.4) | collective-permute-done | bytes 262176 | tf_op jit(solution)/shard_map/ppermute | solution.py:36
  18.1 0.0 copy-done.1
  18.1 0.0 copy-done.2
  18.1 4.5 %density.1 = (f32[24,128]{1,0:T(8,128)}, f32[32,128]{1,0:T(8,128)S(1)}, f32[32,2,128]{2,1,0:T(2,128)}) custom-call(s32[1,32]{1,0:T(1,128)S(1)} %copy-done.1, s32[3,6]{1,0:T(4,128)S(1)} %copy-done.2, bf16[3072,512]{1,0:T(8,128)(2,1)S(1)} %get-tuple-element.15.orbit_ref, bf16[256,512]{1,0:T(8,128)(2,1)S(1)} %constant_dynamic-update-slice_fusion.2.held_ref, ...), custom_call_target="tpu_custom_call" | custom-call | flops 1610612736 | bytes 8388608 | tf_op jit(solution)/shard_map/density/pallas_call | solution.py:372
  22.5 3.8 %all-to-all-start = ((f32[32,2,128]{2,1,0:T(2,128)}), f32[32,2,128]{2,1,0:T(2,128)S(1)}, u32[]{:S(2)}, u32[]{:S(2)}) async-start(f32[32,2,128]{2,1,0:T(2,128)} %get-tuple-element.21), calls=%async_computation | async-start | bytes 65536 | tf_op jit(solution)/shard_map/all_to_all | solution.py:392
  26.3 0.3 collective-permute-start.5
  26.7 0.7 %collective-permute-start.6 = (f32[32,128]{1,0:T(8,128)S(1)}, f32[32,128]{1,0:T(8,128)S(1)}, u32[]{:S(2)}, u32[]{:S(2)}) collective-permute-start(f32[32,128]{1,0:T(8,128)S(1)} %get-tuple-element.20.halo_ref), channel_id=1, source_target_pairs={{1,2},{2,1},{3,4},{4,3},{5,6},{6,5},{7,8},{8,7},{9,10},{10,9},{11,... | collective-permute-start | bytes 49160 | tf_op jit(solution)/shard_map/ppermute | solution.py:391
  27.3 0.0 copy-done.5
  27.3 0.1 copy.12.leaves_ref
  27.4 0.2 collective-permute-done.5.even_ref
  27.6 0.0 collective-permute-done.6.odd_ref
  27.6 6.0 %all-to-all-done.expansion_ref = f32[32,2,128]{2,1,0:T(2,128)S(1)} async-done(((f32[32,2,128]{2,1,0:T(2,128)}), f32[32,2,128]{2,1,0:T(2,128)S(1)}, u32[]{:S(2)}, u32[]{:S(2)}) %all-to-all-start) | async-done | bytes 32800 | tf_op jit(solution)/shard_map/all_to_all | solution.py:392
  33.6 0.0 copy-done
  33.6 0.0 copy-done.3
  33.6 0.0 copy-done.4
  33.6 4.8 %potential.1 = f32[24,128]{1,0:T(8,128)} custom-call(s32[6,3]{1,0:T(8,128)S(1)} %copy.12.leaves_ref, s32[1,16]{1,0:T(1,128)S(1)} %copy-done.3, s32[1,2]{1,0:T(1,128)S(1)} %copy-done.4, f32[32,128]{1,0:T(8,128)S(1)} %get-tuple-element.20.halo_ref, f32[32,128]{1,0:T(8,128)S(1)} %collective-permute-done.5.even_ref, ...), custom_call_target="tpu_custom_call" | custom-call | flops 20971520 | bytes 2097152 | tf_op jit(solution)/shard_map/potential/pallas_call | solution.py:394
  (4 shorter events, 0.0 us)
Async XLA Ops:
  0.6 17.4 %copy-start.1 = (s32[1,32]{1,0:T(1,128)S(1)}, s32[1,32]{1,0:T(1,128)}, u32[]{:S(2)}) copy-start(s32[1,32]{1,0:T(1,128)} %near_ref.1) | copy-start | bytes 388
  0.6 17.4 %copy-start.2 = (s32[3,6]{1,0:T(4,128)S(1)}, s32[3,6]{1,0:T(4,128)}, u32[]{:S(2)}) copy-start(s32[3,6]{1,0:T(4,128)} %coords_ref.1) | copy-start | bytes 220
  0.7 5.1 %collective-permute-start = (bf16[32,512]{1,0:T(8,128)(2,1)}, bf16[32,512]{1,0:T(8,128)(2,1)S(1)}, u32[]{:S(2)}, u32[]{:S(2)}) collective-permute-start(bf16[32,512]{1,0:T(8,128)(2,1)} %param.11), channel_id=1, source_target_pairs={{0,2},{1,3},{2,0},{3,1},{4,6},{5,7},{6,4},{7,5},{8,10},{9,11},{10,... | collective-permute-start | bytes 98312 | tf_op jit(solution)/shard_map/ppermute | solution.py:36
  5.8 8.3 %collective-permute-start.1 = (bf16[64,512]{1,0:T(8,128)(2,1)S(1)}, bf16[64,512]{1,0:T(8,128)(2,1)S(1)}, u32[]{:S(2)}, u32[]{:S(2)}) collective-permute-start(bf16[64,512]{1,0:T(8,128)(2,1)S(1)} %get-tuple-element.22.gate_ref), channel_id=1, source_target_pairs={{0,4},{1,5},{2,6},{3,7},{4,0},{5,1},{6,2},{7,3},{8,12},{9,13},{10,... | collective-permute-start | bytes 196616 | tf_op jit(solution)/shard_map/ppermute | solution.py:36
  7.9 6.6 %collective-permute-start.2 = (bf16[64,512]{1,0:T(8,128)(2,1)S(1)}, bf16[64,512]{1,0:T(8,128)(2,1)S(1)}, u32[]{:S(2)}, u32[]{:S(2)}) collective-permute-start(bf16[64,512]{1,0:T(8,128)(2,1)S(1)} %get-tuple-element.22.gate_ref), channel_id=1, source_target_pairs={{0,8},{1,9},{2,10},{3,11},{4,12},{5,13},{6,14},{7,15},{8,0},{9,1},... | collective-permute-start | bytes 196616 | tf_op jit(solution)/shard_map/ppermute | solution.py:36
  10.5 6.1 %collective-permute-start.3 = (bf16[64,512]{1,0:T(8,128)(2,1)S(1)}, bf16[64,512]{1,0:T(8,128)(2,1)S(1)}, u32[]{:S(2)}, u32[]{:S(2)}) collective-permute-start(bf16[64,512]{1,0:T(8,128)(2,1)S(1)} %get-tuple-element.22.gate_ref), channel_id=1, source_target_pairs={{0,12},{1,13},{2,14},{3,15},{4,8},{5,9},{6,10},{7,11},{8,4},{9,5},... | collective-permute-start | bytes 196616 | tf_op jit(solution)/shard_map/ppermute | solution.py:36
  14.1 13.2 %copy-start.5 = (s32[6,3]{0,1:T(4,128)S(1)}, s32[6,3]{0,1:T(4,128)}, u32[]{:S(2)}) copy-start(s32[6,3]{0,1:T(4,128)} %param.14) | copy-start | bytes 220
  14.1 19.5 %copy-start = (f32[1,64,64]{2,1,0:T(8,128)S(1)}, f32[1,64,64]{2,1,0:T(8,128)}, u32[]{:S(2)}) copy-start(f32[1,64,64]{2,1,0:T(8,128)} %dev_ref.1) | copy-start | bytes 49156
  14.1 19.5 %copy-start.3 = (s32[1,16]{1,0:T(1,128)S(1)}, s32[1,16]{1,0:T(1,128)}, u32[]{:S(2)}) copy-start(s32[1,16]{1,0:T(1,128)} %far_ref.1) | copy-start | bytes 196
  14.1 19.5 %copy-start.4 = (s32[1,2]{1,0:T(1,128)S(1)}, s32[1,2]{1,0:T(1,128)}, u32[]{:S(2)}) copy-start(s32[1,2]{1,0:T(1,128)} %group_far_ref.1) | copy-start | bytes 28
  16.5 1.5 %collective-permute-start.4 = (bf16[256,512]{1,0:T(8,128)(2,1)S(1)}, bf16[256,512]{1,0:T(8,128)(2,1)S(1)}, u32[]{:S(2)}, u32[]{:S(2)}) collective-permute-start(bf16[256,512]{1,0:T(8,128)(2,1)S(1)} %constant_dynamic-update-slice_fusion.2.held_ref), channel_id=1, source_target_pairs={{0,1},{1,0},{2,3},{3,2},{4,5},{5,4},{6,7},{7,6},{8,9},{9,8},{10,11... | collective-permute-start | bytes 786440 | tf_op jit(solution)/shard_map/ppermute | solution.py:36
  22.5 11.1 %all-to-all-start = ((f32[32,2,128]{2,1,0:T(2,128)}), f32[32,2,128]{2,1,0:T(2,128)S(1)}, u32[]{:S(2)}, u32[]{:S(2)}) async-start(f32[32,2,128]{2,1,0:T(2,128)} %get-tuple-element.21), calls=%async_computation | async-start | bytes 65536 | tf_op jit(solution)/shard_map/all_to_all | solution.py:392
  26.3 1.2 %collective-permute-start.5 = (f32[32,128]{1,0:T(8,128)S(1)}, f32[32,128]{1,0:T(8,128)S(1)}, u32[]{:S(2)}, u32[]{:S(2)}) collective-permute-start(f32[32,128]{1,0:T(8,128)S(1)} %get-tuple-element.20.halo_ref), channel_id=1, source_target_pairs={{0,1},{1,0},{2,3},{3,2},{4,5},{5,4},{6,7},{7,6},{8,9},{9,8},{10,11... | collective-permute-start | bytes 49160 | tf_op jit(solution)/shard_map/ppermute | solution.py:36
  26.7 0.9 %collective-permute-start.6 = (f32[32,128]{1,0:T(8,128)S(1)}, f32[32,128]{1,0:T(8,128)S(1)}, u32[]{:S(2)}, u32[]{:S(2)}) collective-permute-start(f32[32,128]{1,0:T(8,128)S(1)} %get-tuple-element.20.halo_ref), channel_id=1, source_target_pairs={{1,2},{2,1},{3,4},{4,3},{5,6},{6,5},{7,8},{8,7},{9,10},{10,9},{11,... | collective-permute-start | bytes 49160 | tf_op jit(solution)/shard_map/ppermute | solution.py:391

commit v3 on v2

v3 whole, which is shorter than its diff:
```python
import functools
import math

import jax
import jax.numpy as jnp
from jax import lax
from jax.experimental import pallas as pl
from jax.experimental.pallas import tpu as pltpu
from jax.sharding import PartitionSpec as P

SIDE = 8
LEAF = 512
CHEB = 4
RANK = CHEB * CHEB * CHEB
BW = 16
BLOCK_ROWS = 2 * BW
NEARL = 3
LANES = 128
LEAF_ROWS = LEAF // LANES
HIGHEST = lax.Precision.HIGHEST

vol_weight = 0.1
soft_square = 1.0


def xor_stages(count):
    bits = count.bit_length() - 1
    stages, bit = ([(2,)], 2) if bits > 1 else ([], 1)
    while bit < bits:
        wide = 2 if bit + 1 < bits else 1
        stages.append(tuple(m << bit for m in range(1, 1 << wide)))
        bit += wide
    return stages


def swap(value, axis, mask):
    return lax.ppermute(value, axis, [(i, i ^ mask) for i in range(lax.axis_size(axis))])


def farthest_first(mask):
    return -(mask & -mask), -mask


def gather_rows(rows, load, prepare):
    held, loaded = rows, load()
    for stage, masks in enumerate(xor_stages(lax.axis_size("dom"))):
        if stage == 1:
            held, loaded = lax.optimization_barrier((held, loaded))
            result = prepare(loaded)
        arrived = {m: swap(held, "dom", m) for m in sorted(masks, key=farthest_first)}
        held = jnp.concatenate([held] + [arrived[m] for m in masks], axis=0)
    held, result = lax.optimization_barrier((held, result))
    return held, swap(held, "dom", 1), loaded, result


def iota(shape, dim):
    return lax.broadcasted_iota(jnp.int32, shape, dim)


def lane_sums(x):
    return jnp.sum(x.T, axis=0, keepdims=True)


def spread_rows(row, count):
    size = row.shape[1]
    diagonal = iota((count, size), 0) == iota((count, size), 1)
    diagonal = jnp.where(diagonal, row, 0.0).astype(jnp.bfloat16)
    return jnp.dot(
        diagonal, jnp.ones((size, LANES), jnp.bfloat16), preferred_element_type=jnp.float32
    )


def split(x):
    high = x.astype(jnp.bfloat16)
    return high, (x - high.astype(jnp.float32)).astype(jnp.bfloat16)


def load_kernel(
    near_hbm,
    transfer_hbm,
    dev_hbm,
    basis_hbm,
    orbitals_hbm,
    orbit_ref,
    pick_ref,
    weights_ref,
    near_ref,
    transfer_ref,
    dev_ref,
    basis_ref,
    sems,
):
    moves = ((near_hbm, near_ref), (transfer_hbm, transfer_ref), (dev_hbm, dev_ref))
    moves += ((basis_hbm, basis_ref), (orbitals_hbm, orbit_ref))
    copies = [pltpu.make_async_copy(a, b, sems.at[i]) for i, (a, b) in enumerate(moves)]
    for copy in copies:
        copy.start()
    copies[0].wait()
    blocks = near_ref.shape[1]
    width = blocks * BW
    expand = (iota((blocks, width), 1) // BW == iota((blocks, width), 0)).astype(jnp.float32)
    near = jnp.broadcast_to(near_ref[...].astype(jnp.float32), (8, blocks))
    column = jnp.dot(near, expand, preferred_element_type=jnp.float32)[:1].astype(jnp.int32) * BW
    column = column + iota((1, width), 1) % BW
    for start in range(0, pick_ref.shape[0], LEAF):
        size = min(LEAF, pick_ref.shape[0] - start)
        hit = iota((size, width), 0) + start == column
        pick_ref[start : start + size, :] = jnp.where(hit, 1.0, 0.0).astype(jnp.bfloat16)
    for copy in copies[1:4]:
        copy.wait()
    leaves = transfer_ref.shape[0]
    transfer = transfer_ref[...].reshape(leaves * RANK, RANK)
    raised = jnp.dot(transfer, dev_ref[0], precision=HIGHEST, preferred_element_type=jnp.float32)
    high, low = split(jnp.concatenate([transfer, raised], axis=1))
    for leaf in range(leaves):
        at, points = slice(leaf * RANK, (leaf + 1) * RANK), slice(leaf * LEAF, (leaf + 1) * LEAF)
        basis_high, basis_low = split(basis_ref[:, points])
        weights_ref[:, points] = lax.dot_general(
            jnp.concatenate([high[at], high[at], low[at]], axis=0),
            jnp.concatenate([basis_high, basis_low, basis_high], axis=0),
            (((0,), (0,)), ((), ())),
            preferred_element_type=jnp.float32,
        )
    copies[4].wait()


def prepare_kernel(
    reorder, far_hbm, group_far_hbm, orbit_ref, pick_ref, mask_ref, *refs
):
    far_ref, group_far_ref, sems = refs[-3:]
    moves = ((far_hbm, far_ref), (group_far_hbm, group_far_ref))
    copies = [pltpu.make_async_copy(a, b, sems.at[i]) for i, (a, b) in enumerate(moves)]
    for copy in copies:
        copy.start()
    if reorder:
        for start in range(0, orbit_ref.shape[0], LEAF):
            part = lax.dot_general(
                orbit_ref[start : start + LEAF, :],
                pick_ref[...],
                (((1,), (1,)), ((), ())),
                preferred_element_type=jnp.float32,
            )
            refs[0][start : start + LEAF, :] = part.astype(jnp.bfloat16)
    for copy in copies:
        copy.wait()
    dom_count, group_count = far_ref.shape[1], group_far_ref.shape[1]
    mask_ref[:dom_count, :] = spread_rows(far_ref[...].astype(jnp.float32), dom_count)
    mask_ref[dom_count:, :] = spread_rows(group_far_ref[...].astype(jnp.float32), group_count)


def density_kernel(
    reorder, coords_ref, orbit_ref, held_ref, other_ref, weights_ref, pick_ref, near_ref, *refs
):
    halo_ref, expansion_ref, rows_ref = refs
    leaves = coords_ref.shape[1]
    me = lax.axis_index("dom")
    if reorder:
        pair_rows = BLOCK_ROWS
        mine = jnp.bitwise_and(me, 1) == 0
        for c in range(held_ref.shape[0] // pair_rows):
            first = jnp.bitwise_xor(lax.shift_right_logical(me, 1), c) * pair_rows
            at = pl.ds(pl.multiple_of(first, pair_rows), pair_rows)
            held, other = held_ref[at, :], other_ref[at, :]
            base = 2 * c * pair_rows
            rows_ref[base : base + pair_rows, :] = jnp.where(mine, held, other)
            rows_ref[base + pair_rows : base + 2 * pair_rows, :] = jnp.where(mine, other, held)
        matrix = rows_ref[...]
    else:
        for k in range(near_ref.shape[1]):
            block = near_ref[0, k]
            apart = jnp.bitwise_xor(lax.shift_right_logical(block, 1), me)
            first = lax.shift_right_logical(apart, 1) * BLOCK_ROWS + jnp.bitwise_and(block, 1) * BW
            at = pl.ds(pl.multiple_of(first, BW), BW)
            mine = jnp.bitwise_and(apart, 1) == 0
            rows_ref[k * BW : (k + 1) * BW, :] = jnp.where(mine, held_ref[at, :], other_ref[at, :])
        matrix = jnp.dot(rows_ref[...], pick_ref[...], preferred_element_type=jnp.float32)
        matrix = matrix.astype(jnp.bfloat16)
    total = jnp.zeros((2 * RANK, LANES), jnp.float32)
    tile = LEAF // 2
    for start in range(0, leaves * LEAF, tile):
        orbit = orbit_ref[start : start + tile, :]
        product = jnp.dot(orbit, matrix, preferred_element_type=jnp.float32)
        product = product * orbit.astype(jnp.float32)
        folded = product[:, :LANES]
        for at in range(LANES, product.shape[1], LANES):
            folded = folded + product[:, at : at + LANES]
        for j in range(tile // LANES):
            row = start // LANES + j
            part = lane_sums(folded[j * LANES : (j + 1) * LANES])
            halo_ref[row : row + 1, :] = part
            total = total + weights_ref[:, row * LANES : (row + 1) * LANES] * part
    coords = coords_ref[...].astype(jnp.float32)
    rows = leaves * LEAF_ROWS
    halo_ref[rows:, :] = jnp.zeros((halo_ref.shape[0] - rows, LANES), jnp.float32)
    halo_ref[rows : rows + 3, :leaves] = coords
    low = SIDE * jnp.min(coords, axis=1, keepdims=True)
    high = SIDE * jnp.max(coords, axis=1, keepdims=True) + (SIDE - 1)
    lane = iota((1, LANES), 1)
    bounds = jnp.zeros((1, LANES), jnp.float32)
    for k in range(3):
        bounds = jnp.where(lane == k, low[k : k + 1], bounds)
        bounds = jnp.where(lane == 3 + k, high[k : k + 1], bounds)
    both = jnp.concatenate([lane_sums(total), bounds], axis=0)
    expansion_ref[...] = jnp.broadcast_to(both[None], expansion_ref.shape)


def pattern(index):
    steps = (index // (CHEB * CHEB) % CHEB, index // CHEB % CHEB, index % CHEB)
    points = [math.cos((2 * a + 1) * math.pi / (2 * CHEB)) for a in range(CHEB)]
    out = []
    for step in steps:
        value = jnp.full(index.shape, points[CHEB - 1], jnp.float32)
        for a in range(CHEB - 1):
            value = jnp.where(step == a, points[a], value)
        out.append(value)
    return out


def nodes(bounds, unit):
    out = []
    for k in range(3):
        low, high = bounds[:, k : k + 1], bounds[:, 3 + k : 4 + k]
        out.append(0.5 * (low + high) + 0.5 * (high - low) * unit[k])
    return out


def node_coupling(target, source):
    square = soft_square
    for t, s in zip(target, source, strict=True):
        apart = t - s
        square = square + apart * apart
    return lax.rsqrt(square)


def places(halo, rows):
    parts = [spread_rows(halo[rows + k : rows + k + 1], 8) for k in range(3)]
    return SIDE * jnp.concatenate(parts, axis=0)


def add_pair(sum_ref, own_place, place, rho, fresh):
    lane, row = iota((8, LANES), 1), iota((8, LANES), 0)
    low = lane < LANES // 2
    half = jnp.where(low, 0.0, 1.0)
    at_y = (lane // SIDE % SIDE).astype(jnp.float32)
    along_z = (row - lane % SIDE).astype(jnp.float32)
    shift = [jnp.broadcast_to(a - b, (8, LANES)) for a, b in zip(own_place, place, strict=True)]
    rho = [jnp.broadcast_to(r, (8, LANES)) for r in rho]
    swapped = [pltpu.roll(r, LANES // 2, 1) for r in rho]
    along = shift[2] + along_z
    square_z = along * along + soft_square
    square_x = []
    for m in range(-6, SIDE + 2, 2):
        apart = shift[0] + (m - half)
        square_x.append(apart * apart)
    for y in range(SIDE):
        apart = shift[1] + (y - at_y)
        square = apart * apart + square_z
        even = [lax.rsqrt(x + square) for x in square_x]
        odd = [jnp.where(low, a, b) for a, b in zip(even[:-1], even[1:], strict=True)]
        for x in range(SIDE):
            first = x // 2 + 3
            kernel, density = (odd, swapped) if x % 2 else (even, rho)
            value = kernel[first] * density[0]
            for j in range(1, LEAF_ROWS):
                value = value + kernel[first - j] * density[j]
            at = slice((x * SIDE + y) * SIDE, (x * SIDE + y + 1) * SIDE)
            if fresh:
                sum_ref[at, :] = value
            else:
                sum_ref[at, :] += value


def near_kernel(leaves_ref, halo_ref, even_ref, odd_ref, out_ref, values_ref, density_ref, place_ref, sum_ref):
    leaves = leaves_ref.shape[0]
    rows = leaves * LEAF_ROWS
    is_odd = jnp.bitwise_and(lax.axis_index("dom"), 1) == 1
    even, odd = even_ref[...], odd_ref[...]
    window = (jnp.where(is_odd, even, odd), halo_ref[...], jnp.where(is_odd, odd, even))
    for side, held in enumerate(window):
        density_ref[side * rows : (side + 1) * rows, :] = held[:rows]
        place_ref[24 * side : 24 * (side + 1), :] = places(held, rows)
    values_ref[...] = halo_ref[:rows, :]

    def one_leaf(leaf, carry):
        own_place = [place_ref[pl.ds(24 + leaf + 8 * k, 1), :] for k in range(3)]
        for slot in range(NEARL):
            position = leaves_ref[leaf, slot]
            side = (position >= leaves).astype(jnp.int32)
            side = side + (position >= 2 * leaves).astype(jnp.int32)
            first = 24 * side + position - leaves * side
            place = [place_ref[pl.ds(first + 8 * k, 1), :] for k in range(3)]
            rho = [density_ref[pl.ds(position * LEAF_ROWS + j, 1), :] for j in range(LEAF_ROWS)]
            add_pair(sum_ref, own_place, place, rho, slot == 0)
        for j in range(LEAF_ROWS):
            part = lane_sums(sum_ref[j * LANES : (j + 1) * LANES, :])
            out_ref[pl.ds(leaf * LEAF_ROWS + j, 1), :] = vol_weight * part
        return carry

    lax.fori_loop(0, leaves, one_leaf, 0)


def far_field(expansion_ref, mask_ref, dev_ref):
    dom_count = lax.axis_size("dom")
    group_count = mask_ref.shape[0] - dom_count
    group, me = lax.axis_index("group"), lax.axis_index("dom")
    sent = expansion_ref[...]
    moments, bounds = sent[:, 0, :], sent[:, 1, :]
    lane = iota((1, LANES), 1)
    unit_row = pattern(lane % RANK)
    unit_column = pattern(iota((RANK, LANES), 0))
    group_bounds = []
    for h in range(group_count):
        part = bounds[h * dom_count : (h + 1) * dom_count]
        low = jnp.min(part, axis=0, keepdims=True)
        high = jnp.max(part, axis=0, keepdims=True)
        group_bounds.append(jnp.where(lane < 3, low, high))
    own_group_bounds = group_bounds[0]
    for h in range(1, group_count):
        own_group_bounds = jnp.where(group == h, group_bounds[h], own_group_bounds)
    target = nodes(own_group_bounds, unit_column)
    total = jnp.zeros((RANK, LANES), jnp.float32)
    for h in range(group_count):
        raised = jnp.sum(moments[h * dom_count : (h + 1) * dom_count], axis=0, keepdims=True)
        raised = jnp.where(lane >= RANK, raised, 0.0) * mask_ref[dom_count + h : dom_count + h + 1, :]
        total = total + node_coupling(target, nodes(group_bounds[h], unit_row)) * raised
    group_local = vol_weight * lane_sums(total)
    local = jnp.sum(dev_ref[0] * group_local, axis=1, keepdims=True)
    base = group * dom_count
    own = expansion_ref[pl.ds(base, dom_count)]
    own_bounds = expansion_ref[pl.ds(base + me, 1)][:, 1, :]
    target = nodes(own_bounds, unit_column)
    source = nodes(own[:, 1, :], unit_row)
    own_moments = jnp.where(lane < RANK, own[:, 0, :], 0.0) * mask_ref[:dom_count, :]
    total = jnp.zeros((RANK, LANES), jnp.float32)
    for s in range(dom_count):
        coupling = node_coupling(target, [x[s : s + 1] for x in source])
        total = total + coupling * own_moments[s : s + 1]
    local = local + vol_weight * jnp.sum(total, axis=1, keepdims=True)
    return jnp.broadcast_to(local, (RANK, LANES))


def potential_kernel(expansion_ref, mask_ref, weights_ref, dev_ref, near_ref, out_ref):
    local = far_field(expansion_ref, mask_ref, dev_ref)
    for row in range(out_ref.shape[0]):
        at = slice(row * LANES, (row + 1) * LANES)
        far = jnp.sum(weights_ref[:RANK, at] * local, axis=0, keepdims=True)
        out_ref[row : row + 1, :] = near_ref[row : row + 1, :] + far


def in_hbm(x):
    return pltpu.with_memory_space_constraint(x, pltpu.HBM)


VMEM = pl.BlockSpec(memory_space=pltpu.VMEM)
SMEM = pl.BlockSpec(memory_space=pltpu.SMEM)
HBM = pl.BlockSpec(memory_space=pltpu.HBM)
ANY = pl.BlockSpec(memory_space=pl.ANY)


def local(
    orbitals,
    density_rows,
    near_blocks,
    leaf_coords,
    near_leaves,
    leaf_basis,
    leaf_transfer,
    dev_transfer,
    dev_far,
    group_far,
):
    points, width = orbitals.shape
    leaves = leaf_coords.shape[1]
    rows = leaves * LEAF_ROWS
    natural = density_rows.shape[1]
    devices = lax.axis_size("group") * lax.axis_size("dom")
    dom_count = lax.axis_size("dom")
    f32 = jnp.float32
    reorder = natural == width
    params = pltpu.CompilerParams(vmem_limit_bytes=(24 << 20) + 4 * natural * natural)

    def cost(flops, transcendentals=0):
        return pl.CostEstimate(
            flops=flops, bytes_accessed=4 << 20, transcendentals=transcendentals
        )

    def load():
        operands = (near_blocks, leaf_transfer, dev_transfer, leaf_basis)
        return pl.pallas_call(
            load_kernel,
            out_shape=(
                jax.ShapeDtypeStruct((points, width), jnp.bfloat16),
                jax.ShapeDtypeStruct((natural, width), jnp.bfloat16),
                jax.ShapeDtypeStruct((2 * RANK, points), f32),
            ),
            in_specs=[HBM] * 5,
            out_specs=(VMEM, VMEM, VMEM),
            scratch_shapes=[pltpu.VMEM(x.shape, x.dtype) for x in operands]
            + [pltpu.SemaphoreType.DMA((5,))],
            compiler_params=params,
            cost_estimate=cost(1 << 20),
            name="load",
        )(*[in_hbm(x) for x in operands], in_hbm(orbitals))

    def prepare(loaded):
        orbit, pick, _ = loaded
        operands = (dev_far, group_far)
        shapes = [jax.ShapeDtypeStruct((dev_far.shape[1] + group_far.shape[1], LANES), f32)]
        if reorder:
            shapes.append(jax.ShapeDtypeStruct((points, natural), jnp.bfloat16))
        out = pl.pallas_call(
            functools.partial(prepare_kernel, reorder),
            out_shape=shapes,
            in_specs=[HBM] * 2 + [VMEM] * 2,
            out_specs=[VMEM] * len(shapes),
            scratch_shapes=[pltpu.VMEM(x.shape, x.dtype) for x in operands]
            + [pltpu.SemaphoreType.DMA((2,))],
            compiler_params=params,
            cost_estimate=cost(2 * points * width * natural),
            name="prepare",
        )(*[in_hbm(x) for x in operands], orbit, pick)
        return out if reorder else [*out, orbit]

    held, other, (_, pick, weights), (mask, orbit) = gather_rows(density_rows, load, prepare)

    halo, expansion = pl.pallas_call(
        functools.partial(density_kernel, reorder),
        out_shape=(
            jax.ShapeDtypeStruct((rows + 8, LANES), f32),
            jax.ShapeDtypeStruct((devices, 2, LANES), f32),
        ),
        in_specs=[VMEM] * 5 + ([ANY, ANY] if reorder else [VMEM, SMEM]),
        out_specs=(VMEM, VMEM),
        scratch_shapes=[pltpu.VMEM((width, natural), jnp.bfloat16)],
        compiler_params=params,
        cost_estimate=cost(2 * points * width * width),
        name="density",
    )(leaf_coords, orbit, held, other, weights, pick, near_blocks)

    even = swap(halo, "dom", 1)
    pairs = [(i, i + 1 if i % 2 else i - 1) for i in range(1, dom_count - 1)]
    odd = lax.ppermute(halo, "dom", pairs)
    everyone = lax.all_to_all(expansion, ("group", "dom"), 0, 0)

    table = jax.ShapeDtypeStruct((rows, LANES), f32)
    near, density = pl.pallas_call(
        near_kernel,
        out_shape=(table, table),
        in_specs=[SMEM] + [VMEM] * 3,
        out_specs=(VMEM, VMEM),
        scratch_shapes=[
            pltpu.VMEM((3 * rows, LANES), f32),
            pltpu.VMEM((72, LANES), f32),
            pltpu.VMEM((LEAF, LANES), f32),
        ],
        compiler_params=params,
        cost_estimate=cost(20 << 20, 4 << 20),
        name="near",
    )(near_leaves, halo, even, odd)
    hartree = pl.pallas_call(
        potential_kernel,
        out_shape=table,
        in_specs=[VMEM] * 5,
        out_specs=VMEM,
        compiler_params=params,
        cost_estimate=cost(4 << 20, 1 << 20),
        name="potential",
    )(everyone, mask, weights, dev_transfer, near)
    return (density.reshape(-1), hartree.reshape(-1))


def solution(mesh):
    in_specs = (
        P(("group", "dom"), None),
        P(("group", "dom"), None),
        P(("group", "dom"), None),
        P(None, ("group", "dom")),
        P(("group", "dom"), None),
        P(None, ("group", "dom")),
        P(("group", "dom"), None, None),
        P(("group", "dom"), None, None),
        P(("group", "dom"), None),
        P("group", None),
    )
    out_specs = (P(("group", "dom")), P(("group", "dom")))
    return jax.shard_map(local, mesh=mesh, in_specs=in_specs, out_specs=out_specs, check_vma=False)
```

time: 38.7 us -> 33.9 us (0.88); the launches traced: 38.4 us -> 33.2 us
  waiting for transfers between devices: 11.4 us -> 4.41 us
  starting transfers between devices: 12.5 us -> 15.7 us
  local copies, waits for them, and re-layouts: 0.95 us -> 0.12 us
  Pallas kernels: 12.9 us -> 12.3 us
    all_to_all x1, waiting for transfers between devices: 6 us -> 0.01 us  [local(): everyone = lax.all_to_all(expansion, ('group', 'dom'), 0, 0)]
    ppermute x6, starting transfers between devices: 8.02 us -> 10.8 us  [swap(): lax.ppermute(value, axis, [(i, i ^ mask) for i in range(lax.axis_size(axi...]
    ppermute x6, waiting for transfers between devices: 5.39 us -> 4.4 us  [swap(): lax.ppermute(value, axis, [(i, i ^ mask) for i in range(lax.axis_size(axi...]
    unnamed x16 -> x11, local copies, waits for them, and re-layouts: 0.94 us -> 0.12 us
    pallas_call x3 -> x5, Pallas kernels: 12.9 us -> 12.3 us  [the longest x1 3.38 us: local(): pl.pallas_call(near_kernel, out_shape=(table, table), in_specs=[SMEM] + [...]
    all_to_all x1, starting transfers between devices: 3.79 us -> 4.24 us  [local(): everyone = lax.all_to_all(expansion, ('group', 'dom'), 0, 0)]
  transfers between devices with their start and end apart: 8 -> 8, of which waited for: 6 -> 4; matrix products, arithmetic and copies ran while one was open for 2% -> 0% of each run, Pallas kernels for 9% -> 25%
where the time goes in v3:
time: 33.9 us; the launch traced here: 33.2 us
  starting transfers between devices  15.7 us (46%)
  Pallas kernels  12.3 us (36%)
  waiting for transfers between devices  4.41 us (13%)
  between operations  0.75 us (2%)
    ppermute x6, starting transfers between devices, swap(): lax.ppermute(value, axis, [(i, i ^ mask) for i in range(lax.axis_size(axi...  10.8 us
    ppermute x6, waiting for transfers between devices, swap(): lax.ppermute(value, axis, [(i, i ^ mask) for i in range(lax.axis_size(axi...  4.4 us
    all_to_all x1, starting transfers between devices, local(): everyone = lax.all_to_all(expansion, ('group', 'dom'), 0, 0)  4.24 us
    pallas_call x1, Pallas kernels, local(): pl.pallas_call(near_kernel, out_shape=(table, table), in_specs=[SMEM] + [...  3.38 us
    pallas_call x1, Pallas kernels, local(): pl.pallas_call(functools.partial(density_kernel, reorder), out_shape=(jax...  2.68 us
    pallas_call x1, Pallas kernels, prepare(): pl.pallas_call(functools.partial(prepare_kernel, reorder), out_shape=shap...  2.5 us
    pallas_call x1, Pallas kernels, load(): pl.pallas_call(load_kernel, out_shape=(jax.ShapeDtypeStruct((points, widt...  2.41 us
    pallas_call x1, Pallas kernels, local(): pl.pallas_call(potential_kernel, out_shape=table, in_specs=[VMEM] * 5, ou...  1.29 us
  transfers between devices with their start and end apart: 8, of which 4 were waited for; matrix products, arithmetic and copies ran while one was open for 0% of the time, Pallas kernels for 25%

profile of v3, /device:TPU:0, one launch (start us, length us, event | category | flops | bytes accessed | tf_op | source)
XLA Modules:
  0.0 33.2 jit_solution(12904225920984201992)
XLA Ops:
  0.6 0.0 copy-start.3
  0.6 3.0 %collective-permute-start = (bf16[32,512]{1,0:T(8,128)(2,1)}, bf16[32,512]{1,0:T(8,128)(2,1)S(1)}, u32[]{:S(2)}, u32[]{:S(2)}) collective-permute-start(bf16[32,512]{1,0:T(8,128)(2,1)} %param.11), channel_id=1, source_target_pairs={{0,2},{1,3},{2,0},{3,1},{4,6},{5,7},{6,4},{7,5},{8,10},{9,11},{10,... | collective-permute-start | bytes 98312 | tf_op jit(solution)/shard_map/ppermute | solution.py:37
  3.7 2.4 %load.1 = (bf16[3072,512]{1,0:T(8,128)(2,1)S(1)}, bf16[512,512]{1,0:T(8,128)(2,1)S(1)}, f32[128,3072]{1,0:T(8,128)S(1)}) custom-call(s32[1,32]{1,0:T(1,128)} %near_ref.1, f32[6,64,64]{2,1,0:T(8,128)} %transfer_hbm.1, f32[1,64,64]{2,1,0:T(8,128)} %dev_ref.1, f32[64,3072]{1,0:T(8,128)} %basis_hbm.1, bf16[3072,512]{1,0:T(8,128)(2,1)} %orbitals_hbm.1), custom_call_target="tpu_custom_call" | custom-call | flops 1048576 | bytes 4194304 | tf_op jit(solution)/shard_map/load/pallas_call | solution.py:389
  6.1 0.0 collective-permute-done
  6.1 0.0 copy-done.3
  6.1 0.0 copy-start.1
  6.1 0.0 copy-start.2
  6.2 3.8 %collective-permute-start.3 = (bf16[64,512]{1,0:T(8,128)(2,1)S(1)}, bf16[64,512]{1,0:T(8,128)(2,1)S(1)}, u32[]{:S(2)}, u32[]{:S(2)}) collective-permute-start(bf16[64,512]{1,0:T(8,128)(2,1)S(1)} %pad_maximum_fusion.1), channel_id=1, source_target_pairs={{0,12},{1,13},{2,14},{3,15},{4,8},{5,9},{6,10},{7,11},{8,4},{9,5},... | collective-permute-start | bytes 196616 | tf_op jit(solution)/shard_map/ppermute | solution.py:37
  10.0 0.0 collective-permute-start.2
  10.0 0.6 %collective-permute-start.1 = (bf16[64,512]{1,0:T(8,128)(2,1)S(1)}, bf16[64,512]{1,0:T(8,128)(2,1)S(1)}, u32[]{:S(2)}, u32[]{:S(2)}) collective-permute-start(bf16[64,512]{1,0:T(8,128)(2,1)S(1)} %pad_maximum_fusion.1), channel_id=1, source_target_pairs={{0,4},{1,5},{2,6},{3,7},{4,0},{5,1},{6,2},{7,3},{8,12},{9,13},{10,... | collective-permute-start | bytes 196616 | tf_op jit(solution)/shard_map/ppermute | solution.py:37
  10.6 2.5 %prepare.1 = (f32[18,128]{1,0:T(8,128)S(1)}, bf16[3072,512]{1,0:T(8,128)(2,1)S(1)}) custom-call(s32[1,16]{1,0:T(1,128)} %far_hbm.1, s32[1,2]{1,0:T(1,128)} %group_far_hbm.1, bf16[3072,512]{1,0:T(8,128)(2,1)S(1)} %get-tuple-element.22.orbit_ref, bf16[512,512]{1,0:T(8,128)(2,1)S(1)} %get-tuple-element.23.pick_ref), custom_call_target="tpu_custom_call" | custom-call | flops 1610612736 | bytes 4194304 | tf_op jit(solution)/shard_map/prepare/pallas_call | solution.py:411
  13.1 0.0 collective-permute-done.3
  13.1 2.1 %collective-permute-done.2 = bf16[64,512]{1,0:T(8,128)(2,1)S(1)} collective-permute-done((bf16[64,512]{1,0:T(8,128)(2,1)S(1)}, bf16[64,512]{1,0:T(8,128)(2,1)S(1)}, u32[]{:S(2)}, u32[]{:S(2)}) %collective-permute-start.2) | collective-permute-done | bytes 65568 | tf_op jit(solution)/shard_map/ppermute | solution.py:37
  15.2 0.1 collective-permute-done.1
  15.3 0.0 copy-start.4
  15.3 0.1 collective-permute-start.4
  15.4 1.5 %collective-permute-done.4.other_ref = bf16[256,512]{1,0:T(8,128)(2,1)S(1)} collective-permute-done((bf16[256,512]{1,0:T(8,128)(2,1)S(1)}, bf16[256,512]{1,0:T(8,128)(2,1)S(1)}, u32[]{:S(2)}, u32[]{:S(2)}) %collective-permute-start.4) | collective-permute-done | bytes 262176 | tf_op jit(solution)/shard_map/ppermute | solution.py:37
  16.9 0.0 copy-done.1
  16.9 0.0 copy-done.2
  16.9 2.7 %density.1 = (f32[32,128]{1,0:T(8,128)S(1)}, f32[32,2,128]{2,1,0:T(2,128)}) custom-call(s32[3,6]{1,0:T(4,128)S(1)} %copy-done.2, bf16[3072,512]{1,0:T(8,128)(2,1)S(1)} %get-tuple-element.26.orbit_ref, bf16[256,512]{1,0:T(8,128)(2,1)S(1)} %pad_maximum_fusion.held_ref, bf16[256,512]{1,0:T(8,128)(2,1)S(1)} %collective-permute-done.4.other_ref, ...), custom_call_target="tpu_custom_call" | custom-call | flops 1610612736 | bytes 4194304 | tf_op jit(solution)/shard_map/density/pallas_call | solution.py:426
  19.6 4.2 %all-to-all-start = ((f32[32,2,128]{2,1,0:T(2,128)}), f32[32,2,128]{2,1,0:T(2,128)S(1)}, u32[]{:S(2)}, u32[]{:S(2)}) async-start(f32[32,2,128]{2,1,0:T(2,128)} %get-tuple-element.31), calls=%async_computation | async-start | bytes 65536 | tf_op jit(solution)/shard_map/all_to_all | solution.py:443
  23.9 0.7 %collective-permute-start.6 = (f32[32,128]{1,0:T(8,128)S(1)}, f32[32,128]{1,0:T(8,128)S(1)}, u32[]{:S(2)}, u32[]{:S(2)}) collective-permute-start(f32[32,128]{1,0:T(8,128)S(1)} %get-tuple-element.29.halo_ref), channel_id=1, source_target_pairs={{1,2},{2,1},{3,4},{4,3},{5,6},{6,5},{7,8},{8,7},{9,10},{10,9},{11,... | collective-permute-start | bytes 49160 | tf_op jit(solution)/shard_map/ppermute | solution.py:442
  24.5 3.2 %collective-permute-start.5 = (f32[32,128]{1,0:T(8,128)S(1)}, f32[32,128]{1,0:T(8,128)S(1)}, u32[]{:S(2)}, u32[]{:S(2)}) collective-permute-start(f32[32,128]{1,0:T(8,128)S(1)} %get-tuple-element.29.halo_ref), channel_id=1, source_target_pairs={{0,1},{1,0},{2,3},{3,2},{4,5},{5,4},{6,7},{7,6},{8,9},{9,8},{10,11... | collective-permute-start | bytes 49160 | tf_op jit(solution)/shard_map/ppermute | solution.py:37
  27.7 0.0 copy-done.4
  27.7 0.1 copy.12.leaves_ref
  27.8 0.0 copy-start
  27.8 0.0 collective-permute-done.6.odd_ref
  27.8 0.7 %collective-permute-done.5.even_ref = f32[32,128]{1,0:T(8,128)S(1)} collective-permute-done((f32[32,128]{1,0:T(8,128)S(1)}, f32[32,128]{1,0:T(8,128)S(1)}, u32[]{:S(2)}, u32[]{:S(2)}) %collective-permute-start.5) | collective-permute-done | bytes 16416 | tf_op jit(solution)/shard_map/ppermute | solution.py:37
  28.6 3.4 %near.1 = (f32[24,128]{1,0:T(8,128)S(1)}, f32[24,128]{1,0:T(8,128)}) custom-call(s32[6,3]{1,0:T(8,128)S(1)} %copy.12.leaves_ref, f32[32,128]{1,0:T(8,128)S(1)} %get-tuple-element.29.halo_ref, f32[32,128]{1,0:T(8,128)S(1)} %collective-permute-done.5.even_ref, f32[32,128]{1,0:T(8,128)S(1)} %collective-permute-done.6.odd_ref), custom_call_target="tpu_custom_call" | custom-call | flops 20971520 | bytes 4194304 | tf_op jit(solution)/shard_map/near/pallas_call | solution.py:446
  31.9 0.0 all-to-all-done.expansion_ref
  31.9 0.0 copy-done
  31.9 1.3 %potential.1 = f32[24,128]{1,0:T(8,128)} custom-call(f32[32,2,128]{2,1,0:T(2,128)S(1)} %all-to-all-done.expansion_ref, f32[18,128]{1,0:T(8,128)S(1)} %get-tuple-element.32.mask_ref, f32[128,3072]{1,0:T(8,128)S(1)} %get-tuple-element.28.weights_ref, f32[1,64,64]{2,1,0:T(8,128)S(1)} %copy-done, f32[24,128]{1,0:T(8,128)S(1)} %get-tuple-element.33.near_ref), custom_call_target="tpu_custom_call" | custom-call | flops 4194304 | bytes 4194304 | tf_op jit(solution)/shard_map/potential/pallas_call | solution.py:460
  (2 shorter events, 0.0 us)
Async XLA Ops:
  0.6 5.5 %copy-start.3 = (bf16[32,512]{1,0:T(8,128)(2,1)S(1)}, bf16[32,512]{1,0:T(8,128)(2,1)}, u32[]{:S(2)}) copy-start(bf16[32,512]{1,0:T(8,128)(2,1)} %param.11) | copy-start | bytes 98308
  0.6 5.5 %collective-permute-start = (bf16[32,512]{1,0:T(8,128)(2,1)}, bf16[32,512]{1,0:T(8,128)(2,1)S(1)}, u32[]{:S(2)}, u32[]{:S(2)}) collective-permute-start(bf16[32,512]{1,0:T(8,128)(2,1)} %param.11), channel_id=1, source_target_pairs={{0,2},{1,3},{2,0},{3,1},{4,6},{5,7},{6,4},{7,5},{8,10},{9,11},{10,... | collective-permute-start | bytes 98312 | tf_op jit(solution)/shard_map/ppermute | solution.py:37
  6.1 10.8 %copy-start.1 = (s32[1,32]{1,0:T(1,128)S(1)}, s32[1,32]{1,0:T(1,128)}, u32[]{:S(2)}) copy-start(s32[1,32]{1,0:T(1,128)} %near_ref.1) | copy-start | bytes 388
  6.1 10.8 %copy-start.2 = (s32[3,6]{1,0:T(4,128)S(1)}, s32[3,6]{1,0:T(4,128)}, u32[]{:S(2)}) copy-start(s32[3,6]{1,0:T(4,128)} %coords_ref.1) | copy-start | bytes 220
  6.2 7.0 %collective-permute-start.3 = (bf16[64,512]{1,0:T(8,128)(2,1)S(1)}, bf16[64,512]{1,0:T(8,128)(2,1)S(1)}, u32[]{:S(2)}, u32[]{:S(2)}) collective-permute-start(bf16[64,512]{1,0:T(8,128)(2,1)S(1)} %pad_maximum_fusion.1), channel_id=1, source_target_pairs={{0,12},{1,13},{2,14},{3,15},{4,8},{5,9},{6,10},{7,11},{8,4},{9,5},... | collective-permute-start | bytes 196616 | tf_op jit(solution)/shard_map/ppermute | solution.py:37
  10.0 5.2 %collective-permute-start.2 = (bf16[64,512]{1,0:T(8,128)(2,1)S(1)}, bf16[64,512]{1,0:T(8,128)(2,1)S(1)}, u32[]{:S(2)}, u32[]{:S(2)}) collective-permute-start(bf16[64,512]{1,0:T(8,128)(2,1)S(1)} %pad_maximum_fusion.1), channel_id=1, source_target_pairs={{0,8},{1,9},{2,10},{3,11},{4,12},{5,13},{6,14},{7,15},{8,0},{9,1},... | collective-permute-start | bytes 196616 | tf_op jit(solution)/shard_map/ppermute | solution.py:37
  10.0 5.3 %collective-permute-start.1 = (bf16[64,512]{1,0:T(8,128)(2,1)S(1)}, bf16[64,512]{1,0:T(8,128)(2,1)S(1)}, u32[]{:S(2)}, u32[]{:S(2)}) collective-permute-start(bf16[64,512]{1,0:T(8,128)(2,1)S(1)} %pad_maximum_fusion.1), channel_id=1, source_target_pairs={{0,4},{1,5},{2,6},{3,7},{4,0},{5,1},{6,2},{7,3},{8,12},{9,13},{10,... | collective-permute-start | bytes 196616 | tf_op jit(solution)/shard_map/ppermute | solution.py:37
  15.3 12.4 %copy-start.4 = (s32[6,3]{0,1:T(4,128)S(1)}, s32[6,3]{0,1:T(4,128)}, u32[]{:S(2)}) copy-start(s32[6,3]{0,1:T(4,128)} %param.14) | copy-start | bytes 220
  15.3 1.6 %collective-permute-start.4 = (bf16[256,512]{1,0:T(8,128)(2,1)S(1)}, bf16[256,512]{1,0:T(8,128)(2,1)S(1)}, u32[]{:S(2)}, u32[]{:S(2)}) collective-permute-start(bf16[256,512]{1,0:T(8,128)(2,1)S(1)} %pad_maximum_fusion.held_ref), channel_id=1, source_target_pairs={{0,1},{1,0},{2,3},{3,2},{4,5},{5,4},{6,7},{7,6},{8,9},{9,8},{10,11... | collective-permute-start | bytes 786440 | tf_op jit(solution)/shard_map/ppermute | solution.py:37
  19.6 12.3 %all-to-all-start = ((f32[32,2,128]{2,1,0:T(2,128)}), f32[32,2,128]{2,1,0:T(2,128)S(1)}, u32[]{:S(2)}, u32[]{:S(2)}) async-start(f32[32,2,128]{2,1,0:T(2,128)} %get-tuple-element.31), calls=%async_computation | async-start | bytes 65536 | tf_op jit(solution)/shard_map/all_to_all | solution.py:443
  23.9 4.0 %collective-permute-start.6 = (f32[32,128]{1,0:T(8,128)S(1)}, f32[32,128]{1,0:T(8,128)S(1)}, u32[]{:S(2)}, u32[]{:S(2)}) collective-permute-start(f32[32,128]{1,0:T(8,128)S(1)} %get-tuple-element.29.halo_ref), channel_id=1, source_target_pairs={{1,2},{2,1},{3,4},{4,3},{5,6},{6,5},{7,8},{8,7},{9,10},{10,9},{11,... | collective-permute-start | bytes 49160 | tf_op jit(solution)/shard_map/ppermute | solution.py:442
  24.5 4.0 %collective-permute-start.5 = (f32[32,128]{1,0:T(8,128)S(1)}, f32[32,128]{1,0:T(8,128)S(1)}, u32[]{:S(2)}, u32[]{:S(2)}) collective-permute-start(f32[32,128]{1,0:T(8,128)S(1)} %get-tuple-element.29.halo_ref), channel_id=1, source_target_pairs={{0,1},{1,0},{2,3},{3,2},{4,5},{5,4},{6,7},{7,6},{8,9},{9,8},{10,11... | collective-permute-start | bytes 49160 | tf_op jit(solution)/shard_map/ppermute | solution.py:37
  27.8 4.1 %copy-start = (f32[1,64,64]{2,1,0:T(8,128)S(1)}, f32[1,64,64]{2,1,0:T(8,128)}, u32[]{:S(2)}) copy-start(f32[1,64,64]{2,1,0:T(8,128)} %dev_ref.1) | copy-start | bytes 49156

commit v4 on v3

--- a/solution.py
+++ b/solution.py
@@ -17,6 +17,7 @@
 NEARL = 3
 LANES = 128
 LEAF_ROWS = LEAF // LANES
+TILE = 256
 HIGHEST = lax.Precision.HIGHEST
 
 vol_weight = 0.1
@@ -75,7 +76,13 @@
     return high, (x - high.astype(jnp.float32)).astype(jnp.bfloat16)
 
 
+def by_core(device, devices):
+    chip = lax.shift_right_logical(device, 1)
+    return jnp.bitwise_and(device, 1) * (devices // 2) + chip
+
+
 def load_kernel(
+    reorder,
     near_hbm,
     transfer_hbm,
     dev_hbm,
@@ -99,7 +106,11 @@
     blocks = near_ref.shape[1]
     width = blocks * BW
     expand = (iota((blocks, width), 1) // BW == iota((blocks, width), 0)).astype(jnp.float32)
-    near = jnp.broadcast_to(near_ref[...].astype(jnp.float32), (8, blocks))
+    near = near_ref[...]
+    if reorder:
+        device = by_core(lax.shift_right_logical(near, 1), blocks // 2)
+        near = 2 * device + jnp.bitwise_and(near, 1)
+    near = jnp.broadcast_to(near.astype(jnp.float32), (8, blocks))
     column = jnp.dot(near, expand, preferred_element_type=jnp.float32)[:1].astype(jnp.int32) * BW
     column = column + iota((1, width), 1) % BW
     for start in range(0, pick_ref.shape[0], LEAF):
@@ -124,15 +135,14 @@
     copies[4].wait()
 
 
-def prepare_kernel(
-    reorder, far_hbm, group_far_hbm, orbit_ref, pick_ref, mask_ref, *refs
-):
+def prepare_kernel(reorder, far_hbm, group_far_hbm, orbit_ref, pick_ref, mask_ref, *refs):
     far_ref, group_far_ref, sems = refs[-3:]
     moves = ((far_hbm, far_ref), (group_far_hbm, group_far_ref))
     copies = [pltpu.make_async_copy(a, b, sems.at[i]) for i, (a, b) in enumerate(moves)]
     for copy in copies:
         copy.start()
     if reorder:
+        sorted_ref, order_ref = refs[:2]
         for start in range(0, orbit_ref.shape[0], LEAF):
             part = lax.dot_general(
                 orbit_ref[start : start + LEAF, :],
@@ -140,7 +150,12 @@
                 (((1,), (1,)), ((), ())),
                 preferred_element_type=jnp.float32,
             )
-            refs[0][start : start + LEAF, :] = part.astype(jnp.bfloat16)
+            sorted_ref[start : start + LEAF, :] = part.astype(jnp.bfloat16)
+        size = order_ref.shape[0]
+        column = iota((size, 1), 0)
+        place = by_core(column // BLOCK_ROWS, size // BLOCK_ROWS) * BLOCK_ROWS + column % BLOCK_ROWS
+        hit = iota((size, size), 1) == place
+        order_ref[...] = jnp.where(hit, 1.0, 0.0).astype(jnp.bfloat16)
     for copy in copies:
         copy.wait()
     dom_count, group_count = far_ref.shape[1], group_far_ref.shape[1]
@@ -148,24 +163,46 @@
     mask_ref[dom_count:, :] = spread_rows(group_far_ref[...].astype(jnp.float32), group_count)
 
 
-def density_kernel(
-    reorder, coords_ref, orbit_ref, held_ref, other_ref, weights_ref, pick_ref, near_ref, *refs
-):
-    halo_ref, expansion_ref, rows_ref = refs
+def half_matrix(pieces_ref, order_ref, rows_ref):
+    chip = lax.shift_right_logical(lax.axis_index("dom"), 1)
+    for c in range(pieces_ref.shape[0] // BLOCK_ROWS):
+        first = jnp.bitwise_xor(chip, c) * BLOCK_ROWS
+        at = pl.ds(pl.multiple_of(first, BLOCK_ROWS), BLOCK_ROWS)
+        rows_ref[c * BLOCK_ROWS : (c + 1) * BLOCK_ROWS, :] = pieces_ref[at, :]
+    matrix = jnp.dot(rows_ref[...], order_ref[...], preferred_element_type=jnp.float32)
+    return matrix.astype(jnp.bfloat16)
+
+
+def quadratic(orbit_ref, start, columns, matrix):
+    points = slice(start, start + TILE)
+    product = jnp.dot(orbit_ref[points, columns], matrix, preferred_element_type=jnp.float32)
+    product = product * orbit_ref[points, :].astype(jnp.float32)
+    folded = product[:, :LANES]
+    for at in range(LANES, product.shape[1], LANES):
+        folded = folded + product[:, at : at + LANES]
+    return folded
+
+
+def core_columns(core, width):
+    return pl.ds(pl.multiple_of(core * (width // 2), LANES), width // 2)
+
+
+def first_kernel(orbit_ref, held_ref, order_ref, out_ref, rows_ref):
+    matrix = half_matrix(held_ref, order_ref, rows_ref)
+    columns = core_columns(jnp.bitwise_and(lax.axis_index("dom"), 1), orbit_ref.shape[1])
+    for start in range(0, orbit_ref.shape[0], TILE):
+        out_ref[start : start + TILE, :] = quadratic(orbit_ref, start, columns, matrix)
+
+
+def density_kernel(reorder, coords_ref, orbit_ref, other_ref, weights_ref, pick_ref, *refs):
+    *inputs, halo_ref, expansion_ref, rows_ref = refs
     leaves = coords_ref.shape[1]
     me = lax.axis_index("dom")
     if reorder:
-        pair_rows = BLOCK_ROWS
-        mine = jnp.bitwise_and(me, 1) == 0
-        for c in range(held_ref.shape[0] // pair_rows):
-            first = jnp.bitwise_xor(lax.shift_right_logical(me, 1), c) * pair_rows
-            at = pl.ds(pl.multiple_of(first, pair_rows), pair_rows)
-            held, other = held_ref[at, :], other_ref[at, :]
-            base = 2 * c * pair_rows
-            rows_ref[base : base + pair_rows, :] = jnp.where(mine, held, other)
-            rows_ref[base + pair_rows : base + 2 * pair_rows, :] = jnp.where(mine, other, held)
-        matrix = rows_ref[...]
+        matrix = half_matrix(other_ref, pick_ref, rows_ref)
+        columns = core_columns(1 - jnp.bitwise_and(me, 1), orbit_ref.shape[1])
     else:
+        held_ref, near_ref = inputs
         for k in range(near_ref.shape[1]):
             block = near_ref[0, k]
             apart = jnp.bitwise_xor(lax.shift_right_logical(block, 1), me)
@@ -175,16 +212,13 @@
             rows_ref[k * BW : (k + 1) * BW, :] = jnp.where(mine, held_ref[at, :], other_ref[at, :])
         matrix = jnp.dot(rows_ref[...], pick_ref[...], preferred_element_type=jnp.float32)
         matrix = matrix.astype(jnp.bfloat16)
+        columns = slice(None)
     total = jnp.zeros((2 * RANK, LANES), jnp.float32)
-    tile = LEAF // 2
-    for start in range(0, leaves * LEAF, tile):
-        orbit = orbit_ref[start : start + tile, :]
-        product = jnp.dot(orbit, matrix, preferred_element_type=jnp.float32)
-        product = product * orbit.astype(jnp.float32)
-        folded = product[:, :LANES]
-        for at in range(LANES, product.shape[1], LANES):
-            folded = folded + product[:, at : at + LANES]
-        for j in range(tile // LANES):
+    for start in range(0, leaves * LEAF, TILE):
+        folded = quadratic(orbit_ref, start, columns, matrix)
+        if reorder:
+            folded = folded + inputs[0][start : start + TILE, :]
+        for j in range(TILE // LANES):
             row = start // LANES + j
             part = lane_sums(folded[j * LANES : (j + 1) * LANES])
             halo_ref[row : row + 1, :] = part
@@ -270,7 +304,7 @@
                 sum_ref[at, :] += value
 
 
-def near_kernel(leaves_ref, halo_ref, even_ref, odd_ref, out_ref, values_ref, density_ref, place_ref, sum_ref):
+def near_kernel(leaves_ref, halo_ref, even_ref, odd_ref, out_ref, density_ref, place_ref, sum_ref):
     leaves = leaves_ref.shape[0]
     rows = leaves * LEAF_ROWS
     is_odd = jnp.bitwise_and(lax.axis_index("dom"), 1) == 1
@@ -279,7 +313,6 @@
     for side, held in enumerate(window):
         density_ref[side * rows : (side + 1) * rows, :] = held[:rows]
         place_ref[24 * side : 24 * (side + 1), :] = places(held, rows)
-    values_ref[...] = halo_ref[:rows, :]
 
     def one_leaf(leaf, carry):
         own_place = [place_ref[pl.ds(24 + leaf + 8 * k, 1), :] for k in range(3)]
@@ -339,7 +372,10 @@
     return jnp.broadcast_to(local, (RANK, LANES))
 
 
-def potential_kernel(expansion_ref, mask_ref, weights_ref, dev_ref, near_ref, out_ref):
+def potential_kernel(
+    expansion_ref, mask_ref, weights_ref, dev_ref, near_ref, halo_ref, out_ref, density_ref
+):
+    density_ref[...] = halo_ref[: density_ref.shape[0], :]
     local = far_field(expansion_ref, mask_ref, dev_ref)
     for row in range(out_ref.shape[0]):
         at = slice(row * LANES, (row + 1) * LANES)
@@ -387,7 +423,7 @@
     def load():
         operands = (near_blocks, leaf_transfer, dev_transfer, leaf_basis)
         return pl.pallas_call(
-            load_kernel,
+            functools.partial(load_kernel, reorder),
             out_shape=(
                 jax.ShapeDtypeStruct((points, width), jnp.bfloat16),
                 jax.ShapeDtypeStruct((natural, width), jnp.bfloat16),
@@ -408,6 +444,7 @@
         shapes = [jax.ShapeDtypeStruct((dev_far.shape[1] + group_far.shape[1], LANES), f32)]
         if reorder:
             shapes.append(jax.ShapeDtypeStruct((points, natural), jnp.bfloat16))
+            shapes.append(jax.ShapeDtypeStruct((natural, natural), jnp.bfloat16))
         out = pl.pallas_call(
             functools.partial(prepare_kernel, reorder),
             out_shape=shapes,
@@ -419,23 +456,39 @@
             cost_estimate=cost(2 * points * width * natural),
             name="prepare",
         )(*[in_hbm(x) for x in operands], orbit, pick)
-        return out if reorder else [*out, orbit]
-
-    held, other, (_, pick, weights), (mask, orbit) = gather_rows(density_rows, load, prepare)
-
+        return out if reorder else [*out, orbit, pick]
+
+    held, other, (_, _, weights), (mask, orbit, pick) = gather_rows(density_rows, load, prepare)
+
+    if reorder:
+        rest = [
+            pl.pallas_call(
+                first_kernel,
+                out_shape=jax.ShapeDtypeStruct((points, LANES), f32),
+                in_specs=[VMEM] * 3,
+                out_specs=VMEM,
+                scratch_shapes=[pltpu.VMEM((natural // 2, natural), jnp.bfloat16)],
+                compiler_params=params,
+                cost_estimate=cost(points * width * width),
+                name="first",
+            )(orbit, held, pick)
+        ]
+        rows_shape = (natural // 2, natural)
+    else:
+        rest, rows_shape = [held, near_blocks], (width, natural)
     halo, expansion = pl.pallas_call(
         functools.partial(density_kernel, reorder),
         out_shape=(
             jax.ShapeDtypeStruct((rows + 8, LANES), f32),
             jax.ShapeDtypeStruct((devices, 2, LANES), f32),
         ),
-        in_specs=[VMEM] * 5 + ([ANY, ANY] if reorder else [VMEM, SMEM]),
+        in_specs=[VMEM] * 6 + ([] if reorder else [SMEM]),
         out_specs=(VMEM, VMEM),
-        scratch_shapes=[pltpu.VMEM((width, natural), jnp.bfloat16)],
+        scratch_shapes=[pltpu.VMEM(rows_shape, jnp.bfloat16)],
         compiler_params=params,
-        cost_estimate=cost(2 * points * width * width),
+        cost_estimate=cost(points * width * width),
         name="density",
-    )(leaf_coords, orbit, held, other, weights, pick, near_blocks)
+    )(leaf_coords, orbit, other, weights, pick, *rest)
 
     even = swap(halo, "dom", 1)
     pairs = [(i, i + 1 if i % 2 else i - 1) for i in range(1, dom_count - 1)]
@@ -443,11 +496,11 @@
     everyone = lax.all_to_all(expansion, ("group", "dom"), 0, 0)
 
     table = jax.ShapeDtypeStruct((rows, LANES), f32)
-    near, density = pl.pallas_call(
+    near = pl.pallas_call(
         near_kernel,
-        out_shape=(table, table),
+        out_shape=table,
         in_specs=[SMEM] + [VMEM] * 3,
-        out_specs=(VMEM, VMEM),
+        out_specs=VMEM,
         scratch_shapes=[
             pltpu.VMEM((3 * rows, LANES), f32),
             pltpu.VMEM((72, LANES), f32),
@@ -456,16 +509,16 @@
         compiler_params=params,
         cost_estimate=cost(20 << 20, 4 << 20),
         name="near",
-    )(near_leaves, halo, even, odd)
-    hartree = pl.pallas_call(
+    )(pltpu.with_memory_space_constraint(near_leaves, pltpu.SMEM), halo, even, odd)
+    hartree, density = pl.pallas_call(
         potential_kernel,
-        out_shape=table,
-        in_specs=[VMEM] * 5,
-        out_specs=VMEM,
+        out_shape=(table, table),
+        in_specs=[VMEM] * 6,
+        out_specs=(VMEM, VMEM),
         compiler_params=params,
         cost_estimate=cost(4 << 20, 1 << 20),
         name="potential",
-    )(everyone, mask, weights, dev_transfer, near)
+    )(everyone, mask, weights, dev_transfer, near, halo)
     return (density.reshape(-1), hartree.reshape(-1))
 
 

time: 33.9 us -> 33.1 us (0.976)
  waiting for transfers between devices: 4.41 us -> 3.32 us
    ppermute x6, waiting for transfers between devices: 4.4 us -> 3.32 us  [swap(): lax.ppermute(value, axis, [(i, i ^ mask) for i in range(lax.axis_size(axi...]
    pallas_call x3 -> x4, Pallas kernels: 7.08 us -> 8.12 us  [the longest x1 3.14 us: local(): pl.pallas_call(near_kernel, out_shape=table, in_specs=[SMEM] + [VMEM] * 3...]
    pallas_call x1, Pallas kernels: 2.68 us -> 2.14 us  [local(): pl.pallas_call(functools.partial(density_kernel, reorder), out_shape=(jax...]
  transfers between devices with their start and end apart: 8 -> 8, of which waited for: 4 -> 5; matrix products, arithmetic and copies ran while one was open for 0% -> 0% of each run, Pallas kernels for 25% -> 28%
where the time goes in v4:
time: 33.1 us; the launch traced here: 32.4 us
  starting transfers between devices  15.7 us (47%)
  Pallas kernels  12.5 us (38%)
  waiting for transfers between devices  3.32 us (10%)
  between operations  0.75 us (2%)
    ppermute x6, starting transfers between devices, swap(): lax.ppermute(value, axis, [(i, i ^ mask) for i in range(lax.axis_size(axi...  10.8 us
    all_to_all x1, starting transfers between devices, local(): everyone = lax.all_to_all(expansion, ('group', 'dom'), 0, 0)  4.24 us
    ppermute x6, waiting for transfers between devices, swap(): lax.ppermute(value, axis, [(i, i ^ mask) for i in range(lax.axis_size(axi...  3.32 us
    pallas_call x1, Pallas kernels, local(): pl.pallas_call(near_kernel, out_shape=table, in_specs=[SMEM] + [VMEM] * 3...  3.14 us
    pallas_call x1, Pallas kernels, load(): pl.pallas_call(functools.partial(load_kernel, reorder), out_shape=(jax.Sh...  2.41 us
    pallas_call x1, Pallas kernels, prepare(): pl.pallas_call(functools.partial(prepare_kernel, reorder), out_shape=shap...  2.29 us
    pallas_call x1, Pallas kernels, local(): pl.pallas_call(functools.partial(density_kernel, reorder), out_shape=(jax...  2.14 us
    pallas_call x1, Pallas kernels, local(): pl.pallas_call(potential_kernel, out_shape=(table, table), in_specs=[VMEM...  1.29 us
  transfers between devices with their start and end apart: 8, of which 5 were waited for; matrix products, arithmetic and copies ran while one was open for 0% of the time, Pallas kernels for 28%

profile of v4, /device:TPU:0, one launch (start us, length us, event | category | flops | bytes accessed | tf_op | source)
XLA Modules:
  0.0 32.4 jit_solution(16534707962404517758)
XLA Ops:
  0.6 0.0 copy-start.2
  0.6 3.0 %collective-permute-start = (bf16[32,512]{1,0:T(8,128)(2,1)}, bf16[32,512]{1,0:T(8,128)(2,1)S(1)}, u32[]{:S(2)}, u32[]{:S(2)}) collective-permute-start(bf16[32,512]{1,0:T(8,128)(2,1)} %param.11), channel_id=1, source_target_pairs={{0,2},{1,3},{2,0},{3,1},{4,6},{5,7},{6,4},{7,5},{8,10},{9,11},{10,... | collective-permute-start | bytes 98312 | tf_op jit(solution)/shard_map/ppermute | solution.py:38
  3.7 2.4 %load.1 = (bf16[3072,512]{1,0:T(8,128)(2,1)S(1)}, bf16[512,512]{1,0:T(8,128)(2,1)S(1)}, f32[128,3072]{1,0:T(8,128)S(1)}) custom-call(s32[1,32]{1,0:T(1,128)} %near_hbm.1, f32[6,64,64]{2,1,0:T(8,128)} %transfer_hbm.1, f32[1,64,64]{2,1,0:T(8,128)} %dev_ref.1, f32[64,3072]{1,0:T(8,128)} %basis_hbm.1, bf16[3072,512]{1,0:T(8,128)(2,1)} %orbitals_hbm.1), custom_call_target="tpu_custom_call" | custom-call | flops 1048576 | bytes 4194304 | tf_op jit(solution)/shard_map/load/pallas_call | solution.py:425
  6.1 0.0 collective-permute-done
  6.1 0.0 copy-done.2
  6.1 3.8 %collective-permute-start.3 = (bf16[64,512]{1,0:T(8,128)(2,1)S(1)}, bf16[64,512]{1,0:T(8,128)(2,1)S(1)}, u32[]{:S(2)}, u32[]{:S(2)}) collective-permute-start(bf16[64,512]{1,0:T(8,128)(2,1)S(1)} %pad_maximum_fusion.1), channel_id=1, source_target_pairs={{0,12},{1,13},{2,14},{3,15},{4,8},{5,9},{6,10},{7,11},{8,4},{9,5},... | collective-permute-start | bytes 196616 | tf_op jit(solution)/shard_map/ppermute | solution.py:38
  10.0 0.0 collective-permute-start.2
  10.0 0.6 %collective-permute-start.1 = (bf16[64,512]{1,0:T(8,128)(2,1)S(1)}, bf16[64,512]{1,0:T(8,128)(2,1)S(1)}, u32[]{:S(2)}, u32[]{:S(2)}) collective-permute-start(bf16[64,512]{1,0:T(8,128)(2,1)S(1)} %pad_maximum_fusion.1), channel_id=1, source_target_pairs={{0,4},{1,5},{2,6},{3,7},{4,0},{5,1},{6,2},{7,3},{8,12},{9,13},{10,... | collective-permute-start | bytes 196616 | tf_op jit(solution)/shard_map/ppermute | solution.py:38
  10.6 2.3 %prepare.1 = (f32[18,128]{1,0:T(8,128)S(1)}, bf16[3072,512]{1,0:T(8,128)(2,1)S(1)}, bf16[512,512]{1,0:T(8,128)(2,1)S(1)}) custom-call(s32[1,16]{1,0:T(1,128)} %far_hbm.1, s32[1,2]{1,0:T(1,128)} %group_far_hbm.1, bf16[3072,512]{1,0:T(8,128)(2,1)S(1)} %get-tuple-element.24.orbit_ref, bf16[512,512]{1,0:T(8,128)(2,1)S(1)} %get-tuple-element.25.pick_ref), custom_call_target="tpu_custom_call" | custom-call | flops 1610612736 | bytes 4194304 | tf_op jit(solution)/shard_map/prepare/pallas_call | solution.py:448
  12.9 0.0 copy-start.1
  12.9 0.2 collective-permute-done.3
  13.1 2.1 %collective-permute-done.2 = bf16[64,512]{1,0:T(8,128)(2,1)S(1)} collective-permute-done((bf16[64,512]{1,0:T(8,128)(2,1)S(1)}, bf16[64,512]{1,0:T(8,128)(2,1)S(1)}, u32[]{:S(2)}, u32[]{:S(2)}) %collective-permute-start.2) | collective-permute-done | bytes 65568 | tf_op jit(solution)/shard_map/ppermute | solution.py:38
  15.2 0.1 collective-permute-done.1
  15.3 0.1 collective-permute-start.4
  15.4 1.3 %first.1.refs_0_ = f32[3072,128]{1,0:T(8,128)S(1)} custom-call(bf16[3072,512]{1,0:T(8,128)(2,1)S(1)} %get-tuple-element.29.orbit_ref, bf16[256,512]{1,0:T(8,128)(2,1)S(1)} %pad_maximum_fusion.held_ref, bf16[512,512]{1,0:T(8,128)(2,1)S(1)} %get-tuple-element.32.order_ref.pick_ref), custom_call_target="tpu_custom_call" | custom-call | flops 805306368 | bytes 4194304 | tf_op jit(solution)/shard_map/first/pallas_call | solution.py:465
  16.6 0.0 copy-start.3
  16.6 0.2 collective-permute-done.4.other_ref
  16.9 0.0 copy-done.1
  16.9 2.1 %density.1 = (f32[32,128]{1,0:T(8,128)S(1)}, f32[32,2,128]{2,1,0:T(2,128)}) custom-call(s32[3,6]{1,0:T(4,128)S(1)} %copy-done.1, bf16[3072,512]{1,0:T(8,128)(2,1)S(1)} %get-tuple-element.29.orbit_ref, bf16[256,512]{1,0:T(8,128)(2,1)S(1)} %collective-permute-done.4.other_ref, f32[128,3072]{1,0:T(8,128)S(1)} %get-tuple-element.31.weights_ref, ...), custom_call_target="tpu_custom_call" | custom-call | flops 805306368 | bytes 4194304 | tf_op jit(solution)/shard_map/density/pallas_call | solution.py:479
  19.0 4.2 %all-to-all-start = ((f32[32,2,128]{2,1,0:T(2,128)}), f32[32,2,128]{2,1,0:T(2,128)S(1)}, u32[]{:S(2)}, u32[]{:S(2)}) async-start(f32[32,2,128]{2,1,0:T(2,128)} %get-tuple-element.33), calls=%async_computation | async-start | bytes 65536 | tf_op jit(solution)/shard_map/all_to_all | solution.py:496
  23.3 0.7 %collective-permute-start.6 = (f32[32,128]{1,0:T(8,128)S(1)}, f32[32,128]{1,0:T(8,128)S(1)}, u32[]{:S(2)}, u32[]{:S(2)}) collective-permute-start(f32[32,128]{1,0:T(8,128)S(1)} %get-tuple-element.35.halo_ref), channel_id=1, source_target_pairs={{1,2},{2,1},{3,4},{4,3},{5,6},{6,5},{7,8},{8,7},{9,10},{10,9},{11,... | collective-permute-start | bytes 49160 | tf_op jit(solution)/shard_map/ppermute | solution.py:495
  23.9 3.2 %collective-permute-start.5 = (f32[32,128]{1,0:T(8,128)S(1)}, f32[32,128]{1,0:T(8,128)S(1)}, u32[]{:S(2)}, u32[]{:S(2)}) collective-permute-start(f32[32,128]{1,0:T(8,128)S(1)} %get-tuple-element.35.halo_ref), channel_id=1, source_target_pairs={{0,1},{1,0},{2,3},{3,2},{4,5},{5,4},{6,7},{7,6},{8,9},{9,8},{10,11... | collective-permute-start | bytes 49160 | tf_op jit(solution)/shard_map/ppermute | solution.py:38
  27.1 0.0 copy-done.3
  27.1 0.1 copy.12.leaves_ref
  27.2 0.0 copy-start
  27.2 0.0 collective-permute-done.6.odd_ref
  27.2 0.7 %collective-permute-done.5.even_ref = f32[32,128]{1,0:T(8,128)S(1)} collective-permute-done((f32[32,128]{1,0:T(8,128)S(1)}, f32[32,128]{1,0:T(8,128)S(1)}, u32[]{:S(2)}, u32[]{:S(2)}) %collective-permute-start.5) | collective-permute-done | bytes 16416 | tf_op jit(solution)/shard_map/ppermute | solution.py:38
  28.0 3.1 %near.1.near_ref = f32[24,128]{1,0:T(8,128)S(1)} custom-call(s32[6,3]{1,0:T(8,128)S(1)} %copy.12.leaves_ref, f32[32,128]{1,0:T(8,128)S(1)} %get-tuple-element.35.halo_ref, f32[32,128]{1,0:T(8,128)S(1)} %collective-permute-done.5.even_ref, f32[32,128]{1,0:T(8,128)S(1)} %collective-permute-done.6.odd_ref), custom_call_target="tpu_custom_call" | custom-call | flops 20971520 | bytes 4194304 | tf_op jit(solution)/shard_map/near/pallas_call | solution.py:499
  31.1 0.0 all-to-all-done.expansion_ref
  31.1 0.0 copy-done
  31.1 1.3 %potential.1 = (f32[24,128]{1,0:T(8,128)}, f32[24,128]{1,0:T(8,128)}) custom-call(f32[32,2,128]{2,1,0:T(2,128)S(1)} %all-to-all-done.expansion_ref, f32[18,128]{1,0:T(8,128)S(1)} %get-tuple-element.34.mask_ref, f32[128,3072]{1,0:T(8,128)S(1)} %get-tuple-element.31.weights_ref, f32[1,64,64]{2,1,0:T(8,128)S(1)} %copy-done, f32[24,128]{1,0:T(8,128)S(1)} %near.1.near_ref, ...), custom_call_target="tpu_custom_call" | custom-call | flops 4194304 | bytes 4194304 | tf_op jit(solution)/shard_map/potential/pallas_call | solution.py:513
  (2 shorter events, 0.0 us)
Async XLA Ops:
  0.6 5.5 %copy-start.2 = (bf16[32,512]{1,0:T(8,128)(2,1)S(1)}, bf16[32,512]{1,0:T(8,128)(2,1)}, u32[]{:S(2)}) copy-start(bf16[32,512]{1,0:T(8,128)(2,1)} %param.11) | copy-start | bytes 98308
  0.6 5.5 %collective-permute-start = (bf16[32,512]{1,0:T(8,128)(2,1)}, bf16[32,512]{1,0:T(8,128)(2,1)S(1)}, u32[]{:S(2)}, u32[]{:S(2)}) collective-permute-start(bf16[32,512]{1,0:T(8,128)(2,1)} %param.11), channel_id=1, source_target_pairs={{0,2},{1,3},{2,0},{3,1},{4,6},{5,7},{6,4},{7,5},{8,10},{9,11},{10,... | collective-permute-start | bytes 98312 | tf_op jit(solution)/shard_map/ppermute | solution.py:38
  6.1 6.9 %collective-permute-start.3 = (bf16[64,512]{1,0:T(8,128)(2,1)S(1)}, bf16[64,512]{1,0:T(8,128)(2,1)S(1)}, u32[]{:S(2)}, u32[]{:S(2)}) collective-permute-start(bf16[64,512]{1,0:T(8,128)(2,1)S(1)} %pad_maximum_fusion.1), channel_id=1, source_target_pairs={{0,12},{1,13},{2,14},{3,15},{4,8},{5,9},{6,10},{7,11},{8,4},{9,5},... | collective-permute-start | bytes 196616 | tf_op jit(solution)/shard_map/ppermute | solution.py:38
  10.0 5.2 %collective-permute-start.2 = (bf16[64,512]{1,0:T(8,128)(2,1)S(1)}, bf16[64,512]{1,0:T(8,128)(2,1)S(1)}, u32[]{:S(2)}, u32[]{:S(2)}) collective-permute-start(bf16[64,512]{1,0:T(8,128)(2,1)S(1)} %pad_maximum_fusion.1), channel_id=1, source_target_pairs={{0,8},{1,9},{2,10},{3,11},{4,12},{5,13},{6,14},{7,15},{8,0},{9,1},... | collective-permute-start | bytes 196616 | tf_op jit(solution)/shard_map/ppermute | solution.py:38
  10.0 5.3 %collective-permute-start.1 = (bf16[64,512]{1,0:T(8,128)(2,1)S(1)}, bf16[64,512]{1,0:T(8,128)(2,1)S(1)}, u32[]{:S(2)}, u32[]{:S(2)}) collective-permute-start(bf16[64,512]{1,0:T(8,128)(2,1)S(1)} %pad_maximum_fusion.1), channel_id=1, source_target_pairs={{0,4},{1,5},{2,6},{3,7},{4,0},{5,1},{6,2},{7,3},{8,12},{9,13},{10,... | collective-permute-start | bytes 196616 | tf_op jit(solution)/shard_map/ppermute | solution.py:38
  12.9 4.0 %copy-start.1 = (s32[3,6]{1,0:T(4,128)S(1)}, s32[3,6]{1,0:T(4,128)}, u32[]{:S(2)}) copy-start(s32[3,6]{1,0:T(4,128)} %coords_ref.1) | copy-start | bytes 220
  15.3 1.6 %collective-permute-start.4 = (bf16[256,512]{1,0:T(8,128)(2,1)S(1)}, bf16[256,512]{1,0:T(8,128)(2,1)S(1)}, u32[]{:S(2)}, u32[]{:S(2)}) collective-permute-start(bf16[256,512]{1,0:T(8,128)(2,1)S(1)} %pad_maximum_fusion.held_ref), channel_id=1, source_target_pairs={{0,1},{1,0},{2,3},{3,2},{4,5},{5,4},{6,7},{7,6},{8,9},{9,8},{10,11... | collective-permute-start | bytes 786440 | tf_op jit(solution)/shard_map/ppermute | solution.py:38
  16.6 10.5 %copy-start.3 = (s32[6,3]{0,1:T(4,128)S(1)}, s32[6,3]{0,1:T(4,128)}, u32[]{:S(2)}) copy-start(s32[6,3]{0,1:T(4,128)} %param.14) | copy-start | bytes 220
  19.0 12.1 %all-to-all-start = ((f32[32,2,128]{2,1,0:T(2,128)}), f32[32,2,128]{2,1,0:T(2,128)S(1)}, u32[]{:S(2)}, u32[]{:S(2)}) async-start(f32[32,2,128]{2,1,0:T(2,128)} %get-tuple-element.33), calls=%async_computation | async-start | bytes 65536 | tf_op jit(solution)/shard_map/all_to_all | solution.py:496
  23.3 4.0 %collective-permute-start.6 = (f32[32,128]{1,0:T(8,128)S(1)}, f32[32,128]{1,0:T(8,128)S(1)}, u32[]{:S(2)}, u32[]{:S(2)}) collective-permute-start(f32[32,128]{1,0:T(8,128)S(1)} %get-tuple-element.35.halo_ref), channel_id=1, source_target_pairs={{1,2},{2,1},{3,4},{4,3},{5,6},{6,5},{7,8},{8,7},{9,10},{10,9},{11,... | collective-permute-start | bytes 49160 | tf_op jit(solution)/shard_map/ppermute | solution.py:495
  23.9 4.0 %collective-permute-start.5 = (f32[32,128]{1,0:T(8,128)S(1)}, f32[32,128]{1,0:T(8,128)S(1)}, u32[]{:S(2)}, u32[]{:S(2)}) collective-permute-start(f32[32,128]{1,0:T(8,128)S(1)} %get-tuple-element.35.halo_ref), channel_id=1, source_target_pairs={{0,1},{1,0},{2,3},{3,2},{4,5},{5,4},{6,7},{7,6},{8,9},{9,8},{10,11... | collective-permute-start | bytes 49160 | tf_op jit(solution)/shard_map/ppermute | solution.py:38
  27.2 3.9 %copy-start = (f32[1,64,64]{2,1,0:T(8,128)S(1)}, f32[1,64,64]{2,1,0:T(8,128)}, u32[]{:S(2)}) copy-start(f32[1,64,64]{2,1,0:T(8,128)} %dev_ref.1) | copy-start | bytes 49156

commit v5 on v4

--- a/solution.py
+++ b/solution.py
@@ -271,40 +271,61 @@
     return SIDE * jnp.concatenate(parts, axis=0)
 
 
-def add_pair(sum_ref, own_place, place, rho, fresh):
+def pair_kernel(shift, y, square_x, square_z):
+    lane = iota((8, LANES), 1)
+    apart = shift[1] + (y - lane // SIDE % SIDE).astype(jnp.float32)
+    square = apart * apart + square_z
+    even = [lax.rsqrt(x + square) for x in square_x]
+    low = lane < LANES // 2
+    return even, [jnp.where(low, a, b) for a, b in zip(even[:-1], even[1:], strict=True)]
+
+
+def pair_squares(shift):
     lane, row = iota((8, LANES), 1), iota((8, LANES), 0)
-    low = lane < LANES // 2
-    half = jnp.where(low, 0.0, 1.0)
-    at_y = (lane // SIDE % SIDE).astype(jnp.float32)
-    along_z = (row - lane % SIDE).astype(jnp.float32)
-    shift = [jnp.broadcast_to(a - b, (8, LANES)) for a, b in zip(own_place, place, strict=True)]
-    rho = [jnp.broadcast_to(r, (8, LANES)) for r in rho]
-    swapped = [pltpu.roll(r, LANES // 2, 1) for r in rho]
-    along = shift[2] + along_z
-    square_z = along * along + soft_square
+    half = jnp.where(lane < LANES // 2, 0.0, 1.0)
+    along = shift[2] + (row - lane % SIDE).astype(jnp.float32)
     square_x = []
     for m in range(-6, SIDE + 2, 2):
         apart = shift[0] + (m - half)
         square_x.append(apart * apart)
+    return square_x, along * along + soft_square
+
+
+def leaf_density(density_ref, leaf):
+    rows = [density_ref[pl.ds(leaf * LEAF_ROWS + j, 1), :] for j in range(LEAF_ROWS)]
+    rows = [jnp.broadcast_to(row, (8, LANES)) for row in rows]
+    return rows, [pltpu.roll(row, LANES // 2, 1) for row in rows]
+
+
+def pair_sums(kernel, density, y):
+    for x in range(SIDE):
+        first = x // 2 + 3
+        k, rho = kernel[x % 2], density[x % 2]
+        value = k[first] * rho[0]
+        for j in range(1, LEAF_ROWS):
+            value = value + k[first - j] * rho[j]
+        yield slice((x * SIDE + y) * SIDE, (x * SIDE + y + 1) * SIDE), value
+
+
+def leaf_place(place_ref, leaf):
+    return [place_ref[pl.ds(leaf + 8 * k, 1), :] for k in range(3)]
+
+
+def self_kernel(halo_ref, sum_ref, place_ref):
+    leaves = sum_ref.shape[0]
+    place_ref[...] = places(halo_ref[...], leaves * LEAF_ROWS)
+    shift = [jnp.zeros((8, LANES), jnp.float32)] * 3
+    square_x, square_z = pair_squares(shift)
     for y in range(SIDE):
-        apart = shift[1] + (y - at_y)
-        square = apart * apart + square_z
-        even = [lax.rsqrt(x + square) for x in square_x]
-        odd = [jnp.where(low, a, b) for a, b in zip(even[:-1], even[1:], strict=True)]
-        for x in range(SIDE):
-            first = x // 2 + 3
-            kernel, density = (odd, swapped) if x % 2 else (even, rho)
-            value = kernel[first] * density[0]
-            for j in range(1, LEAF_ROWS):
-                value = value + kernel[first - j] * density[j]
-            at = slice((x * SIDE + y) * SIDE, (x * SIDE + y + 1) * SIDE)
-            if fresh:
-                sum_ref[at, :] = value
-            else:
-                sum_ref[at, :] += value
-
-
-def near_kernel(leaves_ref, halo_ref, even_ref, odd_ref, out_ref, density_ref, place_ref, sum_ref):
+        kernel = pair_kernel(shift, y, square_x, square_z)
+        for leaf in range(leaves):
+            for at, value in pair_sums(kernel, leaf_density(halo_ref, leaf), y):
+                sum_ref[leaf, at, :] = value
+
+
+def near_kernel(
+    leaves_ref, halo_ref, even_ref, odd_ref, own_ref, part_ref, out_ref, density_ref, place_ref, sum_ref
+):
     leaves = leaves_ref.shape[0]
     rows = leaves * LEAF_ROWS
     is_odd = jnp.bitwise_and(lax.axis_index("dom"), 1) == 1
@@ -312,24 +333,31 @@
     window = (jnp.where(is_odd, even, odd), halo_ref[...], jnp.where(is_odd, odd, even))
     for side, held in enumerate(window):
         density_ref[side * rows : (side + 1) * rows, :] = held[:rows]
-        place_ref[24 * side : 24 * (side + 1), :] = places(held, rows)
-
-    def one_leaf(leaf, carry):
-        own_place = [place_ref[pl.ds(24 + leaf + 8 * k, 1), :] for k in range(3)]
-        for slot in range(NEARL):
-            position = leaves_ref[leaf, slot]
+        place_ref[24 * side : 24 * (side + 1), :] = own_ref[...] if side == 1 else places(held, rows)
+    for leaf in range(leaves):
+        own_place = leaf_place(own_ref, leaf)
+        named = [leaves_ref[leaf, slot] for slot in range(NEARL)]
+        own = leaves + leaf
+        others = (
+            jnp.where(named[0] == own, named[1], named[0]),
+            jnp.where(named[2] == own, named[1], named[2]),
+        )
+        for slot, position in enumerate(others):
             side = (position >= leaves).astype(jnp.int32)
             side = side + (position >= 2 * leaves).astype(jnp.int32)
-            first = 24 * side + position - leaves * side
-            place = [place_ref[pl.ds(first + 8 * k, 1), :] for k in range(3)]
-            rho = [density_ref[pl.ds(position * LEAF_ROWS + j, 1), :] for j in range(LEAF_ROWS)]
-            add_pair(sum_ref, own_place, place, rho, slot == 0)
+            place = leaf_place(place_ref, 24 * side + position - leaves * side)
+            shift = [jnp.broadcast_to(p - q, (8, LANES)) for p, q in zip(own_place, place, strict=True)]
+            square_x, square_z = pair_squares(shift)
+            density = leaf_density(density_ref, position)
+            for y in range(SIDE):
+                kernel = pair_kernel(shift, y, square_x, square_z)
+                for at, value in pair_sums(kernel, density, y):
+                    before = part_ref[leaf, at, :] if slot == 0 else sum_ref[leaf, at, :]
+                    sum_ref[leaf, at, :] = before + value
         for j in range(LEAF_ROWS):
-            part = lane_sums(sum_ref[j * LANES : (j + 1) * LANES, :])
-            out_ref[pl.ds(leaf * LEAF_ROWS + j, 1), :] = vol_weight * part
-        return carry
-
-    lax.fori_loop(0, leaves, one_leaf, 0)
+            part = lane_sums(sum_ref[leaf, j * LANES : (j + 1) * LANES, :])
+            row = leaf * LEAF_ROWS + j
+            out_ref[row : row + 1, :] = vol_weight * part
 
 
 def far_field(expansion_ref, mask_ref, dev_ref):
@@ -496,20 +524,31 @@
     everyone = lax.all_to_all(expansion, ("group", "dom"), 0, 0)
 
     table = jax.ShapeDtypeStruct((rows, LANES), f32)
+    sums = jax.ShapeDtypeStruct((leaves, LEAF, LANES), f32)
+    places_shape = jax.ShapeDtypeStruct((24, LANES), f32)
+    near_sums, own_places = pl.pallas_call(
+        self_kernel,
+        out_shape=(sums, places_shape),
+        in_specs=[VMEM],
+        out_specs=(VMEM, VMEM),
+        compiler_params=params,
+        cost_estimate=cost(20 << 20, 4 << 20),
+        name="self",
+    )(halo)
     near = pl.pallas_call(
         near_kernel,
         out_shape=table,
-        in_specs=[SMEM] + [VMEM] * 3,
+        in_specs=[SMEM] + [VMEM] * 5,
         out_specs=VMEM,
         scratch_shapes=[
             pltpu.VMEM((3 * rows, LANES), f32),
             pltpu.VMEM((72, LANES), f32),
-            pltpu.VMEM((LEAF, LANES), f32),
+            pltpu.VMEM((leaves, LEAF, LANES), f32),
         ],
         compiler_params=params,
         cost_estimate=cost(20 << 20, 4 << 20),
         name="near",
-    )(pltpu.with_memory_space_constraint(near_leaves, pltpu.SMEM), halo, even, odd)
+    )(near_leaves, halo, even, odd, own_places, near_sums)
     hartree, density = pl.pallas_call(
         potential_kernel,
         out_shape=(table, table),

time: 33.1 us -> 32.1 us (0.970); the launches traced: 32.4 us -> 31.8 us
  Pallas kernels: 12.5 us -> 12 us
    pallas_call x1 -> x2, Pallas kernels: 3.14 us -> 2.57 us  [the longest x1 2.12 us: local(): pl.pallas_call(near_kernel, out_shape=table, in_specs=[SMEM] + [VMEM] * 5...]
    ppermute x6, waiting for transfers between devices: 3.32 us -> 2.85 us  [swap(): lax.ppermute(value, axis, [(i, i ^ mask) for i in range(lax.axis_size(axi...]
    all_to_all x1, waiting for transfers between devices: 0.01 us -> 0.42 us  [local(): everyone = lax.all_to_all(expansion, ('group', 'dom'), 0, 0)]
  transfers between devices with their start and end apart: 8 -> 8, of which waited for: 5 -> 6; matrix products, arithmetic and copies ran while one was open for 0% -> 0% of each run, Pallas kernels for 28% -> 27%
where the time goes in v5:
time: 32.1 us; the launch traced here: 31.8 us
  starting transfers between devices  15.7 us (49%)
  Pallas kernels  12 us (37%)
  waiting for transfers between devices  3.27 us (10%)
  between operations  0.75 us (2%)
    ppermute x6, starting transfers between devices, swap(): lax.ppermute(value, axis, [(i, i ^ mask) for i in range(lax.axis_size(axi...  10.8 us
    all_to_all x1, starting transfers between devices, local(): everyone = lax.all_to_all(expansion, ('group', 'dom'), 0, 0)  4.24 us
    ppermute x6, waiting for transfers between devices, swap(): lax.ppermute(value, axis, [(i, i ^ mask) for i in range(lax.axis_size(axi...  2.85 us
    pallas_call x1, Pallas kernels, load(): pl.pallas_call(functools.partial(load_kernel, reorder), out_shape=(jax.Sh...  2.41 us
    pallas_call x1, Pallas kernels, prepare(): pl.pallas_call(functools.partial(prepare_kernel, reorder), out_shape=shap...  2.29 us
    pallas_call x1, Pallas kernels, local(): pl.pallas_call(functools.partial(density_kernel, reorder), out_shape=(jax...  2.14 us
    pallas_call x1, Pallas kernels, local(): pl.pallas_call(near_kernel, out_shape=table, in_specs=[SMEM] + [VMEM] * 5...  2.12 us
    pallas_call x1, Pallas kernels, local(): pl.pallas_call(potential_kernel, out_shape=(table, table), in_specs=[VMEM...  1.29 us
  transfers between devices with their start and end apart: 8, of which 6 were waited for; matrix products, arithmetic and copies ran while one was open for 0% of the time, Pallas kernels for 27%

profile of v5, /device:TPU:0, one launch (start us, length us, event | category | flops | bytes accessed | tf_op | source)
XLA Modules:
  0.0 31.8 jit_solution(13178759729426146634)
XLA Ops:
  0.6 0.0 copy-start.2
  0.6 3.0 %collective-permute-start = (bf16[32,512]{1,0:T(8,128)(2,1)}, bf16[32,512]{1,0:T(8,128)(2,1)S(1)}, u32[]{:S(2)}, u32[]{:S(2)}) collective-permute-start(bf16[32,512]{1,0:T(8,128)(2,1)} %param.11), channel_id=1, source_target_pairs={{0,2},{1,3},{2,0},{3,1},{4,6},{5,7},{6,4},{7,5},{8,10},{9,11},{10,... | collective-permute-start | bytes 98312 | tf_op jit(solution)/shard_map/ppermute | solution.py:38
  3.7 2.4 %load.1 = (bf16[3072,512]{1,0:T(8,128)(2,1)S(1)}, bf16[512,512]{1,0:T(8,128)(2,1)S(1)}, f32[128,3072]{1,0:T(8,128)S(1)}) custom-call(s32[1,32]{1,0:T(1,128)} %near_hbm.1, f32[6,64,64]{2,1,0:T(8,128)} %transfer_hbm.1, f32[1,64,64]{2,1,0:T(8,128)} %dev_ref.1, f32[64,3072]{1,0:T(8,128)} %basis_hbm.1, bf16[3072,512]{1,0:T(8,128)(2,1)} %orbitals_hbm.1), custom_call_target="tpu_custom_call" | custom-call | flops 1048576 | bytes 4194304 | tf_op jit(solution)/shard_map/load/pallas_call | solution.py:453
  6.1 0.0 collective-permute-done
  6.1 0.0 copy-done.2
  6.1 3.8 %collective-permute-start.3 = (bf16[64,512]{1,0:T(8,128)(2,1)S(1)}, bf16[64,512]{1,0:T(8,128)(2,1)S(1)}, u32[]{:S(2)}, u32[]{:S(2)}) collective-permute-start(bf16[64,512]{1,0:T(8,128)(2,1)S(1)} %pad_maximum_fusion.1), channel_id=1, source_target_pairs={{0,12},{1,13},{2,14},{3,15},{4,8},{5,9},{6,10},{7,11},{8,4},{9,5},... | collective-permute-start | bytes 196616 | tf_op jit(solution)/shard_map/ppermute | solution.py:38
  10.0 0.0 collective-permute-start.2
  10.0 0.6 %collective-permute-start.1 = (bf16[64,512]{1,0:T(8,128)(2,1)S(1)}, bf16[64,512]{1,0:T(8,128)(2,1)S(1)}, u32[]{:S(2)}, u32[]{:S(2)}) collective-permute-start(bf16[64,512]{1,0:T(8,128)(2,1)S(1)} %pad_maximum_fusion.1), channel_id=1, source_target_pairs={{0,4},{1,5},{2,6},{3,7},{4,0},{5,1},{6,2},{7,3},{8,12},{9,13},{10,... | collective-permute-start | bytes 196616 | tf_op jit(solution)/shard_map/ppermute | solution.py:38
  10.6 2.3 %prepare.1 = (f32[18,128]{1,0:T(8,128)S(1)}, bf16[3072,512]{1,0:T(8,128)(2,1)S(1)}, bf16[512,512]{1,0:T(8,128)(2,1)S(1)}) custom-call(s32[1,16]{1,0:T(1,128)} %far_hbm.1, s32[1,2]{1,0:T(1,128)} %group_far_hbm.1, bf16[3072,512]{1,0:T(8,128)(2,1)S(1)} %get-tuple-element.26.orbit_ref, bf16[512,512]{1,0:T(8,128)(2,1)S(1)} %get-tuple-element.27.pick_ref), custom_call_target="tpu_custom_call" | custom-call | flops 1610612736 | bytes 4194304 | tf_op jit(solution)/shard_map/prepare/pallas_call | solution.py:476
  12.9 0.0 copy-start.1
  12.9 0.2 collective-permute-done.3
  13.1 2.1 %collective-permute-done.2 = bf16[64,512]{1,0:T(8,128)(2,1)S(1)} collective-permute-done((bf16[64,512]{1,0:T(8,128)(2,1)S(1)}, bf16[64,512]{1,0:T(8,128)(2,1)S(1)}, u32[]{:S(2)}, u32[]{:S(2)}) %collective-permute-start.2) | collective-permute-done | bytes 65568 | tf_op jit(solution)/shard_map/ppermute | solution.py:38
  15.2 0.1 collective-permute-done.1
  15.3 0.1 collective-permute-start.4
  15.4 1.3 %first.1.refs_0_ = f32[3072,128]{1,0:T(8,128)S(1)} custom-call(bf16[3072,512]{1,0:T(8,128)(2,1)S(1)} %get-tuple-element.31.orbit_ref, bf16[256,512]{1,0:T(8,128)(2,1)S(1)} %pad_maximum_fusion.held_ref, bf16[512,512]{1,0:T(8,128)(2,1)S(1)} %get-tuple-element.34.order_ref.pick_ref), custom_call_target="tpu_custom_call" | custom-call | flops 805306368 | bytes 4194304 | tf_op jit(solution)/shard_map/first/pallas_call | solution.py:493
  16.6 0.0 copy-start.3
  16.6 0.2 collective-permute-done.4.other_ref
  16.9 0.0 copy-done.1
  16.9 2.1 %density.1 = (f32[32,128]{1,0:T(8,128)S(1)}, f32[32,2,128]{2,1,0:T(2,128)}) custom-call(s32[3,6]{1,0:T(4,128)S(1)} %copy-done.1, bf16[3072,512]{1,0:T(8,128)(2,1)S(1)} %get-tuple-element.31.orbit_ref, bf16[256,512]{1,0:T(8,128)(2,1)S(1)} %collective-permute-done.4.other_ref, f32[128,3072]{1,0:T(8,128)S(1)} %get-tuple-element.33.weights_ref, ...), custom_call_target="tpu_custom_call" | custom-call | flops 805306368 | bytes 4194304 | tf_op jit(solution)/shard_map/density/pallas_call | solution.py:507
  19.0 4.2 %all-to-all-start = ((f32[32,2,128]{2,1,0:T(2,128)}), f32[32,2,128]{2,1,0:T(2,128)S(1)}, u32[]{:S(2)}, u32[]{:S(2)}) async-start(f32[32,2,128]{2,1,0:T(2,128)} %get-tuple-element.35), calls=%async_computation | async-start | bytes 65536 | tf_op jit(solution)/shard_map/all_to_all | solution.py:524
  23.3 0.7 %collective-permute-start.6 = (f32[32,128]{1,0:T(8,128)S(1)}, f32[32,128]{1,0:T(8,128)S(1)}, u32[]{:S(2)}, u32[]{:S(2)}) collective-permute-start(f32[32,128]{1,0:T(8,128)S(1)} %get-tuple-element.37.halo_ref), channel_id=1, source_target_pairs={{1,2},{2,1},{3,4},{4,3},{5,6},{6,5},{7,8},{8,7},{9,10},{10,9},{11,... | collective-permute-start | bytes 49160 | tf_op jit(solution)/shard_map/ppermute | solution.py:523
  23.9 3.2 %collective-permute-start.5 = (f32[32,128]{1,0:T(8,128)S(1)}, f32[32,128]{1,0:T(8,128)S(1)}, u32[]{:S(2)}, u32[]{:S(2)}) collective-permute-start(f32[32,128]{1,0:T(8,128)S(1)} %get-tuple-element.37.halo_ref), channel_id=1, source_target_pairs={{0,1},{1,0},{2,3},{3,2},{4,5},{5,4},{6,7},{7,6},{8,9},{9,8},{10,11... | collective-permute-start | bytes 49160 | tf_op jit(solution)/shard_map/ppermute | solution.py:38
  27.1 0.0 copy-done.3
  27.1 0.1 copy.12.leaves_ref
  27.2 0.5 %self.1 = (f32[6,512,128]{2,1,0:T(8,128)S(1)}, f32[24,128]{1,0:T(8,128)S(1)}) custom-call(f32[32,128]{1,0:T(8,128)S(1)} %get-tuple-element.37.halo_ref), custom_call_target="tpu_custom_call" | custom-call | flops 20971520 | bytes 4194304 | tf_op jit(solution)/shard_map/self/pallas_call | solution.py:529
  27.7 0.0 collective-permute-done.6.odd_ref
  27.7 0.3 collective-permute-done.5.even_ref
  28.0 0.0 copy-start
  28.0 2.1 %near.1.near_ref = f32[24,128]{1,0:T(8,128)S(1)} custom-call(s32[6,3]{1,0:T(8,128)S(1)} %copy.12.leaves_ref, f32[32,128]{1,0:T(8,128)S(1)} %get-tuple-element.37.halo_ref, f32[32,128]{1,0:T(8,128)S(1)} %collective-permute-done.5.even_ref, f32[32,128]{1,0:T(8,128)S(1)} %collective-permute-done.6.odd_ref, f32[24,128]{1,0:T(8,128)S(1)} %get-tuple-element.38.own_ref, ...), custom_call_target="tpu_custom_call" | custom-call | flops 20971520 | bytes 4194304 | tf_op jit(solution)/shard_map/near/pallas_call | solution.py:538
  30.1 0.4 %all-to-all-done.expansion_ref = f32[32,2,128]{2,1,0:T(2,128)S(1)} async-done(((f32[32,2,128]{2,1,0:T(2,128)}), f32[32,2,128]{2,1,0:T(2,128)S(1)}, u32[]{:S(2)}, u32[]{:S(2)}) %all-to-all-start) | async-done | bytes 32800 | tf_op jit(solution)/shard_map/all_to_all | solution.py:524
  30.5 0.0 copy-done
  30.5 1.3 %potential.1 = (f32[24,128]{1,0:T(8,128)}, f32[24,128]{1,0:T(8,128)}) custom-call(f32[32,2,128]{2,1,0:T(2,128)S(1)} %all-to-all-done.expansion_ref, f32[18,128]{1,0:T(8,128)S(1)} %get-tuple-element.36.mask_ref, f32[128,3072]{1,0:T(8,128)S(1)} %get-tuple-element.33.weights_ref, f32[1,64,64]{2,1,0:T(8,128)S(1)} %copy-done, f32[24,128]{1,0:T(8,128)S(1)} %near.1.near_ref, ...), custom_call_target="tpu_custom_call" | custom-call | flops 4194304 | bytes 4194304 | tf_op jit(solution)/shard_map/potential/pallas_call | solution.py:552
  (2 shorter events, 0.0 us)
Async XLA Ops:
  0.6 5.5 %copy-start.2 = (bf16[32,512]{1,0:T(8,128)(2,1)S(1)}, bf16[32,512]{1,0:T(8,128)(2,1)}, u32[]{:S(2)}) copy-start(bf16[32,512]{1,0:T(8,128)(2,1)} %param.11) | copy-start | bytes 98308
  0.6 5.5 %collective-permute-start = (bf16[32,512]{1,0:T(8,128)(2,1)}, bf16[32,512]{1,0:T(8,128)(2,1)S(1)}, u32[]{:S(2)}, u32[]{:S(2)}) collective-permute-start(bf16[32,512]{1,0:T(8,128)(2,1)} %param.11), channel_id=1, source_target_pairs={{0,2},{1,3},{2,0},{3,1},{4,6},{5,7},{6,4},{7,5},{8,10},{9,11},{10,... | collective-permute-start | bytes 98312 | tf_op jit(solution)/shard_map/ppermute | solution.py:38
  6.1 6.9 %collective-permute-start.3 = (bf16[64,512]{1,0:T(8,128)(2,1)S(1)}, bf16[64,512]{1,0:T(8,128)(2,1)S(1)}, u32[]{:S(2)}, u32[]{:S(2)}) collective-permute-start(bf16[64,512]{1,0:T(8,128)(2,1)S(1)} %pad_maximum_fusion.1), channel_id=1, source_target_pairs={{0,12},{1,13},{2,14},{3,15},{4,8},{5,9},{6,10},{7,11},{8,4},{9,5},... | collective-permute-start | bytes 196616 | tf_op jit(solution)/shard_map/ppermute | solution.py:38
  10.0 5.2 %collective-permute-start.2 = (bf16[64,512]{1,0:T(8,128)(2,1)S(1)}, bf16[64,512]{1,0:T(8,128)(2,1)S(1)}, u32[]{:S(2)}, u32[]{:S(2)}) collective-permute-start(bf16[64,512]{1,0:T(8,128)(2,1)S(1)} %pad_maximum_fusion.1), channel_id=1, source_target_pairs={{0,8},{1,9},{2,10},{3,11},{4,12},{5,13},{6,14},{7,15},{8,0},{9,1},... | collective-permute-start | bytes 196616 | tf_op jit(solution)/shard_map/ppermute | solution.py:38
  10.0 5.3 %collective-permute-start.1 = (bf16[64,512]{1,0:T(8,128)(2,1)S(1)}, bf16[64,512]{1,0:T(8,128)(2,1)S(1)}, u32[]{:S(2)}, u32[]{:S(2)}) collective-permute-start(bf16[64,512]{1,0:T(8,128)(2,1)S(1)} %pad_maximum_fusion.1), channel_id=1, source_target_pairs={{0,4},{1,5},{2,6},{3,7},{4,0},{5,1},{6,2},{7,3},{8,12},{9,13},{10,... | collective-permute-start | bytes 196616 | tf_op jit(solution)/shard_map/ppermute | solution.py:38
  12.9 4.0 %copy-start.1 = (s32[3,6]{1,0:T(4,128)S(1)}, s32[3,6]{1,0:T(4,128)}, u32[]{:S(2)}) copy-start(s32[3,6]{1,0:T(4,128)} %coords_ref.1) | copy-start | bytes 220
  15.3 1.6 %collective-permute-start.4 = (bf16[256,512]{1,0:T(8,128)(2,1)S(1)}, bf16[256,512]{1,0:T(8,128)(2,1)S(1)}, u32[]{:S(2)}, u32[]{:S(2)}) collective-permute-start(bf16[256,512]{1,0:T(8,128)(2,1)S(1)} %pad_maximum_fusion.held_ref), channel_id=1, source_target_pairs={{0,1},{1,0},{2,3},{3,2},{4,5},{5,4},{6,7},{7,6},{8,9},{9,8},{10,11... | collective-permute-start | bytes 786440 | tf_op jit(solution)/shard_map/ppermute | solution.py:38
  16.6 10.5 %copy-start.3 = (s32[6,3]{0,1:T(4,128)S(1)}, s32[6,3]{0,1:T(4,128)}, u32[]{:S(2)}) copy-start(s32[6,3]{0,1:T(4,128)} %param.14) | copy-start | bytes 220
  19.0 11.5 %all-to-all-start = ((f32[32,2,128]{2,1,0:T(2,128)}), f32[32,2,128]{2,1,0:T(2,128)S(1)}, u32[]{:S(2)}, u32[]{:S(2)}) async-start(f32[32,2,128]{2,1,0:T(2,128)} %get-tuple-element.35), calls=%async_computation | async-start | bytes 65536 | tf_op jit(solution)/shard_map/all_to_all | solution.py:524
  23.3 4.4 %collective-permute-start.6 = (f32[32,128]{1,0:T(8,128)S(1)}, f32[32,128]{1,0:T(8,128)S(1)}, u32[]{:S(2)}, u32[]{:S(2)}) collective-permute-start(f32[32,128]{1,0:T(8,128)S(1)} %get-tuple-element.37.halo_ref), channel_id=1, source_target_pairs={{1,2},{2,1},{3,4},{4,3},{5,6},{6,5},{7,8},{8,7},{9,10},{10,9},{11,... | collective-permute-start | bytes 49160 | tf_op jit(solution)/shard_map/ppermute | solution.py:523
  23.9 4.0 %collective-permute-start.5 = (f32[32,128]{1,0:T(8,128)S(1)}, f32[32,128]{1,0:T(8,128)S(1)}, u32[]{:S(2)}, u32[]{:S(2)}) collective-permute-start(f32[32,128]{1,0:T(8,128)S(1)} %get-tuple-element.37.halo_ref), channel_id=1, source_target_pairs={{0,1},{1,0},{2,3},{3,2},{4,5},{5,4},{6,7},{7,6},{8,9},{9,8},{10,11... | collective-permute-start | bytes 49160 | tf_op jit(solution)/shard_map/ppermute | solution.py:38
  28.0 2.5 %copy-start = (f32[1,64,64]{2,1,0:T(8,128)S(1)}, f32[1,64,64]{2,1,0:T(8,128)}, u32[]{:S(2)}) copy-start(f32[1,64,64]{2,1,0:T(8,128)} %dev_ref.1) | copy-start | bytes 49156

commit v6 on v5

--- a/solution.py
+++ b/solution.py
@@ -17,7 +17,7 @@
 NEARL = 3
 LANES = 128
 LEAF_ROWS = LEAF // LANES
-TILE = 256
+TILE = 512
 HIGHEST = lax.Precision.HIGHEST
 
 vol_weight = 0.1
@@ -364,8 +364,7 @@
     dom_count = lax.axis_size("dom")
     group_count = mask_ref.shape[0] - dom_count
     group, me = lax.axis_index("group"), lax.axis_index("dom")
-    sent = expansion_ref[...]
-    moments, bounds = sent[:, 0, :], sent[:, 1, :]
+    moments, bounds = expansion_ref[:, 0, :], expansion_ref[:, 1, :]
     lane = iota((1, LANES), 1)
     unit_row = pattern(lane % RANK)
     unit_column = pattern(iota((RANK, LANES), 0))
@@ -387,13 +386,15 @@
     group_local = vol_weight * lane_sums(total)
     local = jnp.sum(dev_ref[0] * group_local, axis=1, keepdims=True)
     base = group * dom_count
-    own = expansion_ref[pl.ds(base, dom_count)]
-    own_bounds = expansion_ref[pl.ds(base + me, 1)][:, 1, :]
+    at = pl.ds(base, dom_count)
+    own_bounds = expansion_ref[pl.ds(base + me, 1), 1, :]
     target = nodes(own_bounds, unit_column)
-    source = nodes(own[:, 1, :], unit_row)
-    own_moments = jnp.where(lane < RANK, own[:, 0, :], 0.0) * mask_ref[:dom_count, :]
+    low, half = lane < RANK, dom_count // 2
+    source = [jnp.where(low, x[:half], x[half:]) for x in nodes(expansion_ref[at, 1, :], unit_row)]
+    own_moments = expansion_ref[at, 0, :] * mask_ref[:dom_count, :]
+    own_moments = jnp.where(low, own_moments[:half], pltpu.roll(own_moments[half:], RANK, 1))
     total = jnp.zeros((RANK, LANES), jnp.float32)
-    for s in range(dom_count):
+    for s in range(half):
         coupling = node_coupling(target, [x[s : s + 1] for x in source])
         total = total + coupling * own_moments[s : s + 1]
     local = local + vol_weight * jnp.sum(total, axis=1, keepdims=True)
@@ -538,7 +539,7 @@
     near = pl.pallas_call(
         near_kernel,
         out_shape=table,
-        in_specs=[SMEM] + [VMEM] * 5,
+        in_specs=[VMEM] * 6,
         out_specs=VMEM,
         scratch_shapes=[
             pltpu.VMEM((3 * rows, LANES), f32),

time: 32.1 us -> 32 us (level)
  Pallas kernels: 12 us -> 11.4 us
  waiting for transfers between devices: 3.27 us -> 3.85 us
    all_to_all x1, waiting for transfers between devices: 0.42 us -> 0.98 us  [local(): everyone = lax.all_to_all(expansion, ('group', 'dom'), 0, 0)]
    pallas_call x1, Pallas kernels: 2.12 us -> 1.56 us  [local(): pl.pallas_call(near_kernel, out_shape=table, in_specs=[VMEM] * 6, out_spe...]
  transfers between devices with their start and end apart: 8 -> 8, of which waited for: 6 -> 6; matrix products, arithmetic and copies ran while one was open for 0% -> 0% of each run, Pallas kernels for 27% -> 25%
where the time goes in v6:
time: 32 us; the launch traced here: 31.8 us
  starting transfers between devices  15.7 us (49%)
  Pallas kernels  11.4 us (36%)
  waiting for transfers between devices  3.85 us (12%)
  between operations  0.75 us (2%)
    ppermute x6, starting transfers between devices, swap(): lax.ppermute(value, axis, [(i, i ^ mask) for i in range(lax.axis_size(axi...  10.8 us
    all_to_all x1, starting transfers between devices, local(): everyone = lax.all_to_all(expansion, ('group', 'dom'), 0, 0)  4.24 us
    ppermute x6, waiting for transfers between devices, swap(): lax.ppermute(value, axis, [(i, i ^ mask) for i in range(lax.axis_size(axi...  2.86 us
    pallas_call x1, Pallas kernels, load(): pl.pallas_call(functools.partial(load_kernel, reorder), out_shape=(jax.Sh...  2.41 us
    pallas_call x1, Pallas kernels, prepare(): pl.pallas_call(functools.partial(prepare_kernel, reorder), out_shape=shap...  2.29 us
    pallas_call x1, Pallas kernels, local(): pl.pallas_call(functools.partial(density_kernel, reorder), out_shape=(jax...  2.13 us
    pallas_call x1, Pallas kernels, local(): pl.pallas_call(near_kernel, out_shape=table, in_specs=[VMEM] * 6, out_spe...  1.56 us
    pallas_call x1, Pallas kernels, local(): pl.pallas_call(potential_kernel, out_shape=(table, table), in_specs=[VMEM...  1.27 us
  transfers between devices with their start and end apart: 8, of which 6 were waited for; matrix products, arithmetic and copies ran while one was open for 0% of the time, Pallas kernels for 25%

profile of v6, /device:TPU:0, one launch (start us, length us, event | category | flops | bytes accessed | tf_op | source)
XLA Modules:
  0.0 31.8 jit_solution(7433902128921913786)
XLA Ops:
  0.6 0.0 copy-start.2
  0.6 3.0 %collective-permute-start = (bf16[32,512]{1,0:T(8,128)(2,1)}, bf16[32,512]{1,0:T(8,128)(2,1)S(1)}, u32[]{:S(2)}, u32[]{:S(2)}) collective-permute-start(bf16[32,512]{1,0:T(8,128)(2,1)} %param.11), channel_id=1, source_target_pairs={{0,2},{1,3},{2,0},{3,1},{4,6},{5,7},{6,4},{7,5},{8,10},{9,11},{10,... | collective-permute-start | bytes 98312 | tf_op jit(solution)/shard_map/ppermute | solution.py:38
  3.7 2.4 %load.1 = (bf16[3072,512]{1,0:T(8,128)(2,1)S(1)}, bf16[512,512]{1,0:T(8,128)(2,1)S(1)}, f32[128,3072]{1,0:T(8,128)S(1)}) custom-call(s32[1,32]{1,0:T(1,128)} %near_hbm.1, f32[6,64,64]{2,1,0:T(8,128)} %transfer_hbm.1, f32[1,64,64]{2,1,0:T(8,128)} %dev_ref.1, f32[64,3072]{1,0:T(8,128)} %basis_hbm.1, bf16[3072,512]{1,0:T(8,128)(2,1)} %orbitals_hbm.1), custom_call_target="tpu_custom_call" | custom-call | flops 1048576 | bytes 4194304 | tf_op jit(solution)/shard_map/load/pallas_call | solution.py:454
  6.1 0.0 collective-permute-done
  6.1 0.0 copy-done.2
  6.1 3.8 %collective-permute-start.3 = (bf16[64,512]{1,0:T(8,128)(2,1)S(1)}, bf16[64,512]{1,0:T(8,128)(2,1)S(1)}, u32[]{:S(2)}, u32[]{:S(2)}) collective-permute-start(bf16[64,512]{1,0:T(8,128)(2,1)S(1)} %pad_maximum_fusion.1), channel_id=1, source_target_pairs={{0,12},{1,13},{2,14},{3,15},{4,8},{5,9},{6,10},{7,11},{8,4},{9,5},... | collective-permute-start | bytes 196616 | tf_op jit(solution)/shard_map/ppermute | solution.py:38
  10.0 0.0 collective-permute-start.2
  10.0 0.6 %collective-permute-start.1 = (bf16[64,512]{1,0:T(8,128)(2,1)S(1)}, bf16[64,512]{1,0:T(8,128)(2,1)S(1)}, u32[]{:S(2)}, u32[]{:S(2)}) collective-permute-start(bf16[64,512]{1,0:T(8,128)(2,1)S(1)} %pad_maximum_fusion.1), channel_id=1, source_target_pairs={{0,4},{1,5},{2,6},{3,7},{4,0},{5,1},{6,2},{7,3},{8,12},{9,13},{10,... | collective-permute-start | bytes 196616 | tf_op jit(solution)/shard_map/ppermute | solution.py:38
  10.6 2.3 %prepare.1 = (f32[18,128]{1,0:T(8,128)S(1)}, bf16[3072,512]{1,0:T(8,128)(2,1)S(1)}, bf16[512,512]{1,0:T(8,128)(2,1)S(1)}) custom-call(s32[1,16]{1,0:T(1,128)} %far_hbm.1, s32[1,2]{1,0:T(1,128)} %group_far_hbm.1, bf16[3072,512]{1,0:T(8,128)(2,1)S(1)} %get-tuple-element.26.orbit_ref, bf16[512,512]{1,0:T(8,128)(2,1)S(1)} %get-tuple-element.27.pick_ref), custom_call_target="tpu_custom_call" | custom-call | flops 1610612736 | bytes 4194304 | tf_op jit(solution)/shard_map/prepare/pallas_call | solution.py:477
  12.9 0.0 copy-start.1
  12.9 0.2 collective-permute-done.3
  13.1 2.1 %collective-permute-done.2 = bf16[64,512]{1,0:T(8,128)(2,1)S(1)} collective-permute-done((bf16[64,512]{1,0:T(8,128)(2,1)S(1)}, bf16[64,512]{1,0:T(8,128)(2,1)S(1)}, u32[]{:S(2)}, u32[]{:S(2)}) %collective-permute-start.2) | collective-permute-done | bytes 65568 | tf_op jit(solution)/shard_map/ppermute | solution.py:38
  15.2 0.1 collective-permute-done.1
  15.3 0.1 collective-permute-start.4
  15.4 1.3 %first.1.refs_0_ = f32[3072,128]{1,0:T(8,128)S(1)} custom-call(bf16[3072,512]{1,0:T(8,128)(2,1)S(1)} %get-tuple-element.31.orbit_ref, bf16[256,512]{1,0:T(8,128)(2,1)S(1)} %pad_maximum_fusion.held_ref, bf16[512,512]{1,0:T(8,128)(2,1)S(1)} %get-tuple-element.34.order_ref.pick_ref), custom_call_target="tpu_custom_call" | custom-call | flops 805306368 | bytes 4194304 | tf_op jit(solution)/shard_map/first/pallas_call | solution.py:494
  16.6 0.0 copy-start.3
  16.6 0.2 collective-permute-done.4.other_ref
  16.9 0.0 copy-done.1
  16.9 2.1 %density.1 = (f32[32,128]{1,0:T(8,128)S(1)}, f32[32,2,128]{2,1,0:T(2,128)}) custom-call(s32[3,6]{1,0:T(4,128)S(1)} %copy-done.1, bf16[3072,512]{1,0:T(8,128)(2,1)S(1)} %get-tuple-element.31.orbit_ref, bf16[256,512]{1,0:T(8,128)(2,1)S(1)} %collective-permute-done.4.other_ref, f32[128,3072]{1,0:T(8,128)S(1)} %get-tuple-element.33.weights_ref, ...), custom_call_target="tpu_custom_call" | custom-call | flops 805306368 | bytes 4194304 | tf_op jit(solution)/shard_map/density/pallas_call | solution.py:508
  19.0 4.2 %all-to-all-start = ((f32[32,2,128]{2,1,0:T(2,128)}), f32[32,2,128]{2,1,0:T(2,128)S(1)}, u32[]{:S(2)}, u32[]{:S(2)}) async-start(f32[32,2,128]{2,1,0:T(2,128)} %get-tuple-element.35), calls=%async_computation | async-start | bytes 65536 | tf_op jit(solution)/shard_map/all_to_all | solution.py:525
  23.3 0.7 %collective-permute-start.6 = (f32[32,128]{1,0:T(8,128)S(1)}, f32[32,128]{1,0:T(8,128)S(1)}, u32[]{:S(2)}, u32[]{:S(2)}) collective-permute-start(f32[32,128]{1,0:T(8,128)S(1)} %get-tuple-element.37.halo_ref), channel_id=1, source_target_pairs={{1,2},{2,1},{3,4},{4,3},{5,6},{6,5},{7,8},{8,7},{9,10},{10,9},{11,... | collective-permute-start | bytes 49160 | tf_op jit(solution)/shard_map/ppermute | solution.py:524
  23.9 3.2 %collective-permute-start.5 = (f32[32,128]{1,0:T(8,128)S(1)}, f32[32,128]{1,0:T(8,128)S(1)}, u32[]{:S(2)}, u32[]{:S(2)}) collective-permute-start(f32[32,128]{1,0:T(8,128)S(1)} %get-tuple-element.37.halo_ref), channel_id=1, source_target_pairs={{0,1},{1,0},{2,3},{3,2},{4,5},{5,4},{6,7},{7,6},{8,9},{9,8},{10,11... | collective-permute-start | bytes 49160 | tf_op jit(solution)/shard_map/ppermute | solution.py:38
  27.1 0.0 copy-done.3
  27.1 0.1 copy.12.leaves_ref
  27.2 0.5 %self.1 = (f32[6,512,128]{2,1,0:T(8,128)S(1)}, f32[24,128]{1,0:T(8,128)S(1)}) custom-call(f32[32,128]{1,0:T(8,128)S(1)} %get-tuple-element.37.halo_ref), custom_call_target="tpu_custom_call" | custom-call | flops 20971520 | bytes 4194304 | tf_op jit(solution)/shard_map/self/pallas_call | solution.py:530
  27.7 0.0 collective-permute-done.6.odd_ref
  27.7 0.3 collective-permute-done.5.even_ref
  28.0 0.0 copy-start
  28.0 1.6 %near.1.near_ref = f32[24,128]{1,0:T(8,128)S(1)} custom-call(s32[6,3]{1,0:T(8,128)S(1)} %copy.12.leaves_ref, f32[32,128]{1,0:T(8,128)S(1)} %get-tuple-element.37.halo_ref, f32[32,128]{1,0:T(8,128)S(1)} %collective-permute-done.5.even_ref, f32[32,128]{1,0:T(8,128)S(1)} %collective-permute-done.6.odd_ref, f32[24,128]{1,0:T(8,128)S(1)} %get-tuple-element.38.own_ref, ...), custom_call_target="tpu_custom_call" | custom-call | flops 20971520 | bytes 4194304 | tf_op jit(solution)/shard_map/near/pallas_call | solution.py:539
  29.5 1.0 %all-to-all-done.expansion_ref = f32[32,2,128]{2,1,0:T(2,128)S(1)} async-done(((f32[32,2,128]{2,1,0:T(2,128)}), f32[32,2,128]{2,1,0:T(2,128)S(1)}, u32[]{:S(2)}, u32[]{:S(2)}) %all-to-all-start) | async-done | bytes 32800 | tf_op jit(solution)/shard_map/all_to_all | solution.py:525
  30.5 0.0 copy-done
  30.5 1.3 %potential.1 = (f32[24,128]{1,0:T(8,128)}, f32[24,128]{1,0:T(8,128)}) custom-call(f32[32,2,128]{2,1,0:T(2,128)S(1)} %all-to-all-done.expansion_ref, f32[18,128]{1,0:T(8,128)S(1)} %get-tuple-element.36.mask_ref, f32[128,3072]{1,0:T(8,128)S(1)} %get-tuple-element.33.weights_ref, f32[1,64,64]{2,1,0:T(8,128)S(1)} %copy-done, f32[24,128]{1,0:T(8,128)S(1)} %near.1.near_ref, ...), custom_call_target="tpu_custom_call" | custom-call | flops 4194304 | bytes 4194304 | tf_op jit(solution)/shard_map/potential/pallas_call | solution.py:553
  (2 shorter events, 0.0 us)
Async XLA Ops:
  0.6 5.5 %copy-start.2 = (bf16[32,512]{1,0:T(8,128)(2,1)S(1)}, bf16[32,512]{1,0:T(8,128)(2,1)}, u32[]{:S(2)}) copy-start(bf16[32,512]{1,0:T(8,128)(2,1)} %param.11) | copy-start | bytes 98308
  0.6 5.5 %collective-permute-start = (bf16[32,512]{1,0:T(8,128)(2,1)}, bf16[32,512]{1,0:T(8,128)(2,1)S(1)}, u32[]{:S(2)}, u32[]{:S(2)}) collective-permute-start(bf16[32,512]{1,0:T(8,128)(2,1)} %param.11), channel_id=1, source_target_pairs={{0,2},{1,3},{2,0},{3,1},{4,6},{5,7},{6,4},{7,5},{8,10},{9,11},{10,... | collective-permute-start | bytes 98312 | tf_op jit(solution)/shard_map/ppermute | solution.py:38
  6.1 6.9 %collective-permute-start.3 = (bf16[64,512]{1,0:T(8,128)(2,1)S(1)}, bf16[64,512]{1,0:T(8,128)(2,1)S(1)}, u32[]{:S(2)}, u32[]{:S(2)}) collective-permute-start(bf16[64,512]{1,0:T(8,128)(2,1)S(1)} %pad_maximum_fusion.1), channel_id=1, source_target_pairs={{0,12},{1,13},{2,14},{3,15},{4,8},{5,9},{6,10},{7,11},{8,4},{9,5},... | collective-permute-start | bytes 196616 | tf_op jit(solution)/shard_map/ppermute | solution.py:38
  10.0 5.2 %collective-permute-start.2 = (bf16[64,512]{1,0:T(8,128)(2,1)S(1)}, bf16[64,512]{1,0:T(8,128)(2,1)S(1)}, u32[]{:S(2)}, u32[]{:S(2)}) collective-permute-start(bf16[64,512]{1,0:T(8,128)(2,1)S(1)} %pad_maximum_fusion.1), channel_id=1, source_target_pairs={{0,8},{1,9},{2,10},{3,11},{4,12},{5,13},{6,14},{7,15},{8,0},{9,1},... | collective-permute-start | bytes 196616 | tf_op jit(solution)/shard_map/ppermute | solution.py:38
  10.0 5.3 %collective-permute-start.1 = (bf16[64,512]{1,0:T(8,128)(2,1)S(1)}, bf16[64,512]{1,0:T(8,128)(2,1)S(1)}, u32[]{:S(2)}, u32[]{:S(2)}) collective-permute-start(bf16[64,512]{1,0:T(8,128)(2,1)S(1)} %pad_maximum_fusion.1), channel_id=1, source_target_pairs={{0,4},{1,5},{2,6},{3,7},{4,0},{5,1},{6,2},{7,3},{8,12},{9,13},{10,... | collective-permute-start | bytes 196616 | tf_op jit(solution)/shard_map/ppermute | solution.py:38
  12.9 4.0 %copy-start.1 = (s32[3,6]{1,0:T(4,128)S(1)}, s32[3,6]{1,0:T(4,128)}, u32[]{:S(2)}) copy-start(s32[3,6]{1,0:T(4,128)} %coords_ref.1) | copy-start | bytes 220
  15.3 1.6 %collective-permute-start.4 = (bf16[256,512]{1,0:T(8,128)(2,1)S(1)}, bf16[256,512]{1,0:T(8,128)(2,1)S(1)}, u32[]{:S(2)}, u32[]{:S(2)}) collective-permute-start(bf16[256,512]{1,0:T(8,128)(2,1)S(1)} %pad_maximum_fusion.held_ref), channel_id=1, source_target_pairs={{0,1},{1,0},{2,3},{3,2},{4,5},{5,4},{6,7},{7,6},{8,9},{9,8},{10,11... | collective-permute-start | bytes 786440 | tf_op jit(solution)/shard_map/ppermute | solution.py:38
  16.6 10.5 %copy-start.3 = (s32[6,3]{0,1:T(4,128)S(1)}, s32[6,3]{0,1:T(4,128)}, u32[]{:S(2)}) copy-start(s32[6,3]{0,1:T(4,128)} %param.14) | copy-start | bytes 220
  19.0 11.5 %all-to-all-start = ((f32[32,2,128]{2,1,0:T(2,128)}), f32[32,2,128]{2,1,0:T(2,128)S(1)}, u32[]{:S(2)}, u32[]{:S(2)}) async-start(f32[32,2,128]{2,1,0:T(2,128)} %get-tuple-element.35), calls=%async_computation | async-start | bytes 65536 | tf_op jit(solution)/shard_map/all_to_all | solution.py:525
  23.3 4.4 %collective-permute-start.6 = (f32[32,128]{1,0:T(8,128)S(1)}, f32[32,128]{1,0:T(8,128)S(1)}, u32[]{:S(2)}, u32[]{:S(2)}) collective-permute-start(f32[32,128]{1,0:T(8,128)S(1)} %get-tuple-element.37.halo_ref), channel_id=1, source_target_pairs={{1,2},{2,1},{3,4},{4,3},{5,6},{6,5},{7,8},{8,7},{9,10},{10,9},{11,... | collective-permute-start | bytes 49160 | tf_op jit(solution)/shard_map/ppermute | solution.py:524
  23.9 4.0 %collective-permute-start.5 = (f32[32,128]{1,0:T(8,128)S(1)}, f32[32,128]{1,0:T(8,128)S(1)}, u32[]{:S(2)}, u32[]{:S(2)}) collective-permute-start(f32[32,128]{1,0:T(8,128)S(1)} %get-tuple-element.37.halo_ref), channel_id=1, source_target_pairs={{0,1},{1,0},{2,3},{3,2},{4,5},{5,4},{6,7},{7,6},{8,9},{9,8},{10,11... | collective-permute-start | bytes 49160 | tf_op jit(solution)/shard_map/ppermute | solution.py:38
  28.0 2.5 %copy-start = (f32[1,64,64]{2,1,0:T(8,128)S(1)}, f32[1,64,64]{2,1,0:T(8,128)}, u32[]{:S(2)}) copy-start(f32[1,64,64]{2,1,0:T(8,128)} %dev_ref.1) | copy-start | bytes 49156

commit v7 on v6

--- a/solution.py
+++ b/solution.py
@@ -24,32 +24,31 @@
 soft_square = 1.0
 
 
-def xor_stages(count):
-    bits = count.bit_length() - 1
-    stages, bit = ([(2,)], 2) if bits > 1 else ([], 1)
-    while bit < bits:
-        wide = 2 if bit + 1 < bits else 1
-        stages.append(tuple(m << bit for m in range(1, 1 << wide)))
-        bit += wide
-    return stages
-
-
 def swap(value, axis, mask):
     return lax.ppermute(value, axis, [(i, i ^ mask) for i in range(lax.axis_size(axis))])
 
 
-def farthest_first(mask):
-    return -(mask & -mask), -mask
+def piece_of(apart):
+    pair = jnp.bitwise_and(lax.shift_right_logical(apart, 1), 3)
+    place = jnp.where(pair == 0, 0, jnp.where(pair == 3, 1, pair + 1))
+    return apart + 2 * (place - pair)
 
 
 def gather_rows(rows, load, prepare):
-    held, loaded = rows, load()
-    for stage, masks in enumerate(xor_stages(lax.axis_size("dom"))):
-        if stage == 1:
-            held, loaded = lax.optimization_barrier((held, loaded))
-            result = prepare(loaded)
-        arrived = {m: swap(held, "dom", m) for m in sorted(masks, key=farthest_first)}
-        held = jnp.concatenate([held] + [arrived[m] for m in masks], axis=0)
+    count = lax.axis_size("dom")
+    beside, middle = swap(rows, "dom", 2), swap(rows, "dom", 8)
+    own, *loaded = load()
+    beside, loaded = lax.optimization_barrier((beside, loaded))
+    pair = jnp.concatenate([own, beside], axis=0)
+    far, close = swap(pair, "dom", 12), swap(pair, "dom", 4)
+    middle, loaded = lax.optimization_barrier((middle, loaded))
+    other_middle = swap(middle, "dom", 2)
+    result = prepare(loaded)
+    held = jnp.concatenate([pair, far, close, middle, other_middle], axis=0)
+    bit = 16
+    while bit < count:
+        held = jnp.concatenate([held, swap(held, "dom", bit)], axis=0)
+        bit *= 2
     held, result = lax.optimization_barrier((held, result))
     return held, swap(held, "dom", 1), loaded, result
 
@@ -88,6 +87,8 @@
     dev_hbm,
     basis_hbm,
     orbitals_hbm,
+    rows_hbm,
+    own_ref,
     orbit_ref,
     pick_ref,
     weights_ref,
@@ -98,7 +99,7 @@
     sems,
 ):
     moves = ((near_hbm, near_ref), (transfer_hbm, transfer_ref), (dev_hbm, dev_ref))
-    moves += ((basis_hbm, basis_ref), (orbitals_hbm, orbit_ref))
+    moves += ((basis_hbm, basis_ref), (orbitals_hbm, orbit_ref), (rows_hbm, own_ref))
     copies = [pltpu.make_async_copy(a, b, sems.at[i]) for i, (a, b) in enumerate(moves)]
     for copy in copies:
         copy.start()
@@ -132,7 +133,8 @@
             (((0,), (0,)), ((), ())),
             preferred_element_type=jnp.float32,
         )
-    copies[4].wait()
+    for copy in copies[4:]:
+        copy.wait()
 
 
 def prepare_kernel(reorder, far_hbm, group_far_hbm, orbit_ref, pick_ref, mask_ref, *refs):
@@ -166,7 +168,7 @@
 def half_matrix(pieces_ref, order_ref, rows_ref):
     chip = lax.shift_right_logical(lax.axis_index("dom"), 1)
     for c in range(pieces_ref.shape[0] // BLOCK_ROWS):
-        first = jnp.bitwise_xor(chip, c) * BLOCK_ROWS
+        first = piece_of(jnp.bitwise_xor(chip, c)) * BLOCK_ROWS
         at = pl.ds(pl.multiple_of(first, BLOCK_ROWS), BLOCK_ROWS)
         rows_ref[c * BLOCK_ROWS : (c + 1) * BLOCK_ROWS, :] = pieces_ref[at, :]
     matrix = jnp.dot(rows_ref[...], order_ref[...], preferred_element_type=jnp.float32)
@@ -206,7 +208,8 @@
         for k in range(near_ref.shape[1]):
             block = near_ref[0, k]
             apart = jnp.bitwise_xor(lax.shift_right_logical(block, 1), me)
-            first = lax.shift_right_logical(apart, 1) * BLOCK_ROWS + jnp.bitwise_and(block, 1) * BW
+            piece = piece_of(lax.shift_right_logical(apart, 1))
+            first = piece * BLOCK_ROWS + jnp.bitwise_and(block, 1) * BW
             at = pl.ds(pl.multiple_of(first, BW), BW)
             mine = jnp.bitwise_and(apart, 1) == 0
             rows_ref[k * BW : (k + 1) * BW, :] = jnp.where(mine, held_ref[at, :], other_ref[at, :])
@@ -454,18 +457,19 @@
         return pl.pallas_call(
             functools.partial(load_kernel, reorder),
             out_shape=(
+                jax.ShapeDtypeStruct(density_rows.shape, jnp.bfloat16),
                 jax.ShapeDtypeStruct((points, width), jnp.bfloat16),
                 jax.ShapeDtypeStruct((natural, width), jnp.bfloat16),
                 jax.ShapeDtypeStruct((2 * RANK, points), f32),
             ),
-            in_specs=[HBM] * 5,
-            out_specs=(VMEM, VMEM, VMEM),
+            in_specs=[HBM] * 6,
+            out_specs=(VMEM,) * 4,
             scratch_shapes=[pltpu.VMEM(x.shape, x.dtype) for x in operands]
-            + [pltpu.SemaphoreType.DMA((5,))],
+            + [pltpu.SemaphoreType.DMA((6,))],
             compiler_params=params,
             cost_estimate=cost(1 << 20),
             name="load",
-        )(*[in_hbm(x) for x in operands], in_hbm(orbitals))
+        )(*[in_hbm(x) for x in operands], in_hbm(orbitals), in_hbm(density_rows))
 
     def prepare(loaded):
         orbit, pick, _ = loaded

time: 32 us -> 31.3 us (0.978)
  starting transfers between devices: 15.7 us -> 13 us
  waiting for transfers between devices: 3.85 us -> 5.74 us
    all_to_all x1, waiting for transfers between devices: 0.98 us -> 4.11 us  [local(): everyone = lax.all_to_all(expansion, ('group', 'dom'), 0, 0)]
    ppermute x6 -> x7, starting transfers between devices: 10.8 us -> 8.68 us  [swap(): lax.ppermute(value, axis, [(i, i ^ mask) for i in range(lax.axis_size(axi...]
    ppermute x6 -> x7, waiting for transfers between devices: 2.86 us -> 1.63 us  [swap(): lax.ppermute(value, axis, [(i, i ^ mask) for i in range(lax.axis_size(axi...]
    all_to_all x1, starting transfers between devices: 4.24 us -> 3.71 us  [local(): everyone = lax.all_to_all(expansion, ('group', 'dom'), 0, 0)]
  transfers between devices with their start and end apart: 8 -> 9, of which waited for: 6 -> 4; matrix products, arithmetic and copies ran while one was open for 0% -> 0% of each run, Pallas kernels for 25% -> 26%
where the time goes in v7:
time: 31.3 us; the launch traced here: 31.1 us
  starting transfers between devices  13 us (42%)
  Pallas kernels  11.4 us (36%)
  waiting for transfers between devices  5.74 us (18%)
  between operations  0.78 us (2%)
    ppermute x7, starting transfers between devices, swap(): lax.ppermute(value, axis, [(i, i ^ mask) for i in range(lax.axis_size(axi...  8.68 us
    all_to_all x1, waiting for transfers between devices, local(): everyone = lax.all_to_all(expansion, ('group', 'dom'), 0, 0)  4.11 us
    all_to_all x1, starting transfers between devices, local(): everyone = lax.all_to_all(expansion, ('group', 'dom'), 0, 0)  3.71 us
    pallas_call x1, Pallas kernels, load(): pl.pallas_call(functools.partial(load_kernel, reorder), out_shape=(jax.Sh...  2.42 us
    pallas_call x1, Pallas kernels, prepare(): pl.pallas_call(functools.partial(prepare_kernel, reorder), out_shape=shap...  2.3 us
    pallas_call x1, Pallas kernels, local(): pl.pallas_call(functools.partial(density_kernel, reorder), out_shape=(jax...  2.14 us
    ppermute x7, waiting for transfers between devices, swap(): lax.ppermute(value, axis, [(i, i ^ mask) for i in range(lax.axis_size(axi...  1.63 us
    pallas_call x1, Pallas kernels, local(): pl.pallas_call(near_kernel, out_shape=table, in_specs=[VMEM] * 6, out_spe...  1.56 us
  transfers between devices with their start and end apart: 9, of which 4 were waited for; matrix products, arithmetic and copies ran while one was open for 0% of the time, Pallas kernels for 26%

profile of v7, /device:TPU:0, one launch (start us, length us, event | category | flops | bytes accessed | tf_op | source)
XLA Modules:
  0.0 31.1 jit_solution(5577002524809009159)
XLA Ops:
  0.6 3.0 %collective-permute-start = (bf16[32,512]{1,0:T(8,128)(2,1)}, bf16[32,512]{1,0:T(8,128)(2,1)S(1)}, u32[]{:S(2)}, u32[]{:S(2)}) collective-permute-start(bf16[32,512]{1,0:T(8,128)(2,1)} %rows_hbm.1), channel_id=1, source_target_pairs={{0,2},{1,3},{2,0},{3,1},{4,6},{5,7},{6,4},{7,5},{8,10},{9,11},{10,... | collective-permute-start | bytes 98312 | tf_op jit(solution)/shard_map/ppermute | solution.py:28
  3.7 2.6 %collective-permute-start.3 = (bf16[32,512]{1,0:T(8,128)(2,1)}, bf16[32,512]{1,0:T(8,128)(2,1)S(1)}, u32[]{:S(2)}, u32[]{:S(2)}) collective-permute-start(bf16[32,512]{1,0:T(8,128)(2,1)} %rows_hbm.1), channel_id=1, source_target_pairs={{0,8},{1,9},{2,10},{3,11},{4,12},{5,13},{6,14},{7,15},{8,0},{9,1},... | collective-permute-start | bytes 98312 | tf_op jit(solution)/shard_map/ppermute | solution.py:28
  6.3 2.4 %load.1 = (bf16[32,512]{1,0:T(8,128)(2,1)S(1)}, bf16[3072,512]{1,0:T(8,128)(2,1)S(1)}, bf16[512,512]{1,0:T(8,128)(2,1)S(1)}, f32[128,3072]{1,0:T(8,128)S(1)}) custom-call(s32[1,32]{1,0:T(1,128)} %near_hbm.1, f32[6,64,64]{2,1,0:T(8,128)} %transfer_hbm.1, f32[1,64,64]{2,1,0:T(8,128)} %dev_ref.1, f32[64,3072]{1,0:T(8,128)} %basis_hbm.1, ...), custom_call_target="tpu_custom_call" | custom-call | flops 1048576 | bytes 4194304 | tf_op jit(solution)/shard_map/load/pallas_call | solution.py:457
  8.7 0.0 collective-permute-done
  8.7 1.4 %collective-permute-start.1 = (bf16[64,512]{1,0:T(8,128)(2,1)S(1)}, bf16[64,512]{1,0:T(8,128)(2,1)S(1)}, u32[]{:S(2)}, u32[]{:S(2)}) collective-permute-start(bf16[64,512]{1,0:T(8,128)(2,1)S(1)} %get-tuple-element.52), channel_id=1, source_target_pairs={{0,12},{1,13},{2,14},{3,15},{4,8},{5,9},{6,10},{7,11},{8,4},{9,5},... | collective-permute-start | bytes 196616 | tf_op jit(solution)/shard_map/ppermute | solution.py:28
  10.1 0.3 collective-permute-start.2
  10.4 0.0 collective-permute-done.3
  10.5 1.0 %collective-permute-start.4 = (bf16[32,512]{1,0:T(8,128)(2,1)S(1)}, bf16[32,512]{1,0:T(8,128)(2,1)S(1)}, u32[]{:S(2)}, u32[]{:S(2)}) collective-permute-start(bf16[32,512]{1,0:T(8,128)(2,1)S(1)} %collective-permute-done.3), channel_id=1, source_target_pairs={{0,2},{1,3},{2,0},{3,1},{4,6},{5,7},{6,4},{7,5},{8,10},{9,11},{10,... | collective-permute-start | bytes 98312 | tf_op jit(solution)/shard_map/ppermute | solution.py:28
  11.4 2.3 %prepare.1 = (f32[18,128]{1,0:T(8,128)S(1)}, bf16[3072,512]{1,0:T(8,128)(2,1)S(1)}, bf16[512,512]{1,0:T(8,128)(2,1)S(1)}) custom-call(s32[1,16]{1,0:T(1,128)} %far_hbm.1, s32[1,2]{1,0:T(1,128)} %group_far_hbm.1, bf16[3072,512]{1,0:T(8,128)(2,1)S(1)} %get-tuple-element.36.orbit_ref, bf16[512,512]{1,0:T(8,128)(2,1)S(1)} %get-tuple-element.37.pick_ref), custom_call_target="tpu_custom_call" | custom-call | flops 1610612736 | bytes 4194304 | tf_op jit(solution)/shard_map/prepare/pallas_call | solution.py:481
  13.7 0.0 copy-start.1
  13.7 1.2 %collective-permute-done.1 = bf16[64,512]{1,0:T(8,128)(2,1)S(1)} collective-permute-done((bf16[64,512]{1,0:T(8,128)(2,1)S(1)}, bf16[64,512]{1,0:T(8,128)(2,1)S(1)}, u32[]{:S(2)}, u32[]{:S(2)}) %collective-permute-start.1) | collective-permute-done | bytes 65568 | tf_op jit(solution)/shard_map/ppermute | solution.py:28
  15.0 0.1 collective-permute-done.2
  15.1 0.0 collective-permute-done.4
  15.1 0.1 collective-permute-start.5
  15.2 1.3 %first.1.refs_0_ = f32[3072,128]{1,0:T(8,128)S(1)} custom-call(bf16[3072,512]{1,0:T(8,128)(2,1)S(1)} %get-tuple-element.41.orbit_ref, bf16[256,512]{1,0:T(8,128)(2,1)S(1)} %constant_dynamic-update-slice_fusion.2.held_ref, bf16[512,512]{1,0:T(8,128)(2,1)S(1)} %get-tuple-element.44.order_ref.pick_ref), custom_call_target="tpu_custom_call" | custom-call | flops 805306368 | bytes 4194304 | tf_op jit(solution)/shard_map/first/pallas_call | solution.py:498
  16.5 0.0 copy-start.2
  16.5 0.2 collective-permute-done.5.other_ref
  16.7 0.0 copy-done.1
  16.7 2.1 %density.1 = (f32[32,128]{1,0:T(8,128)S(1)}, f32[32,2,128]{2,1,0:T(2,128)}) custom-call(s32[3,6]{1,0:T(4,128)S(1)} %copy-done.1, bf16[3072,512]{1,0:T(8,128)(2,1)S(1)} %get-tuple-element.41.orbit_ref, bf16[256,512]{1,0:T(8,128)(2,1)S(1)} %collective-permute-done.5.other_ref, f32[128,3072]{1,0:T(8,128)S(1)} %get-tuple-element.43.weights_ref, ...), custom_call_target="tpu_custom_call" | custom-call | flops 805306368 | bytes 4194304 | tf_op jit(solution)/shard_map/density/pallas_call | solution.py:512
  18.9 3.7 %all-to-all-start = ((f32[32,2,128]{2,1,0:T(2,128)}), f32[32,2,128]{2,1,0:T(2,128)S(1)}, u32[]{:S(2)}, u32[]{:S(2)}) async-start(f32[32,2,128]{2,1,0:T(2,128)} %get-tuple-element.45), calls=%async_computation | async-start | bytes 65536 | tf_op jit(solution)/shard_map/all_to_all | solution.py:529
  22.6 0.3 %collective-permute-start.6 = (f32[32,128]{1,0:T(8,128)S(1)}, f32[32,128]{1,0:T(8,128)S(1)}, u32[]{:S(2)}, u32[]{:S(2)}) collective-permute-start(f32[32,128]{1,0:T(8,128)S(1)} %get-tuple-element.47.halo_ref), channel_id=1, source_target_pairs={{0,1},{1,0},{2,3},{3,2},{4,5},{5,4},{6,7},{7,6},{8,9},{9,8},{10,11... | collective-permute-start | bytes 49160 | tf_op jit(solution)/shard_map/ppermute | solution.py:28
  22.9 0.7 %collective-permute-start.7 = (f32[32,128]{1,0:T(8,128)S(1)}, f32[32,128]{1,0:T(8,128)S(1)}, u32[]{:S(2)}, u32[]{:S(2)}) collective-permute-start(f32[32,128]{1,0:T(8,128)S(1)} %get-tuple-element.47.halo_ref), channel_id=1, source_target_pairs={{1,2},{2,1},{3,4},{4,3},{5,6},{6,5},{7,8},{8,7},{9,10},{10,9},{11,... | collective-permute-start | bytes 49160 | tf_op jit(solution)/shard_map/ppermute | solution.py:528
  23.6 0.0 copy-done.2
  23.6 0.1 copy.12.leaves_ref
  23.7 0.5 %self.1 = (f32[6,512,128]{2,1,0:T(8,128)S(1)}, f32[24,128]{1,0:T(8,128)S(1)}) custom-call(f32[32,128]{1,0:T(8,128)S(1)} %get-tuple-element.47.halo_ref), custom_call_target="tpu_custom_call" | custom-call | flops 20971520 | bytes 4194304 | tf_op jit(solution)/shard_map/self/pallas_call | solution.py:534
  24.1 0.0 collective-permute-done.6.even_ref
  24.2 0.0 collective-permute-done.7.odd_ref
  24.2 0.0 copy-start
  24.2 1.6 %near.1.near_ref = f32[24,128]{1,0:T(8,128)S(1)} custom-call(s32[6,3]{1,0:T(8,128)S(1)} %copy.12.leaves_ref, f32[32,128]{1,0:T(8,128)S(1)} %get-tuple-element.47.halo_ref, f32[32,128]{1,0:T(8,128)S(1)} %collective-permute-done.6.even_ref, f32[32,128]{1,0:T(8,128)S(1)} %collective-permute-done.7.odd_ref, f32[24,128]{1,0:T(8,128)S(1)} %get-tuple-element.48.own_ref, ...), custom_call_target="tpu_custom_call" | custom-call | flops 20971520 | bytes 4194304 | tf_op jit(solution)/shard_map/near/pallas_call | solution.py:543
  25.7 4.1 %all-to-all-done.expansion_ref = f32[32,2,128]{2,1,0:T(2,128)S(1)} async-done(((f32[32,2,128]{2,1,0:T(2,128)}), f32[32,2,128]{2,1,0:T(2,128)S(1)}, u32[]{:S(2)}, u32[]{:S(2)}) %all-to-all-start) | async-done | bytes 32800 | tf_op jit(solution)/shard_map/all_to_all | solution.py:529
  29.9 0.0 copy-done
  29.9 1.3 %potential.1 = (f32[24,128]{1,0:T(8,128)}, f32[24,128]{1,0:T(8,128)}) custom-call(f32[32,2,128]{2,1,0:T(2,128)S(1)} %all-to-all-done.expansion_ref, f32[18,128]{1,0:T(8,128)S(1)} %get-tuple-element.46.mask_ref, f32[128,3072]{1,0:T(8,128)S(1)} %get-tuple-element.43.weights_ref, f32[1,64,64]{2,1,0:T(8,128)S(1)} %copy-done, f32[24,128]{1,0:T(8,128)S(1)} %near.1.near_ref, ...), custom_call_target="tpu_custom_call" | custom-call | flops 4194304 | bytes 4194304 | tf_op jit(solution)/shard_map/potential/pallas_call | solution.py:557
  (6 shorter events, 0.0 us)
Async XLA Ops:
  0.6 8.1 %collective-permute-start = (bf16[32,512]{1,0:T(8,128)(2,1)}, bf16[32,512]{1,0:T(8,128)(2,1)S(1)}, u32[]{:S(2)}, u32[]{:S(2)}) collective-permute-start(bf16[32,512]{1,0:T(8,128)(2,1)} %rows_hbm.1), channel_id=1, source_target_pairs={{0,2},{1,3},{2,0},{3,1},{4,6},{5,7},{6,4},{7,5},{8,10},{9,11},{10,... | collective-permute-start | bytes 98312 | tf_op jit(solution)/shard_map/ppermute | solution.py:28
  3.7 6.8 %collective-permute-start.3 = (bf16[32,512]{1,0:T(8,128)(2,1)}, bf16[32,512]{1,0:T(8,128)(2,1)S(1)}, u32[]{:S(2)}, u32[]{:S(2)}) collective-permute-start(bf16[32,512]{1,0:T(8,128)(2,1)} %rows_hbm.1), channel_id=1, source_target_pairs={{0,8},{1,9},{2,10},{3,11},{4,12},{5,13},{6,14},{7,15},{8,0},{9,1},... | collective-permute-start | bytes 98312 | tf_op jit(solution)/shard_map/ppermute | solution.py:28
  8.7 6.2 %collective-permute-start.1 = (bf16[64,512]{1,0:T(8,128)(2,1)S(1)}, bf16[64,512]{1,0:T(8,128)(2,1)S(1)}, u32[]{:S(2)}, u32[]{:S(2)}) collective-permute-start(bf16[64,512]{1,0:T(8,128)(2,1)S(1)} %get-tuple-element.52), channel_id=1, source_target_pairs={{0,12},{1,13},{2,14},{3,15},{4,8},{5,9},{6,10},{7,11},{8,4},{9,5},... | collective-permute-start | bytes 196616 | tf_op jit(solution)/shard_map/ppermute | solution.py:28
  10.1 5.0 %collective-permute-start.2 = (bf16[64,512]{1,0:T(8,128)(2,1)S(1)}, bf16[64,512]{1,0:T(8,128)(2,1)S(1)}, u32[]{:S(2)}, u32[]{:S(2)}) collective-permute-start(bf16[64,512]{1,0:T(8,128)(2,1)S(1)} %get-tuple-element.52), channel_id=1, source_target_pairs={{0,4},{1,5},{2,6},{3,7},{4,0},{5,1},{6,2},{7,3},{8,12},{9,13},{10,... | collective-permute-start | bytes 196616 | tf_op jit(solution)/shard_map/ppermute | solution.py:28
  10.5 4.7 %collective-permute-start.4 = (bf16[32,512]{1,0:T(8,128)(2,1)S(1)}, bf16[32,512]{1,0:T(8,128)(2,1)S(1)}, u32[]{:S(2)}, u32[]{:S(2)}) collective-permute-start(bf16[32,512]{1,0:T(8,128)(2,1)S(1)} %collective-permute-done.3), channel_id=1, source_target_pairs={{0,2},{1,3},{2,0},{3,1},{4,6},{5,7},{6,4},{7,5},{8,10},{9,11},{10,... | collective-permute-start | bytes 98312 | tf_op jit(solution)/shard_map/ppermute | solution.py:28
  13.7 3.0 %copy-start.1 = (s32[3,6]{1,0:T(4,128)S(1)}, s32[3,6]{1,0:T(4,128)}, u32[]{:S(2)}) copy-start(s32[3,6]{1,0:T(4,128)} %coords_ref.1) | copy-start | bytes 220
  15.1 1.6 %collective-permute-start.5 = (bf16[256,512]{1,0:T(8,128)(2,1)S(1)}, bf16[256,512]{1,0:T(8,128)(2,1)S(1)}, u32[]{:S(2)}, u32[]{:S(2)}) collective-permute-start(bf16[256,512]{1,0:T(8,128)(2,1)S(1)} %constant_dynamic-update-slice_fusion.2.held_ref), channel_id=1, source_target_pairs={{0,1},{1,0},{2,3},{3,2},{4,5},{5,4},{6,7},{7,6},{8,9},{9,8},{10,11... | collective-permute-start | bytes 786440 | tf_op jit(solution)/shard_map/ppermute | solution.py:28
  16.5 7.1 %copy-start.2 = (s32[6,3]{0,1:T(4,128)S(1)}, s32[6,3]{0,1:T(4,128)}, u32[]{:S(2)}) copy-start(s32[6,3]{0,1:T(4,128)} %param.14) | copy-start | bytes 220
  18.9 11.0 %all-to-all-start = ((f32[32,2,128]{2,1,0:T(2,128)}), f32[32,2,128]{2,1,0:T(2,128)S(1)}, u32[]{:S(2)}, u32[]{:S(2)}) async-start(f32[32,2,128]{2,1,0:T(2,128)} %get-tuple-element.45), calls=%async_computation | async-start | bytes 65536 | tf_op jit(solution)/shard_map/all_to_all | solution.py:529
  22.6 1.5 %collective-permute-start.6 = (f32[32,128]{1,0:T(8,128)S(1)}, f32[32,128]{1,0:T(8,128)S(1)}, u32[]{:S(2)}, u32[]{:S(2)}) collective-permute-start(f32[32,128]{1,0:T(8,128)S(1)} %get-tuple-element.47.halo_ref), channel_id=1, source_target_pairs={{0,1},{1,0},{2,3},{3,2},{4,5},{5,4},{6,7},{7,6},{8,9},{9,8},{10,11... | collective-permute-start | bytes 49160 | tf_op jit(solution)/shard_map/ppermute | solution.py:28
  22.9 1.2 %collective-permute-start.7 = (f32[32,128]{1,0:T(8,128)S(1)}, f32[32,128]{1,0:T(8,128)S(1)}, u32[]{:S(2)}, u32[]{:S(2)}) collective-permute-start(f32[32,128]{1,0:T(8,128)S(1)} %get-tuple-element.47.halo_ref), channel_id=1, source_target_pairs={{1,2},{2,1},{3,4},{4,3},{5,6},{6,5},{7,8},{8,7},{9,10},{10,9},{11,... | collective-permute-start | bytes 49160 | tf_op jit(solution)/shard_map/ppermute | solution.py:528
  24.2 5.7 %copy-start = (f32[1,64,64]{2,1,0:T(8,128)S(1)}, f32[1,64,64]{2,1,0:T(8,128)}, u32[]{:S(2)}) copy-start(f32[1,64,64]{2,1,0:T(8,128)} %dev_ref.1) | copy-start | bytes 49156

commit v8 on v7

--- a/solution.py
+++ b/solution.py
@@ -18,7 +18,6 @@
 LANES = 128
 LEAF_ROWS = LEAF // LANES
 TILE = 512
-HIGHEST = lax.Precision.HIGHEST
 
 vol_weight = 0.1
 soft_square = 1.0
@@ -122,7 +121,13 @@
         copy.wait()
     leaves = transfer_ref.shape[0]
     transfer = transfer_ref[...].reshape(leaves * RANK, RANK)
-    raised = jnp.dot(transfer, dev_ref[0], precision=HIGHEST, preferred_element_type=jnp.float32)
+    high, low = split(transfer)
+    dev_high, dev_low = split(dev_ref[0])
+    raised = jnp.dot(
+        jnp.concatenate([high, high, low], axis=1),
+        jnp.concatenate([dev_high, dev_low, dev_high], axis=0),
+        preferred_element_type=jnp.float32,
+    )
     high, low = split(jnp.concatenate([transfer, raised], axis=1))
     for leaf in range(leaves):
         at, points = slice(leaf * RANK, (leaf + 1) * RANK), slice(leaf * LEAF, (leaf + 1) * LEAF)
@@ -137,32 +142,20 @@
         copy.wait()
 
 
-def prepare_kernel(reorder, far_hbm, group_far_hbm, orbit_ref, pick_ref, mask_ref, *refs):
-    far_ref, group_far_ref, sems = refs[-3:]
-    moves = ((far_hbm, far_ref), (group_far_hbm, group_far_ref))
-    copies = [pltpu.make_async_copy(a, b, sems.at[i]) for i, (a, b) in enumerate(moves)]
-    for copy in copies:
-        copy.start()
-    if reorder:
-        sorted_ref, order_ref = refs[:2]
-        for start in range(0, orbit_ref.shape[0], LEAF):
-            part = lax.dot_general(
-                orbit_ref[start : start + LEAF, :],
-                pick_ref[...],
-                (((1,), (1,)), ((), ())),
-                preferred_element_type=jnp.float32,
-            )
-            sorted_ref[start : start + LEAF, :] = part.astype(jnp.bfloat16)
-        size = order_ref.shape[0]
-        column = iota((size, 1), 0)
-        place = by_core(column // BLOCK_ROWS, size // BLOCK_ROWS) * BLOCK_ROWS + column % BLOCK_ROWS
-        hit = iota((size, size), 1) == place
-        order_ref[...] = jnp.where(hit, 1.0, 0.0).astype(jnp.bfloat16)
-    for copy in copies:
-        copy.wait()
-    dom_count, group_count = far_ref.shape[1], group_far_ref.shape[1]
-    mask_ref[:dom_count, :] = spread_rows(far_ref[...].astype(jnp.float32), dom_count)
-    mask_ref[dom_count:, :] = spread_rows(group_far_ref[...].astype(jnp.float32), group_count)
+def prepare_kernel(orbit_ref, pick_ref, sorted_ref, order_ref):
+    for start in range(0, orbit_ref.shape[0], LEAF):
+        part = lax.dot_general(
+            orbit_ref[start : start + LEAF, :],
+            pick_ref[...],
+            (((1,), (1,)), ((), ())),
+            preferred_element_type=jnp.float32,
+        )
+        sorted_ref[start : start + LEAF, :] = part.astype(jnp.bfloat16)
+    size = order_ref.shape[0]
+    column = iota((size, 1), 0)
+    place = by_core(column // BLOCK_ROWS, size // BLOCK_ROWS) * BLOCK_ROWS + column % BLOCK_ROWS
+    hit = iota((size, size), 1) == place
+    order_ref[...] = jnp.where(hit, 1.0, 0.0).astype(jnp.bfloat16)
 
 
 def half_matrix(pieces_ref, order_ref, rows_ref):
@@ -314,7 +307,13 @@
     return [place_ref[pl.ds(leaf + 8 * k, 1), :] for k in range(3)]
 
 
-def self_kernel(halo_ref, sum_ref, place_ref):
+def self_kernel(
+    far_hbm, group_far_hbm, halo_ref, sum_ref, place_ref, mask_ref, far_ref, group_far_ref, sems
+):
+    moves = ((far_hbm, far_ref), (group_far_hbm, group_far_ref))
+    copies = [pltpu.make_async_copy(a, b, sems.at[i]) for i, (a, b) in enumerate(moves)]
+    for copy in copies:
+        copy.start()
     leaves = sum_ref.shape[0]
     place_ref[...] = places(halo_ref[...], leaves * LEAF_ROWS)
     shift = [jnp.zeros((8, LANES), jnp.float32)] * 3
@@ -324,6 +323,11 @@
         for leaf in range(leaves):
             for at, value in pair_sums(kernel, leaf_density(halo_ref, leaf), y):
                 sum_ref[leaf, at, :] = value
+    for copy in copies:
+        copy.wait()
+    dom_count, group_count = far_ref.shape[1], group_far_ref.shape[1]
+    mask_ref[:dom_count, :] = spread_rows(far_ref[...].astype(jnp.float32), dom_count)
+    mask_ref[dom_count:, :] = spread_rows(group_far_ref[...].astype(jnp.float32), group_count)
 
 
 def near_kernel(
@@ -473,25 +477,22 @@
 
     def prepare(loaded):
         orbit, pick, _ = loaded
-        operands = (dev_far, group_far)
-        shapes = [jax.ShapeDtypeStruct((dev_far.shape[1] + group_far.shape[1], LANES), f32)]
-        if reorder:
-            shapes.append(jax.ShapeDtypeStruct((points, natural), jnp.bfloat16))
-            shapes.append(jax.ShapeDtypeStruct((natural, natural), jnp.bfloat16))
-        out = pl.pallas_call(
-            functools.partial(prepare_kernel, reorder),
-            out_shape=shapes,
-            in_specs=[HBM] * 2 + [VMEM] * 2,
-            out_specs=[VMEM] * len(shapes),
-            scratch_shapes=[pltpu.VMEM(x.shape, x.dtype) for x in operands]
-            + [pltpu.SemaphoreType.DMA((2,))],
+        if not reorder:
+            return [orbit, pick]
+        return pl.pallas_call(
+            prepare_kernel,
+            out_shape=(
+                jax.ShapeDtypeStruct((points, natural), jnp.bfloat16),
+                jax.ShapeDtypeStruct((natural, natural), jnp.bfloat16),
+            ),
+            in_specs=[VMEM] * 2,
+            out_specs=(VMEM, VMEM),
             compiler_params=params,
             cost_estimate=cost(2 * points * width * natural),
             name="prepare",
-        )(*[in_hbm(x) for x in operands], orbit, pick)
-        return out if reorder else [*out, orbit, pick]
-
-    held, other, (_, _, weights), (mask, orbit, pick) = gather_rows(density_rows, load, prepare)
+        )(orbit, pick)
+
+    held, other, (_, _, weights), (orbit, pick) = gather_rows(density_rows, load, prepare)
 
     if reorder:
         rest = [
@@ -531,15 +532,21 @@
     table = jax.ShapeDtypeStruct((rows, LANES), f32)
     sums = jax.ShapeDtypeStruct((leaves, LEAF, LANES), f32)
     places_shape = jax.ShapeDtypeStruct((24, LANES), f32)
-    near_sums, own_places = pl.pallas_call(
+    masks = jax.ShapeDtypeStruct((dev_far.shape[1] + group_far.shape[1], LANES), f32)
+    near_sums, own_places, mask = pl.pallas_call(
         self_kernel,
-        out_shape=(sums, places_shape),
-        in_specs=[VMEM],
-        out_specs=(VMEM, VMEM),
+        out_shape=(sums, places_shape, masks),
+        in_specs=[HBM, HBM, VMEM],
+        out_specs=(VMEM, VMEM, VMEM),
+        scratch_shapes=[
+            pltpu.VMEM(dev_far.shape, jnp.int32),
+            pltpu.VMEM(group_far.shape, jnp.int32),
+            pltpu.SemaphoreType.DMA((2,)),
+        ],
         compiler_params=params,
         cost_estimate=cost(20 << 20, 4 << 20),
         name="self",
-    )(halo)
+    )(in_hbm(dev_far), in_hbm(group_far), halo)
     near = pl.pallas_call(
         near_kernel,
         out_shape=table,

time: 31.3 us -> 31.3 us (level)
    all_to_all x1, waiting for transfers between devices: 4.11 us -> 3.75 us  [local(): everyone = lax.all_to_all(expansion, ('group', 'dom'), 0, 0)]
where the time goes in v8:
time: 31.3 us; the launch traced here: 31 us
  starting transfers between devices  13.1 us (42%)
  Pallas kernels  11.4 us (36%)
  waiting for transfers between devices  5.53 us (18%)
  between operations  0.78 us (2%)
    ppermute x7, starting transfers between devices, swap(): lax.ppermute(value, axis, [(i, i ^ mask) for i in range(lax.axis_size(axi...  8.78 us
    all_to_all x1, waiting for transfers between devices, local(): everyone = lax.all_to_all(expansion, ('group', 'dom'), 0, 0)  3.75 us
    all_to_all x1, starting transfers between devices, local(): everyone = lax.all_to_all(expansion, ('group', 'dom'), 0, 0)  3.71 us
    pallas_call x1, Pallas kernels, load(): pl.pallas_call(functools.partial(load_kernel, reorder), out_shape=(jax.Sh...  2.33 us
    pallas_call x1, Pallas kernels, local(): pl.pallas_call(functools.partial(density_kernel, reorder), out_shape=(jax...  2.14 us
    pallas_call x1, Pallas kernels, prepare(): pl.pallas_call(prepare_kernel, out_shape=(jax.ShapeDtypeStruct((points, n...  2.07 us
    ppermute x7, waiting for transfers between devices, swap(): lax.ppermute(value, axis, [(i, i ^ mask) for i in range(lax.axis_size(axi...  1.78 us
    pallas_call x1, Pallas kernels, local(): pl.pallas_call(near_kernel, out_shape=table, in_specs=[VMEM] * 6, out_spe...  1.57 us
  transfers between devices with their start and end apart: 9, of which 4 were waited for; matrix products, arithmetic and copies ran while one was open for 0% of the time, Pallas kernels for 26%

profile of v8, /device:TPU:0, one launch (start us, length us, event | category | flops | bytes accessed | tf_op | source)
XLA Modules:
  0.0 31.0 jit_solution(9529907389754868405)
XLA Ops:
  0.6 3.0 %collective-permute-start = (bf16[32,512]{1,0:T(8,128)(2,1)}, bf16[32,512]{1,0:T(8,128)(2,1)S(1)}, u32[]{:S(2)}, u32[]{:S(2)}) collective-permute-start(bf16[32,512]{1,0:T(8,128)(2,1)} %rows_hbm.1), channel_id=1, source_target_pairs={{0,2},{1,3},{2,0},{3,1},{4,6},{5,7},{6,4},{7,5},{8,10},{9,11},{10,... | collective-permute-start | bytes 98312 | tf_op jit(solution)/shard_map/ppermute | solution.py:27
  3.7 2.6 %collective-permute-start.3 = (bf16[32,512]{1,0:T(8,128)(2,1)}, bf16[32,512]{1,0:T(8,128)(2,1)S(1)}, u32[]{:S(2)}, u32[]{:S(2)}) collective-permute-start(bf16[32,512]{1,0:T(8,128)(2,1)} %rows_hbm.1), channel_id=1, source_target_pairs={{0,8},{1,9},{2,10},{3,11},{4,12},{5,13},{6,14},{7,15},{8,0},{9,1},... | collective-permute-start | bytes 98312 | tf_op jit(solution)/shard_map/ppermute | solution.py:27
  6.3 2.3 %load.1 = (bf16[32,512]{1,0:T(8,128)(2,1)S(1)}, bf16[3072,512]{1,0:T(8,128)(2,1)S(1)}, bf16[512,512]{1,0:T(8,128)(2,1)S(1)}, f32[128,3072]{1,0:T(8,128)S(1)}) custom-call(s32[1,32]{1,0:T(1,128)} %near_hbm.1, f32[6,64,64]{2,1,0:T(8,128)} %transfer_hbm.1, f32[1,64,64]{2,1,0:T(8,128)} %dev_ref.1, f32[64,3072]{1,0:T(8,128)} %basis_hbm.1, ...), custom_call_target="tpu_custom_call" | custom-call | flops 1048576 | bytes 4194304 | tf_op jit(solution)/shard_map/load/pallas_call | solution.py:461
  8.6 0.0 collective-permute-done
  8.6 1.4 %collective-permute-start.1 = (bf16[64,512]{1,0:T(8,128)(2,1)S(1)}, bf16[64,512]{1,0:T(8,128)(2,1)S(1)}, u32[]{:S(2)}, u32[]{:S(2)}) collective-permute-start(bf16[64,512]{1,0:T(8,128)(2,1)S(1)} %get-tuple-element.50), channel_id=1, source_target_pairs={{0,12},{1,13},{2,14},{3,15},{4,8},{5,9},{6,10},{7,11},{8,4},{9,5},... | collective-permute-start | bytes 196616 | tf_op jit(solution)/shard_map/ppermute | solution.py:27
  10.0 0.3 collective-permute-start.2
  10.4 0.0 collective-permute-done.3
  10.4 1.0 %collective-permute-start.4 = (bf16[32,512]{1,0:T(8,128)(2,1)S(1)}, bf16[32,512]{1,0:T(8,128)(2,1)S(1)}, u32[]{:S(2)}, u32[]{:S(2)}) collective-permute-start(bf16[32,512]{1,0:T(8,128)(2,1)S(1)} %collective-permute-done.3), channel_id=1, source_target_pairs={{0,2},{1,3},{2,0},{3,1},{4,6},{5,7},{6,4},{7,5},{8,10},{9,11},{10,... | collective-permute-start | bytes 98312 | tf_op jit(solution)/shard_map/ppermute | solution.py:27
  11.4 2.1 %prepare.1 = (bf16[3072,512]{1,0:T(8,128)(2,1)S(1)}, bf16[512,512]{1,0:T(8,128)(2,1)S(1)}) custom-call(bf16[3072,512]{1,0:T(8,128)(2,1)S(1)} %get-tuple-element.35.orbit_ref, bf16[512,512]{1,0:T(8,128)(2,1)S(1)} %get-tuple-element.36.pick_ref), custom_call_target="tpu_custom_call" | custom-call | flops 1610612736 | bytes 4194304 | tf_op jit(solution)/shard_map/prepare/pallas_call | solution.py:482
  13.5 0.0 copy-start.1
  13.5 1.4 %collective-permute-done.1 = bf16[64,512]{1,0:T(8,128)(2,1)S(1)} collective-permute-done((bf16[64,512]{1,0:T(8,128)(2,1)S(1)}, bf16[64,512]{1,0:T(8,128)(2,1)S(1)}, u32[]{:S(2)}, u32[]{:S(2)}) %collective-permute-start.1) | collective-permute-done | bytes 65568 | tf_op jit(solution)/shard_map/ppermute | solution.py:27
  14.9 0.1 collective-permute-done.2
  15.0 0.0 collective-permute-done.4
  15.1 0.1 collective-permute-start.5
  15.1 1.3 %first.1.refs_0_ = f32[3072,128]{1,0:T(8,128)S(1)} custom-call(bf16[3072,512]{1,0:T(8,128)(2,1)S(1)} %get-tuple-element.39.orbit_ref, bf16[256,512]{1,0:T(8,128)(2,1)S(1)} %constant_dynamic-update-slice_fusion.2.held_ref, bf16[512,512]{1,0:T(8,128)(2,1)S(1)} %get-tuple-element.42.order_ref.pick_ref), custom_call_target="tpu_custom_call" | custom-call | flops 805306368 | bytes 4194304 | tf_op jit(solution)/shard_map/first/pallas_call | solution.py:499
  16.4 0.0 copy-start.2
  16.4 0.2 collective-permute-done.5.other_ref
  16.7 0.0 copy-done.1
  16.7 2.1 %density.1 = (f32[32,128]{1,0:T(8,128)S(1)}, f32[32,2,128]{2,1,0:T(2,128)}) custom-call(s32[3,6]{1,0:T(4,128)S(1)} %copy-done.1, bf16[3072,512]{1,0:T(8,128)(2,1)S(1)} %get-tuple-element.39.orbit_ref, bf16[256,512]{1,0:T(8,128)(2,1)S(1)} %collective-permute-done.5.other_ref, f32[128,3072]{1,0:T(8,128)S(1)} %get-tuple-element.41.weights_ref, ...), custom_call_target="tpu_custom_call" | custom-call | flops 805306368 | bytes 4194304 | tf_op jit(solution)/shard_map/density/pallas_call | solution.py:513
  18.8 3.7 %all-to-all-start = ((f32[32,2,128]{2,1,0:T(2,128)}), f32[32,2,128]{2,1,0:T(2,128)S(1)}, u32[]{:S(2)}, u32[]{:S(2)}) async-start(f32[32,2,128]{2,1,0:T(2,128)} %get-tuple-element.43), calls=%async_computation | async-start | bytes 65536 | tf_op jit(solution)/shard_map/all_to_all | solution.py:530
  22.5 0.3 %collective-permute-start.6 = (f32[32,128]{1,0:T(8,128)S(1)}, f32[32,128]{1,0:T(8,128)S(1)}, u32[]{:S(2)}, u32[]{:S(2)}) collective-permute-start(f32[32,128]{1,0:T(8,128)S(1)} %get-tuple-element.44.halo_ref), channel_id=1, source_target_pairs={{0,1},{1,0},{2,3},{3,2},{4,5},{5,4},{6,7},{7,6},{8,9},{9,8},{10,11... | collective-permute-start | bytes 49160 | tf_op jit(solution)/shard_map/ppermute | solution.py:27
  22.8 0.7 %collective-permute-start.7 = (f32[32,128]{1,0:T(8,128)S(1)}, f32[32,128]{1,0:T(8,128)S(1)}, u32[]{:S(2)}, u32[]{:S(2)}) collective-permute-start(f32[32,128]{1,0:T(8,128)S(1)} %get-tuple-element.44.halo_ref), channel_id=1, source_target_pairs={{1,2},{2,1},{3,4},{4,3},{5,6},{6,5},{7,8},{8,7},{9,10},{10,9},{11,... | collective-permute-start | bytes 49160 | tf_op jit(solution)/shard_map/ppermute | solution.py:529
  23.5 0.0 copy-done.2
  23.5 0.1 copy.12.leaves_ref
  23.6 0.8 %self.1 = (f32[6,512,128]{2,1,0:T(8,128)S(1)}, f32[24,128]{1,0:T(8,128)S(1)}, f32[18,128]{1,0:T(8,128)S(1)}) custom-call(s32[1,16]{1,0:T(1,128)} %far_hbm.1, s32[1,2]{1,0:T(1,128)} %group_far_hbm.1, f32[32,128]{1,0:T(8,128)S(1)} %get-tuple-element.44.halo_ref), custom_call_target="tpu_custom_call" | custom-call | flops 20971520 | bytes 4194304 | tf_op jit(solution)/shard_map/self/pallas_call | solution.py:536
  24.4 0.0 collective-permute-done.6.even_ref
  24.4 0.0 collective-permute-done.7.odd_ref
  24.4 0.0 copy-start
  24.4 1.6 %near.1.near_ref = f32[24,128]{1,0:T(8,128)S(1)} custom-call(s32[6,3]{1,0:T(8,128)S(1)} %copy.12.leaves_ref, f32[32,128]{1,0:T(8,128)S(1)} %get-tuple-element.44.halo_ref, f32[32,128]{1,0:T(8,128)S(1)} %collective-permute-done.6.even_ref, f32[32,128]{1,0:T(8,128)S(1)} %collective-permute-done.7.odd_ref, f32[24,128]{1,0:T(8,128)S(1)} %get-tuple-element.46.own_ref, ...), custom_call_target="tpu_custom_call" | custom-call | flops 20971520 | bytes 4194304 | tf_op jit(solution)/shard_map/near/pallas_call | solution.py:550
  26.0 3.7 %all-to-all-done.expansion_ref = f32[32,2,128]{2,1,0:T(2,128)S(1)} async-done(((f32[32,2,128]{2,1,0:T(2,128)}), f32[32,2,128]{2,1,0:T(2,128)S(1)}, u32[]{:S(2)}, u32[]{:S(2)}) %all-to-all-start) | async-done | bytes 32800 | tf_op jit(solution)/shard_map/all_to_all | solution.py:530
  29.8 0.0 copy-done
  29.8 1.3 %potential.1 = (f32[24,128]{1,0:T(8,128)}, f32[24,128]{1,0:T(8,128)}) custom-call(f32[32,2,128]{2,1,0:T(2,128)S(1)} %all-to-all-done.expansion_ref, f32[18,128]{1,0:T(8,128)S(1)} %get-tuple-element.45.mask_ref, f32[128,3072]{1,0:T(8,128)S(1)} %get-tuple-element.41.weights_ref, f32[1,64,64]{2,1,0:T(8,128)S(1)} %copy-done, f32[24,128]{1,0:T(8,128)S(1)} %near.1.near_ref, ...), custom_call_target="tpu_custom_call" | custom-call | flops 4194304 | bytes 4194304 | tf_op jit(solution)/shard_map/potential/pallas_call | solution.py:564
  (6 shorter events, 0.0 us)
Async XLA Ops:
  0.6 8.0 %collective-permute-start = (bf16[32,512]{1,0:T(8,128)(2,1)}, bf16[32,512]{1,0:T(8,128)(2,1)S(1)}, u32[]{:S(2)}, u32[]{:S(2)}) collective-permute-start(bf16[32,512]{1,0:T(8,128)(2,1)} %rows_hbm.1), channel_id=1, source_target_pairs={{0,2},{1,3},{2,0},{3,1},{4,6},{5,7},{6,4},{7,5},{8,10},{9,11},{10,... | collective-permute-start | bytes 98312 | tf_op jit(solution)/shard_map/ppermute | solution.py:27
  3.7 6.7 %collective-permute-start.3 = (bf16[32,512]{1,0:T(8,128)(2,1)}, bf16[32,512]{1,0:T(8,128)(2,1)S(1)}, u32[]{:S(2)}, u32[]{:S(2)}) collective-permute-start(bf16[32,512]{1,0:T(8,128)(2,1)} %rows_hbm.1), channel_id=1, source_target_pairs={{0,8},{1,9},{2,10},{3,11},{4,12},{5,13},{6,14},{7,15},{8,0},{9,1},... | collective-permute-start | bytes 98312 | tf_op jit(solution)/shard_map/ppermute | solution.py:27
  8.6 6.2 %collective-permute-start.1 = (bf16[64,512]{1,0:T(8,128)(2,1)S(1)}, bf16[64,512]{1,0:T(8,128)(2,1)S(1)}, u32[]{:S(2)}, u32[]{:S(2)}) collective-permute-start(bf16[64,512]{1,0:T(8,128)(2,1)S(1)} %get-tuple-element.50), channel_id=1, source_target_pairs={{0,12},{1,13},{2,14},{3,15},{4,8},{5,9},{6,10},{7,11},{8,4},{9,5},... | collective-permute-start | bytes 196616 | tf_op jit(solution)/shard_map/ppermute | solution.py:27
  10.0 5.0 %collective-permute-start.2 = (bf16[64,512]{1,0:T(8,128)(2,1)S(1)}, bf16[64,512]{1,0:T(8,128)(2,1)S(1)}, u32[]{:S(2)}, u32[]{:S(2)}) collective-permute-start(bf16[64,512]{1,0:T(8,128)(2,1)S(1)} %get-tuple-element.50), channel_id=1, source_target_pairs={{0,4},{1,5},{2,6},{3,7},{4,0},{5,1},{6,2},{7,3},{8,12},{9,13},{10,... | collective-permute-start | bytes 196616 | tf_op jit(solution)/shard_map/ppermute | solution.py:27
  10.4 4.7 %collective-permute-start.4 = (bf16[32,512]{1,0:T(8,128)(2,1)S(1)}, bf16[32,512]{1,0:T(8,128)(2,1)S(1)}, u32[]{:S(2)}, u32[]{:S(2)}) collective-permute-start(bf16[32,512]{1,0:T(8,128)(2,1)S(1)} %collective-permute-done.3), channel_id=1, source_target_pairs={{0,2},{1,3},{2,0},{3,1},{4,6},{5,7},{6,4},{7,5},{8,10},{9,11},{10,... | collective-permute-start | bytes 98312 | tf_op jit(solution)/shard_map/ppermute | solution.py:27
  13.5 3.2 %copy-start.1 = (s32[3,6]{1,0:T(4,128)S(1)}, s32[3,6]{1,0:T(4,128)}, u32[]{:S(2)}) copy-start(s32[3,6]{1,0:T(4,128)} %coords_ref.1) | copy-start | bytes 220
  15.1 1.6 %collective-permute-start.5 = (bf16[256,512]{1,0:T(8,128)(2,1)S(1)}, bf16[256,512]{1,0:T(8,128)(2,1)S(1)}, u32[]{:S(2)}, u32[]{:S(2)}) collective-permute-start(bf16[256,512]{1,0:T(8,128)(2,1)S(1)} %constant_dynamic-update-slice_fusion.2.held_ref), channel_id=1, source_target_pairs={{0,1},{1,0},{2,3},{3,2},{4,5},{5,4},{6,7},{7,6},{8,9},{9,8},{10,11... | collective-permute-start | bytes 786440 | tf_op jit(solution)/shard_map/ppermute | solution.py:27
  16.4 7.1 %copy-start.2 = (s32[6,3]{0,1:T(4,128)S(1)}, s32[6,3]{0,1:T(4,128)}, u32[]{:S(2)}) copy-start(s32[6,3]{0,1:T(4,128)} %param.14) | copy-start | bytes 220
  18.8 11.0 %all-to-all-start = ((f32[32,2,128]{2,1,0:T(2,128)}), f32[32,2,128]{2,1,0:T(2,128)S(1)}, u32[]{:S(2)}, u32[]{:S(2)}) async-start(f32[32,2,128]{2,1,0:T(2,128)} %get-tuple-element.43), calls=%async_computation | async-start | bytes 65536 | tf_op jit(solution)/shard_map/all_to_all | solution.py:530
  22.5 1.9 %collective-permute-start.6 = (f32[32,128]{1,0:T(8,128)S(1)}, f32[32,128]{1,0:T(8,128)S(1)}, u32[]{:S(2)}, u32[]{:S(2)}) collective-permute-start(f32[32,128]{1,0:T(8,128)S(1)} %get-tuple-element.44.halo_ref), channel_id=1, source_target_pairs={{0,1},{1,0},{2,3},{3,2},{4,5},{5,4},{6,7},{7,6},{8,9},{9,8},{10,11... | collective-permute-start | bytes 49160 | tf_op jit(solution)/shard_map/ppermute | solution.py:27
  22.8 1.6 %collective-permute-start.7 = (f32[32,128]{1,0:T(8,128)S(1)}, f32[32,128]{1,0:T(8,128)S(1)}, u32[]{:S(2)}, u32[]{:S(2)}) collective-permute-start(f32[32,128]{1,0:T(8,128)S(1)} %get-tuple-element.44.halo_ref), channel_id=1, source_target_pairs={{1,2},{2,1},{3,4},{4,3},{5,6},{6,5},{7,8},{8,7},{9,10},{10,9},{11,... | collective-permute-start | bytes 49160 | tf_op jit(solution)/shard_map/ppermute | solution.py:529
  24.4 5.3 %copy-start = (f32[1,64,64]{2,1,0:T(8,128)S(1)}, f32[1,64,64]{2,1,0:T(8,128)}, u32[]{:S(2)}) copy-start(f32[1,64,64]{2,1,0:T(8,128)} %dev_ref.1) | copy-start | bytes 49156

commit v9 on v8

--- a/solution.py
+++ b/solution.py
@@ -29,7 +29,7 @@
 
 def piece_of(apart):
     pair = jnp.bitwise_and(lax.shift_right_logical(apart, 1), 3)
-    place = jnp.where(pair == 0, 0, jnp.where(pair == 3, 1, pair + 1))
+    place = jnp.where(pair == 0, 0, jnp.where(pair == 1, 3, pair - 1))
     return apart + 2 * (place - pair)
 
 
@@ -43,7 +43,7 @@
     middle, loaded = lax.optimization_barrier((middle, loaded))
     other_middle = swap(middle, "dom", 2)
     result = prepare(loaded)
-    held = jnp.concatenate([pair, far, close, middle, other_middle], axis=0)
+    held = jnp.concatenate([pair, middle, other_middle, far, close], axis=0)
     bit = 16
     while bit < count:
         held = jnp.concatenate([held, swap(held, "dom", bit)], axis=0)

time: 31.3 us -> 31.2 us (level)
  transfers between devices with their start and end apart: 9 -> 9, of which waited for: 4 -> 5; matrix products, arithmetic and copies ran while one was open for 0% -> 0% of each run, Pallas kernels for 26% -> 26%
where the time goes in v9:
time: 31.2 us; the launch traced here: 30.9 us
  starting transfers between devices  13.1 us (42%)
  Pallas kernels  11.4 us (37%)
  waiting for transfers between devices  5.51 us (18%)
  between operations  0.77 us (2%)
    ppermute x7, starting transfers between devices, swap(): lax.ppermute(value, axis, [(i, i ^ mask) for i in range(lax.axis_size(axi...  8.71 us
    all_to_all x1, waiting for transfers between devices, local(): everyone = lax.all_to_all(expansion, ('group', 'dom'), 0, 0)  3.75 us
    all_to_all x1, starting transfers between devices, local(): everyone = lax.all_to_all(expansion, ('group', 'dom'), 0, 0)  3.71 us
    pallas_call x1, Pallas kernels, load(): pl.pallas_call(functools.partial(load_kernel, reorder), out_shape=(jax.Sh...  2.33 us
    pallas_call x1, Pallas kernels, local(): pl.pallas_call(functools.partial(density_kernel, reorder), out_shape=(jax...  2.14 us
    pallas_call x1, Pallas kernels, prepare(): pl.pallas_call(prepare_kernel, out_shape=(jax.ShapeDtypeStruct((points, n...  2.07 us
    ppermute x7, waiting for transfers between devices, swap(): lax.ppermute(value, axis, [(i, i ^ mask) for i in range(lax.axis_size(axi...  1.76 us
    pallas_call x1, Pallas kernels, local(): pl.pallas_call(near_kernel, out_shape=table, in_specs=[VMEM] * 6, out_spe...  1.56 us
  transfers between devices with their start and end apart: 9, of which 5 were waited for; matrix products, arithmetic and copies ran while one was open for 0% of the time, Pallas kernels for 26%

profile of v9, /device:TPU:0, one launch (start us, length us, event | category | flops | bytes accessed | tf_op | source)
XLA Modules:
  0.0 30.9 jit_solution(2009137829758247053)
XLA Ops:
  0.6 3.0 %collective-permute-start = (bf16[32,512]{1,0:T(8,128)(2,1)}, bf16[32,512]{1,0:T(8,128)(2,1)S(1)}, u32[]{:S(2)}, u32[]{:S(2)}) collective-permute-start(bf16[32,512]{1,0:T(8,128)(2,1)} %rows_hbm.1), channel_id=1, source_target_pairs={{0,2},{1,3},{2,0},{3,1},{4,6},{5,7},{6,4},{7,5},{8,10},{9,11},{10,... | collective-permute-start | bytes 98312 | tf_op jit(solution)/shard_map/ppermute | solution.py:27
  3.7 2.6 %collective-permute-start.1 = (bf16[32,512]{1,0:T(8,128)(2,1)}, bf16[32,512]{1,0:T(8,128)(2,1)S(1)}, u32[]{:S(2)}, u32[]{:S(2)}) collective-permute-start(bf16[32,512]{1,0:T(8,128)(2,1)} %rows_hbm.1), channel_id=1, source_target_pairs={{0,8},{1,9},{2,10},{3,11},{4,12},{5,13},{6,14},{7,15},{8,0},{9,1},... | collective-permute-start | bytes 98312 | tf_op jit(solution)/shard_map/ppermute | solution.py:27
  6.3 2.3 %load.1 = (bf16[32,512]{1,0:T(8,128)(2,1)S(1)}, bf16[3072,512]{1,0:T(8,128)(2,1)S(1)}, bf16[512,512]{1,0:T(8,128)(2,1)S(1)}, f32[128,3072]{1,0:T(8,128)S(1)}) custom-call(s32[1,32]{1,0:T(1,128)} %near_hbm.1, f32[6,64,64]{2,1,0:T(8,128)} %transfer_hbm.1, f32[1,64,64]{2,1,0:T(8,128)} %dev_ref.1, f32[64,3072]{1,0:T(8,128)} %basis_hbm.1, ...), custom_call_target="tpu_custom_call" | custom-call | flops 1048576 | bytes 4194304 | tf_op jit(solution)/shard_map/load/pallas_call | solution.py:461
  8.6 0.0 collective-permute-done
  8.6 1.4 %collective-permute-start.3 = (bf16[64,512]{1,0:T(8,128)(2,1)S(1)}, bf16[64,512]{1,0:T(8,128)(2,1)S(1)}, u32[]{:S(2)}, u32[]{:S(2)}) collective-permute-start(bf16[64,512]{1,0:T(8,128)(2,1)S(1)} %get-tuple-element.50), channel_id=1, source_target_pairs={{0,12},{1,13},{2,14},{3,15},{4,8},{5,9},{6,10},{7,11},{8,4},{9,5},... | collective-permute-start | bytes 196616 | tf_op jit(solution)/shard_map/ppermute | solution.py:27
  10.0 0.3 collective-permute-start.4
  10.4 0.0 collective-permute-done.1
  10.4 1.0 %collective-permute-start.2 = (bf16[32,512]{1,0:T(8,128)(2,1)S(1)}, bf16[32,512]{1,0:T(8,128)(2,1)S(1)}, u32[]{:S(2)}, u32[]{:S(2)}) collective-permute-start(bf16[32,512]{1,0:T(8,128)(2,1)S(1)} %collective-permute-done.1), channel_id=1, source_target_pairs={{0,2},{1,3},{2,0},{3,1},{4,6},{5,7},{6,4},{7,5},{8,10},{9,11},{10,... | collective-permute-start | bytes 98312 | tf_op jit(solution)/shard_map/ppermute | solution.py:27
  11.4 2.1 %prepare.1 = (bf16[3072,512]{1,0:T(8,128)(2,1)S(1)}, bf16[512,512]{1,0:T(8,128)(2,1)S(1)}) custom-call(bf16[3072,512]{1,0:T(8,128)(2,1)S(1)} %get-tuple-element.35.orbit_ref, bf16[512,512]{1,0:T(8,128)(2,1)S(1)} %get-tuple-element.36.pick_ref), custom_call_target="tpu_custom_call" | custom-call | flops 1610612736 | bytes 4194304 | tf_op jit(solution)/shard_map/prepare/pallas_call | solution.py:482
  13.5 0.0 copy-start.1
  13.5 0.8 %collective-permute-done.2 = bf16[32,512]{1,0:T(8,128)(2,1)S(1)} collective-permute-done((bf16[32,512]{1,0:T(8,128)(2,1)S(1)}, bf16[32,512]{1,0:T(8,128)(2,1)S(1)}, u32[]{:S(2)}, u32[]{:S(2)}) %collective-permute-start.2) | collective-permute-done | bytes 32800 | tf_op jit(solution)/shard_map/ppermute | solution.py:27
  14.3 0.6 %collective-permute-done.3 = bf16[64,512]{1,0:T(8,128)(2,1)S(1)} collective-permute-done((bf16[64,512]{1,0:T(8,128)(2,1)S(1)}, bf16[64,512]{1,0:T(8,128)(2,1)S(1)}, u32[]{:S(2)}, u32[]{:S(2)}) %collective-permute-start.3) | collective-permute-done | bytes 65568 | tf_op jit(solution)/shard_map/ppermute | solution.py:27
  14.9 0.1 collective-permute-done.4
  15.0 0.0 collective-permute-start.5
  15.0 1.3 %first.1.refs_0_ = f32[3072,128]{1,0:T(8,128)S(1)} custom-call(bf16[3072,512]{1,0:T(8,128)(2,1)S(1)} %get-tuple-element.39.orbit_ref, bf16[256,512]{1,0:T(8,128)(2,1)S(1)} %constant_dynamic-update-slice_fusion.2.held_ref, bf16[512,512]{1,0:T(8,128)(2,1)S(1)} %get-tuple-element.42.order_ref.pick_ref), custom_call_target="tpu_custom_call" | custom-call | flops 805306368 | bytes 4194304 | tf_op jit(solution)/shard_map/first/pallas_call | solution.py:499
  16.3 0.0 copy-start.2
  16.3 0.3 collective-permute-done.5.other_ref
  16.6 0.0 copy-done.1
  16.6 2.1 %density.1 = (f32[32,128]{1,0:T(8,128)S(1)}, f32[32,2,128]{2,1,0:T(2,128)}) custom-call(s32[3,6]{1,0:T(4,128)S(1)} %copy-done.1, bf16[3072,512]{1,0:T(8,128)(2,1)S(1)} %get-tuple-element.39.orbit_ref, bf16[256,512]{1,0:T(8,128)(2,1)S(1)} %collective-permute-done.5.other_ref, f32[128,3072]{1,0:T(8,128)S(1)} %get-tuple-element.41.weights_ref, ...), custom_call_target="tpu_custom_call" | custom-call | flops 805306368 | bytes 4194304 | tf_op jit(solution)/shard_map/density/pallas_call | solution.py:513
  18.7 3.7 %all-to-all-start = ((f32[32,2,128]{2,1,0:T(2,128)}), f32[32,2,128]{2,1,0:T(2,128)S(1)}, u32[]{:S(2)}, u32[]{:S(2)}) async-start(f32[32,2,128]{2,1,0:T(2,128)} %get-tuple-element.43), calls=%async_computation | async-start | bytes 65536 | tf_op jit(solution)/shard_map/all_to_all | solution.py:530
  22.4 0.3 %collective-permute-start.6 = (f32[32,128]{1,0:T(8,128)S(1)}, f32[32,128]{1,0:T(8,128)S(1)}, u32[]{:S(2)}, u32[]{:S(2)}) collective-permute-start(f32[32,128]{1,0:T(8,128)S(1)} %get-tuple-element.44.halo_ref), channel_id=1, source_target_pairs={{0,1},{1,0},{2,3},{3,2},{4,5},{5,4},{6,7},{7,6},{8,9},{9,8},{10,11... | collective-permute-start | bytes 49160 | tf_op jit(solution)/shard_map/ppermute | solution.py:27
  22.7 0.7 %collective-permute-start.7 = (f32[32,128]{1,0:T(8,128)S(1)}, f32[32,128]{1,0:T(8,128)S(1)}, u32[]{:S(2)}, u32[]{:S(2)}) collective-permute-start(f32[32,128]{1,0:T(8,128)S(1)} %get-tuple-element.44.halo_ref), channel_id=1, source_target_pairs={{1,2},{2,1},{3,4},{4,3},{5,6},{6,5},{7,8},{8,7},{9,10},{10,9},{11,... | collective-permute-start | bytes 49160 | tf_op jit(solution)/shard_map/ppermute | solution.py:529
  23.4 0.0 copy-done.2
  23.4 0.1 copy.12.leaves_ref
  23.5 0.8 %self.1 = (f32[6,512,128]{2,1,0:T(8,128)S(1)}, f32[24,128]{1,0:T(8,128)S(1)}, f32[18,128]{1,0:T(8,128)S(1)}) custom-call(s32[1,16]{1,0:T(1,128)} %far_hbm.1, s32[1,2]{1,0:T(1,128)} %group_far_hbm.1, f32[32,128]{1,0:T(8,128)S(1)} %get-tuple-element.44.halo_ref), custom_call_target="tpu_custom_call" | custom-call | flops 20971520 | bytes 4194304 | tf_op jit(solution)/shard_map/self/pallas_call | solution.py:536
  24.3 0.0 collective-permute-done.6.even_ref
  24.3 0.0 collective-permute-done.7.odd_ref
  24.3 0.0 copy-start
  24.4 1.6 %near.1.near_ref = f32[24,128]{1,0:T(8,128)S(1)} custom-call(s32[6,3]{1,0:T(8,128)S(1)} %copy.12.leaves_ref, f32[32,128]{1,0:T(8,128)S(1)} %get-tuple-element.44.halo_ref, f32[32,128]{1,0:T(8,128)S(1)} %collective-permute-done.6.even_ref, f32[32,128]{1,0:T(8,128)S(1)} %collective-permute-done.7.odd_ref, f32[24,128]{1,0:T(8,128)S(1)} %get-tuple-element.46.own_ref, ...), custom_call_target="tpu_custom_call" | custom-call | flops 20971520 | bytes 4194304 | tf_op jit(solution)/shard_map/near/pallas_call | solution.py:550
  25.9 3.7 %all-to-all-done.expansion_ref = f32[32,2,128]{2,1,0:T(2,128)S(1)} async-done(((f32[32,2,128]{2,1,0:T(2,128)}), f32[32,2,128]{2,1,0:T(2,128)S(1)}, u32[]{:S(2)}, u32[]{:S(2)}) %all-to-all-start) | async-done | bytes 32800 | tf_op jit(solution)/shard_map/all_to_all | solution.py:530
  29.7 0.0 copy-done
  29.7 1.3 %potential.1 = (f32[24,128]{1,0:T(8,128)}, f32[24,128]{1,0:T(8,128)}) custom-call(f32[32,2,128]{2,1,0:T(2,128)S(1)} %all-to-all-done.expansion_ref, f32[18,128]{1,0:T(8,128)S(1)} %get-tuple-element.45.mask_ref, f32[128,3072]{1,0:T(8,128)S(1)} %get-tuple-element.41.weights_ref, f32[1,64,64]{2,1,0:T(8,128)S(1)} %copy-done, f32[24,128]{1,0:T(8,128)S(1)} %near.1.near_ref, ...), custom_call_target="tpu_custom_call" | custom-call | flops 4194304 | bytes 4194304 | tf_op jit(solution)/shard_map/potential/pallas_call | solution.py:564
  (6 shorter events, 0.0 us)
Async XLA Ops:
  0.6 8.0 %collective-permute-start = (bf16[32,512]{1,0:T(8,128)(2,1)}, bf16[32,512]{1,0:T(8,128)(2,1)S(1)}, u32[]{:S(2)}, u32[]{:S(2)}) collective-permute-start(bf16[32,512]{1,0:T(8,128)(2,1)} %rows_hbm.1), channel_id=1, source_target_pairs={{0,2},{1,3},{2,0},{3,1},{4,6},{5,7},{6,4},{7,5},{8,10},{9,11},{10,... | collective-permute-start | bytes 98312 | tf_op jit(solution)/shard_map/ppermute | solution.py:27
  3.7 6.7 %collective-permute-start.1 = (bf16[32,512]{1,0:T(8,128)(2,1)}, bf16[32,512]{1,0:T(8,128)(2,1)S(1)}, u32[]{:S(2)}, u32[]{:S(2)}) collective-permute-start(bf16[32,512]{1,0:T(8,128)(2,1)} %rows_hbm.1), channel_id=1, source_target_pairs={{0,8},{1,9},{2,10},{3,11},{4,12},{5,13},{6,14},{7,15},{8,0},{9,1},... | collective-permute-start | bytes 98312 | tf_op jit(solution)/shard_map/ppermute | solution.py:27
  8.6 6.2 %collective-permute-start.3 = (bf16[64,512]{1,0:T(8,128)(2,1)S(1)}, bf16[64,512]{1,0:T(8,128)(2,1)S(1)}, u32[]{:S(2)}, u32[]{:S(2)}) collective-permute-start(bf16[64,512]{1,0:T(8,128)(2,1)S(1)} %get-tuple-element.50), channel_id=1, source_target_pairs={{0,12},{1,13},{2,14},{3,15},{4,8},{5,9},{6,10},{7,11},{8,4},{9,5},... | collective-permute-start | bytes 196616 | tf_op jit(solution)/shard_map/ppermute | solution.py:27
  10.0 5.0 %collective-permute-start.4 = (bf16[64,512]{1,0:T(8,128)(2,1)S(1)}, bf16[64,512]{1,0:T(8,128)(2,1)S(1)}, u32[]{:S(2)}, u32[]{:S(2)}) collective-permute-start(bf16[64,512]{1,0:T(8,128)(2,1)S(1)} %get-tuple-element.50), channel_id=1, source_target_pairs={{0,4},{1,5},{2,6},{3,7},{4,0},{5,1},{6,2},{7,3},{8,12},{9,13},{10,... | collective-permute-start | bytes 196616 | tf_op jit(solution)/shard_map/ppermute | solution.py:27
  10.4 3.9 %collective-permute-start.2 = (bf16[32,512]{1,0:T(8,128)(2,1)S(1)}, bf16[32,512]{1,0:T(8,128)(2,1)S(1)}, u32[]{:S(2)}, u32[]{:S(2)}) collective-permute-start(bf16[32,512]{1,0:T(8,128)(2,1)S(1)} %collective-permute-done.1), channel_id=1, source_target_pairs={{0,2},{1,3},{2,0},{3,1},{4,6},{5,7},{6,4},{7,5},{8,10},{9,11},{10,... | collective-permute-start | bytes 98312 | tf_op jit(solution)/shard_map/ppermute | solution.py:27
  13.5 3.1 %copy-start.1 = (s32[3,6]{1,0:T(4,128)S(1)}, s32[3,6]{1,0:T(4,128)}, u32[]{:S(2)}) copy-start(s32[3,6]{1,0:T(4,128)} %coords_ref.1) | copy-start | bytes 220
  15.0 1.5 %collective-permute-start.5 = (bf16[256,512]{1,0:T(8,128)(2,1)S(1)}, bf16[256,512]{1,0:T(8,128)(2,1)S(1)}, u32[]{:S(2)}, u32[]{:S(2)}) collective-permute-start(bf16[256,512]{1,0:T(8,128)(2,1)S(1)} %constant_dynamic-update-slice_fusion.2.held_ref), channel_id=1, source_target_pairs={{0,1},{1,0},{2,3},{3,2},{4,5},{5,4},{6,7},{7,6},{8,9},{9,8},{10,11... | collective-permute-start | bytes 786440 | tf_op jit(solution)/shard_map/ppermute | solution.py:27
  16.3 7.1 %copy-start.2 = (s32[6,3]{0,1:T(4,128)S(1)}, s32[6,3]{0,1:T(4,128)}, u32[]{:S(2)}) copy-start(s32[6,3]{0,1:T(4,128)} %param.14) | copy-start | bytes 220
  18.7 11.0 %all-to-all-start = ((f32[32,2,128]{2,1,0:T(2,128)}), f32[32,2,128]{2,1,0:T(2,128)S(1)}, u32[]{:S(2)}, u32[]{:S(2)}) async-start(f32[32,2,128]{2,1,0:T(2,128)} %get-tuple-element.43), calls=%async_computation | async-start | bytes 65536 | tf_op jit(solution)/shard_map/all_to_all | solution.py:530
  22.4 1.9 %collective-permute-start.6 = (f32[32,128]{1,0:T(8,128)S(1)}, f32[32,128]{1,0:T(8,128)S(1)}, u32[]{:S(2)}, u32[]{:S(2)}) collective-permute-start(f32[32,128]{1,0:T(8,128)S(1)} %get-tuple-element.44.halo_ref), channel_id=1, source_target_pairs={{0,1},{1,0},{2,3},{3,2},{4,5},{5,4},{6,7},{7,6},{8,9},{9,8},{10,11... | collective-permute-start | bytes 49160 | tf_op jit(solution)/shard_map/ppermute | solution.py:27
  22.7 1.6 %collective-permute-start.7 = (f32[32,128]{1,0:T(8,128)S(1)}, f32[32,128]{1,0:T(8,128)S(1)}, u32[]{:S(2)}, u32[]{:S(2)}) collective-permute-start(f32[32,128]{1,0:T(8,128)S(1)} %get-tuple-element.44.halo_ref), channel_id=1, source_target_pairs={{1,2},{2,1},{3,4},{4,3},{5,6},{6,5},{7,8},{8,7},{9,10},{10,9},{11,... | collective-permute-start | bytes 49160 | tf_op jit(solution)/shard_map/ppermute | solution.py:529
  24.3 5.3 %copy-start = (f32[1,64,64]{2,1,0:T(8,128)S(1)}, f32[1,64,64]{2,1,0:T(8,128)}, u32[]{:S(2)}) copy-start(f32[1,64,64]{2,1,0:T(8,128)} %dev_ref.1) | copy-start | bytes 49156
